TPU v7x, 32 devices: a whole 2x2x4 slice. The times are simulated.
32 devices in a mesh: role: 2 (over core), dev: 16 (over z, y, x).
Axes of the slice: x: 2, y: 2, z: 4, core: 2. Of those that a mesh axis runs over, the one named last changes fastest.
Arguments:
- moe_rows: bfloat16 [1024, 3584], P(('role', 'dev')), may hold values from -6 to 6
- expert_ids: int32 [1024, 8], P(('role', 'dev')), may hold values from 0 to 15, all different within a row; in each aligned block of 32 rows (0 to 31, 32 to 63, ...) at most 32 rows name the same one
- gate_weights: float32 [1024, 8], P(('role', 'dev')), may hold values from 0.05 to 0.6
- w_gate: bfloat16 [16, 3584, 1024], P('dev', None, 'role'), may hold values from -0.09375 to 0.09375
- w_up: bfloat16 [16, 3584, 1024], P('dev', None, 'role'), may hold values from -0.09375 to 0.09375
- w_down: bfloat16 [16, 3584, 1024], P('dev', None, 'role'), may hold values from -0.1875 to 0.1875
- q_latent: bfloat16 [128, 64, 512], P(('role', 'dev')), may hold values from -40 to 40
- q_rope: bfloat16 [128, 4096], P(('role', 'dev')), may hold values from -4 to 4
- latent_cache: bfloat16 [128, 2048, 512], P(('role', 'dev')), may hold values from -4 to 4
- rope_cache: bfloat16 [128, 64, 2048], P(('role', 'dev')), may hold values from -4 to 4
- lengths: int32 [128], P(('role', 'dev')), may hold values from 2 to 2048, as said below
Outputs:
- moe_out: bfloat16 [1024, 3584], P(('role', 'dev'))
- attended: bfloat16 [128, 64, 512], P(('role', 'dev'))
Inputs may be any that keep to these rules, and one draw needn't show every extreme that they name: `expert_ids`: each row names 8 different experts; among the rows of one device no expert is named more than 32 times. `lengths`: the first row holds all 2048 cached tokens.
All inputs are finite; a program needn't handle non-finite values.
Results may differ from a plain program's by a relative error of at most 0.0057.
Values may be sent and summed in bfloat16 or wider, within the bound.
No kernel may reach another device: no remote copies, remote signals or barrier semaphores. Data moves between devices by JAX's collectives and lax.ppermute only.
A program may use at most 128 MiB of HBM per device.

v0:
```python
import jax
import jax.numpy as jnp
from jax import lax
from jax.sharding import PartitionSpec as P

score_scale = 192.0 ** (-0.5)


def expert_block(chosen, gate_matrix, up_matrix, down_matrix):
    gate_part = jnp.dot(chosen, gate_matrix, preferred_element_type=jnp.float32)
    up_part = jnp.dot(chosen, up_matrix, preferred_element_type=jnp.float32)
    hidden_units = (jax.nn.silu(gate_part) * up_part).astype(jnp.bfloat16)
    return lax.dot_general(
        hidden_units, down_matrix, (((1,), (1,)), ((), ())), preferred_element_type=jnp.float32
    )


def attend_row(query_lat, query_rope, cache_lat, cache_rope, length):
    head_count = query_lat.shape[0]
    rope_width = cache_rope.shape[0]
    scores = lax.dot_general(
        query_lat, cache_lat, (((1,), (1,)), ((), ())), preferred_element_type=jnp.float32
    )
    scores = scores + jnp.dot(
        query_rope.reshape(head_count, rope_width), cache_rope, preferred_element_type=jnp.float32
    )
    scores = scores * score_scale
    positions = jnp.arange(cache_lat.shape[0], dtype=jnp.int32)
    valid = (positions < length)[None, :]
    scores = jnp.where(valid, scores, jnp.float32(-1e30))
    highest = jnp.max(scores, axis=1, keepdims=True)
    weights = jnp.where(valid, jnp.exp(scores - highest), jnp.float32(0.0))
    probs = (weights / jnp.sum(weights, axis=1, keepdims=True)).astype(jnp.bfloat16)
    return jnp.dot(probs, cache_lat, preferred_element_type=jnp.float32).astype(jnp.bfloat16)


def per_device(
    moe_rows,
    expert_ids,
    gate_weights,
    w_gate,
    w_up,
    w_down,
    q_latent,
    q_rope,
    latent_cache,
    rope_cache,
    lengths,
):
    tok_count = moe_rows.shape[0]
    width = moe_rows.shape[1]
    topk_count = expert_ids.shape[1]
    experts = lax.axis_size("dev")
    capacity = min(tok_count, 2 * tok_count * topk_count // experts)
    flat_ids = expert_ids.reshape(-1)
    pair_count = flat_ids.shape[0]
    one_hot = (flat_ids[:, None] == jnp.arange(experts, dtype=jnp.int32)[None, :]).astype(jnp.int32)
    earlier = jnp.cumsum(one_hot, axis=0) - one_hot
    slot_index = jnp.sum(earlier * one_hot, axis=1)
    destination = flat_ids * capacity + slot_index
    source_row = jnp.full((experts * capacity,), tok_count, jnp.int32)
    source_row = source_row.at[destination].set(
        jnp.arange(pair_count, dtype=jnp.int32) // topk_count
    )
    padded_rows = jnp.concatenate([moe_rows, jnp.zeros((1, width), jnp.bfloat16)], axis=0)
    outgoing = padded_rows[source_row].reshape(experts, capacity, width)
    arrived = lax.all_to_all(outgoing, "dev", split_axis=0, concat_axis=0, tiled=True)
    own_rows = arrived.reshape(experts * capacity, width)
    both_rows = lax.all_gather(own_rows, "role", axis=0, tiled=True)
    expert_sum = lax.psum_scatter(
        expert_block(both_rows, w_gate[0], w_up[0], w_down[0]),
        "role",
        scatter_dimension=0,
        tiled=True,
    )
    finished = expert_sum.astype(jnp.bfloat16).reshape(experts, capacity, width)
    returned = lax.all_to_all(finished, "dev", split_axis=0, concat_axis=0, tiled=True)
    flat_back = returned.reshape(experts * capacity, width)
    picked = flat_back[destination].reshape(tok_count, topk_count, width).astype(jnp.float32)
    moe_out = jnp.sum(picked * gate_weights[:, :, None], axis=1).astype(jnp.bfloat16)
    attended = jax.vmap(attend_row)(q_latent, q_rope, latent_cache, rope_cache, lengths)
    return (moe_out, attended)


def solution(mesh):
    placed = (
        P(("role", "dev"), None),
        P(("role", "dev"), None),
        P(("role", "dev"), None),
        P("dev", None, "role"),
        P("dev", None, "role"),
        P("dev", None, "role"),
        P(("role", "dev"), None, None),
        P(("role", "dev"), None),
        P(("role", "dev"), None, None),
        P(("role", "dev"), None, None),
        P(("role", "dev")),
    )
    return jax.shard_map(
        per_device,
        mesh=mesh,
        in_specs=placed,
        out_specs=(P(("role", "dev"), None), P(("role", "dev"), None, None)),
        check_vma=False,
    )
```

profile of v0, /device:TPU:14, one launch (start us, length us, event | category | flops | bytes accessed | tf_op | source)
XLA Modules:
  0.0 282.5 jit_solution(15987377377622578204)
XLA Ops:
  7.2 0.0 all-gather.2.cloned.1.call-start
  7.2 0.8 copy.15
  8.1 0.1 eq.29
  8.2 0.1 eq.25
  8.2 0.7 broadcast_multiply_fusion
  8.9 0.6 reduce-window.6
  9.5 0.2 slice_reduce_fusion
  9.8 0.1 copy.14
  9.8 0.1 mul.42
  9.9 0.1 fusion.21
  10.0 1.4 scatter_custom_fusion
  11.5 1.0 concatenate.3
  12.4 4.2 %gather_fusion = bf16[512,3584]{1,0:T(8,128)(2,1)} fusion(bf16[33,3584]{1,0:T(8,128)(2,1)S(1)} %concatenate.3, s32[1024]{0:T(1024)S(1)} %pad_clamp_fusion.1), kind=kCustom, calls=%fused_computation | custom fusion | bytes 7342080 | tf_op jit(solution)/shard_map/gather | solution.py:66
  16.6 87.7 %all_to_all.10 = bf16[16,32,3584]{2,1,0:T(8,128)(2,1)} all-to-all(bf16[16,32,3584]{2,1,0:T(8,128)(2,1)} %bitcast.48), channel_id=1, replica_groups=mesh['role'=2,'dev'=16] {'dev'}, dimensions={0} | all-to-all | bytes 7340032 | tf_op jit(solution)/shard_map/all_to_all | solution.py:67
  104.3 0.0 all-gather.2.cloned.1.call-update
  104.3 0.0 reduce-scatter.2.cloned.1.call-start
  104.4 18.6 %all-gather.2.cloned.1.call-done = bf16[1024,3584]{1,0:T(8,128)(2,1)} async-done(((bf16[512,3584]{1,0:T(8,128)(2,1)}), bf16[1024,3584]{1,0:T(8,128)(2,1)}) %all-gather.2.cloned.1.call-update) | async-done | bytes 7340048 | tf_op jit(solution)/shard_map/all_gather | solution.py:69
  123.0 7.3 %fusion.4 = f32[1024,512]{1,0:T(8,128)S(1)} fusion(bf16[1024,3584]{1,0:T(8,128)(2,1)} %all-gather.2.cloned.1.call-done, bf16[1,3584,512]{2,1,0:T(8,128)(2,1)} %param.15), kind=kOutput, calls=%fused_computation.8 | convolution fusion | flops 3758096384 | bytes 13107200 | tf_op jit(solution)/shard_map/dot_general | solution.py:11
  130.3 15.5 %fusion.2 = f32[1024,3584]{1,0:T(8,128)} fusion(bf16[1,3584,512]{2,1,0:T(8,128)(2,1)} %param.16, f32[1024,512]{1,0:T(8,128)S(1)} %fusion.4, bf16[1024,3584]{1,0:T(8,128)(2,1)} %all-gather.2.cloned.1.call-done, bf16[1,3584,512]{2,1,0:T(8,128)(2,1)} %param.14), kind=kOutput, calls=%fused_computation.6 | convolution fusion | flops 7519338496 | bytes 31457280 | tf_op jit(solution)/shard_map/dot_general | solution.py:13
  145.8 0.0 reduce-scatter.2.cloned.1.call-update
  145.8 25.3 %reduce-scatter.2.cloned.1.call-done = f32[512,3584]{1,0:T(8,128)} async-done(((f32[1024,3584]{1,0:T(8,128)}), f32[512,3584]{1,0:T(8,128)}) %reduce-scatter.2.cloned.1.call-update) | async-done | bytes 7340048 | tf_op jit(solution)/shard_map/reduce_scatter | solution.py:70
  171.1 5.3 %convert_element_type.31 = bf16[512,3584]{1,0:T(8,128)(2,1)} convert(f32[512,3584]{1,0:T(8,128)} %reduce-scatter.2.cloned.1.call-done) | non-fusion elementwise | flops 1835008 | bytes 11010048 | tf_op jit(solution)/shard_map/convert_element_type | solution.py:76
  176.4 7.1 %all-to-all-start.1 = ((bf16[16,32,3584]{2,1,0:T(8,128)(2,1)}), bf16[16,32,3584]{2,1,0:T(8,128)(2,1)}, u32[]{:S(2)}, u32[]{:S(2)}) async-start(bf16[16,32,3584]{2,1,0:T(8,128)(2,1)} %bitcast.50), calls=%async_computation.2 | async-start | bytes 7340032 | tf_op jit(solution)/shard_map/all_to_all | solution.py:77
  183.5 0.1 copy.18
  183.6 0.1 reshape.93
  183.7 0.1 iota_compare_fusion
  183.8 6.0 %fusion.27 = f32[4,64,2048]{2,1,0:T(8,128)S(1)} fusion(bf16[4,64,512]{2,1,0:T(8,128)(2,1)S(1)} %copy-done.1, bf16[4,2048,512]{2,1,0:T(8,128)(2,1)} %param.19), kind=kOutput, calls=%fused_computation.46 | convolution fusion | flops 536870912 | bytes 10747904 | tf_op jit(solution)/shard_map/vmap()/dot_general | solution.py:21
  189.9 2.4 fusion.26
  192.2 6.3 %convolution_convert_fusion = bf16[4,64,512]{2,1,0:T(8,128)(2,1)} fusion(bf16[4,2048,512]{2,1,0:T(8,128)(2,1)} %param.19, f32[4,64,2048]{2,1,0:T(8,128)} %get-tuple-element.3, f32[4,64]{1,0:T(4,128)S(1)} %get-tuple-element.2), kind=kOutput, calls=%fused_computation.20 | convolution fusion | flops 538050560 | bytes 10748928 | tf_op jit(solution)/shard_map/vmap()/dot_general | solution.py:34
  198.6 68.9 %all-to-all-done.1 = bf16[16,32,3584]{2,1,0:T(8,128)(2,1)} async-done(((bf16[16,32,3584]{2,1,0:T(8,128)(2,1)}), bf16[16,32,3584]{2,1,0:T(8,128)(2,1)}, u32[]{:S(2)}, u32[]{:S(2)}) %all-to-all-start.1) | async-done | bytes 3670048 | tf_op jit(solution)/shard_map/all_to_all | solution.py:77
  267.4 6.0 %gather_fusion.1 = bf16[256,3584]{1,0:T(8,128)(2,1)S(1)} fusion(bf16[512,3584]{1,0:T(8,128)(2,1)} %bitcast.9, s32[1024]{0:T(1024)S(1)} %pad_clamp_fusion), kind=kCustom, calls=%fused_computation.1 | custom fusion | bytes 3671040 | tf_op jit(solution)/shard_map/gather | solution.py:79
  273.5 2.1 fusion.1
  (18 shorter events, 0.1 us)
Async XLA Ops:
  7.2 182.7 %copy-start = (bf16[4,64,2048]{2,1,0:T(8,128)(2,1)S(1)}, bf16[4,64,2048]{2,1,0:T(8,128)(2,1)}, u32[]{:S(2)}) copy-start(bf16[4,64,2048]{2,1,0:T(8,128)(2,1)} %param.20) | copy-start | bytes 3145732
  7.2 115.9 %all-gather.2.cloned.1.call-start = ((), (), s32[]{:S(2)}) async-start(), calls=%async_computation.3 | async-start | bytes 11010048 | tf_op jit(solution)/shard_map/all_gather | solution.py:69
  104.3 66.8 %reduce-scatter.2.cloned.1.call-start = ((), (), s32[]{:S(2)}) async-start(), calls=%async_computation.4 | async-start | bytes 22020096 | tf_op jit(solution)/shard_map/reduce_scatter | solution.py:70
  176.4 7.1 %copy-start.3 = (f32[32,8]{0,1:T(8,128)S(1)}, f32[32,8]{0,1:T(8,128)}, u32[]{:S(2)}) copy-start(f32[32,8]{0,1:T(8,128)} %param.13) | copy-start | bytes 3076
  176.4 7.2 %copy-start.2 = (bf16[4,4096]{1,0:T(4,128)(2,1)S(1)}, bf16[4,4096]{1,0:T(4,128)(2,1)}, u32[]{:S(2)}) copy-start(bf16[4,4096]{1,0:T(4,128)(2,1)} %param.18) | copy-start | bytes 98308
  176.4 7.3 %copy-start.4 = (s32[4]{0:T(128)S(1)}, s32[4]{0:T(128)}, u32[]{:S(2)}) copy-start(s32[4]{0:T(128)} %param.21) | copy-start | bytes 52
  176.4 7.4 %copy-start.1 = (bf16[4,64,512]{2,1,0:T(8,128)(2,1)S(1)}, bf16[4,64,512]{2,1,0:T(8,128)(2,1)}, u32[]{:S(2)}) copy-start(bf16[4,64,512]{2,1,0:T(8,128)(2,1)} %param.17) | copy-start | bytes 786436
  176.4 91.0 %all-to-all-start.1 = ((bf16[16,32,3584]{2,1,0:T(8,128)(2,1)}), bf16[16,32,3584]{2,1,0:T(8,128)(2,1)}, u32[]{:S(2)}, u32[]{:S(2)}) async-start(bf16[16,32,3584]{2,1,0:T(8,128)(2,1)} %bitcast.50), calls=%async_computation.2 | async-start | bytes 7340032 | tf_op jit(solution)/shard_map/all_to_all | solution.py:77
Sparse Core Ops, SparseCore 0:
  104.5 18.5 all-gather.1
  145.9 25.1 reduce-scatter.1
where the time goes:
time: 283 us; the launch traced here: 282 us
  waiting for transfers between devices  113 us (40%)
  blocking collectives  87.7 us (31%)
  matrix products  37.5 us (13%)
  local copies, waits for them, and re-layouts  14.2 us (5%)
  between operations  14.1 us (5%)
  other arithmetic  8.93 us (3%)
  starting transfers between devices  7.18 us (3%)
    all_to_all x1, blocking collectives, per_device(): lax.all_to_all(outgoing, 'dev', split_axis=0, concat_axis=0, tiled=True)  87.7 us
    all_to_all x1, waiting for transfers between devices, per_device(): lax.all_to_all(finished, 'dev', split_axis=0, concat_axis=0, tiled=True)  68.9 us
    reduce_scatter x1, waiting for transfers between devices, per_device(): lax.psum_scatter(expert_block(both_rows, w_gate[0], w_up[0], w_down[0]),...  25.3 us
    all_gather x1, waiting for transfers between devices, per_device(): both_rows = lax.all_gather(own_rows, 'role', axis=0, tiled=True)  18.6 us
    dot_general x1, matrix products, expert_block(): lax.dot_general(hidden_units, down_matrix, (((1,), (1,)), ((), ())), pref...  15.5 us
    dot_general x1, matrix products, expert_block(): up_part = jnp.dot(chosen, up_matrix, preferred_element_type=jnp.float32)  7.29 us
    all_to_all x1, starting transfers between devices, per_device(): lax.all_to_all(finished, 'dev', split_axis=0, concat_axis=0, tiled=True)  7.1 us
    dot_general x1, matrix products, attend_row(): jnp.dot(probs, cache_lat, preferred_element_type=jnp.float32)  6.34 us
  transfers between devices with their start and end apart: 3, of which 3 were waited for; matrix products, arithmetic and copies ran while one was open for 5% of the time, Pallas kernels for 0%

commit v1 on v0

v1 whole, which is shorter than its diff:
```python
import functools

import jax
import jax.numpy as jnp
from jax import lax
from jax.experimental import pallas as pl
from jax.experimental.pallas import tpu as pltpu
from jax.sharding import PartitionSpec as P

score_scale = 192.0 ** (-0.5)
both_axes = ("role", "dev")
chunk_count = 2


def shift_pairs(kind, step, depth, side):
    pairs = []
    for r in range(2):
        for z in range(depth):
            for y in range(side):
                for x in range(side):
                    to_r, to_z, to_y, to_x = r, z, y, x
                    if kind == "role":
                        to_r = 1 - r
                    elif kind == "z":
                        to_z = (z + step) % depth
                    elif (kind == "first") == (r == 0):
                        to_y = (y + step) % side
                    else:
                        to_x = (x + step) % side
                    here = ((r * depth + z) * side + y) * side + x
                    there = ((to_r * depth + to_z) * side + to_y) * side + to_x
                    pairs.append((here, there))
    return pairs


def attend_row(query_lat, query_rope, cache_lat, cache_rope, length):
    head_count = query_lat.shape[0]
    rope_width = cache_rope.shape[0]
    scores = lax.dot_general(
        query_lat, cache_lat, (((1,), (1,)), ((), ())), preferred_element_type=jnp.float32
    )
    scores = scores + jnp.dot(
        query_rope.reshape(head_count, rope_width), cache_rope, preferred_element_type=jnp.float32
    )
    scores = scores * score_scale
    positions = jnp.arange(cache_lat.shape[0], dtype=jnp.int32)
    valid = (positions < length)[None, :]
    scores = jnp.where(valid, scores, jnp.float32(-1e30))
    highest = jnp.max(scores, axis=1, keepdims=True)
    weights = jnp.where(valid, jnp.exp(scores - highest), jnp.float32(0.0))
    probs = (weights / jnp.sum(weights, axis=1, keepdims=True)).astype(jnp.bfloat16)
    return jnp.dot(probs, cache_lat, preferred_element_type=jnp.float32).astype(jnp.bfloat16)


def expert_kernel(count, lane_ref, *refs):
    blocks, refs = refs[:count], refs[count:]
    (gate_mat, up_mat, down_mat), refs = refs[:3], refs[3:]
    results, refs = refs[:count], refs[count:]
    rows, hidden, finished, in_sem, out_sem = refs
    block = blocks[0].shape[0]
    width, units = gate_mat.shape
    together = max(1, min(count, 256 // block))
    slab = width // 2

    def load(at):
        return pltpu.make_async_copy(
            blocks[at], rows.at[pl.ds(at * block, block)], in_sem.at[at]
        )

    def store(at):
        return pltpu.make_async_copy(
            finished.at[pl.ds(at * block, block)], results[at], out_sem.at[at]
        )

    for at in range(count):
        load(at).start()
    for first in range(0, count, together):
        group = range(first, first + together)
        for at in group:
            load(at).wait()
        cut = pl.ds(first * block, together * block)
        row_gates = jnp.sum(
            rows[cut, width:].astype(jnp.float32) * lane_ref[...], axis=1, keepdims=True
        )
        chosen = rows[cut, :width]
        gate_part = jnp.dot(chosen, gate_mat[...], preferred_element_type=jnp.float32)
        up_part = jnp.dot(chosen, up_mat[...], preferred_element_type=jnp.float32)
        silu = gate_part / (1.0 + jnp.exp(-gate_part))
        hidden[cut] = (silu * up_part).astype(jnp.bfloat16)
        for piece in range(2):
            lanes = pl.ds(piece * slab, slab)
            result = lax.dot_general(
                hidden[cut],
                down_mat[lanes, :],
                (((1,), (1,)), ((), ())),
                preferred_element_type=jnp.float32,
            )
            finished[cut, lanes] = (result * row_gates).astype(jnp.bfloat16)
        for at in group:
            store(at).start()
    for at in range(count):
        store(at).wait()


def expert_blocks(blocks, gate_matrix, up_matrix, down_matrix, own_lane):
    count = len(blocks)
    block, padded = blocks[0].shape
    width, units = gate_matrix.shape
    total = count * block
    anywhere = pl.BlockSpec(memory_space=pl.ANY)
    inside = pl.BlockSpec(memory_space=pltpu.VMEM)
    return pl.pallas_call(
        functools.partial(expert_kernel, count),
        out_shape=[jax.ShapeDtypeStruct((block, width), jnp.bfloat16)] * count,
        in_specs=[inside] + [anywhere] * count + [inside] * 3,
        out_specs=[anywhere] * count,
        scratch_shapes=[
            pltpu.VMEM((total, padded), jnp.bfloat16),
            pltpu.VMEM((total, units), jnp.bfloat16),
            pltpu.VMEM((total, width), jnp.bfloat16),
            pltpu.SemaphoreType.DMA((count,)),
            pltpu.SemaphoreType.DMA((count,)),
        ],
        compiler_params=pltpu.CompilerParams(vmem_limit_bytes=24 * 1024 * 1024),
        cost_estimate=pl.CostEstimate(
            flops=6 * total * width * units,
            bytes_accessed=6 * width * units + 4 * total * width,
            transcendentals=total * units,
        ),
        name="expert_blocks",
    )(own_lane, *blocks, gate_matrix, up_matrix, down_matrix)


def after(value, *earlier):
    return lax.optimization_barrier((value, *earlier))[0]


def per_device(
    moe_rows,
    expert_ids,
    gate_weights,
    w_gate,
    w_up,
    w_down,
    q_latent,
    q_rope,
    latent_cache,
    rope_cache,
    lengths,
):
    tok_count, width = moe_rows.shape
    experts = lax.axis_size("dev")
    side = 1
    while experts % (4 * side * side) == 0 and (2 * side) ** 2 * 4 <= experts:
        side *= 2
    depth = experts // (side * side)
    chunk = tok_count // chunk_count
    block = depth * chunk

    def send(value, kind, step=1):
        return lax.ppermute(value, both_axes, shift_pairs(kind, step, depth, side))

    place = lax.axis_index("dev")
    named = expert_ids[:, :, None] == jnp.arange(experts, dtype=jnp.int32)[None, None, :]
    dense_gates = jnp.sum(jnp.where(named, gate_weights[:, :, None], 0.0), axis=1)
    kept_part = lax.reduce_precision(dense_gates, exponent_bits=8, mantissa_bits=7)
    upper = kept_part.astype(jnp.bfloat16)
    lower = (dense_gates - kept_part).astype(jnp.bfloat16)
    spare = -(2 * experts) % 128
    tail = jnp.concatenate([upper, lower, jnp.zeros((tok_count, spare), jnp.bfloat16)], axis=1)
    tail_width = tail.shape[1]
    payload = jnp.concatenate([moe_rows, tail], axis=1)
    lane = jnp.arange(tail_width, dtype=jnp.int32)
    own_lane = ((lane == place) | (lane == place + experts)).astype(jnp.float32)[None, :]

    gathered = []
    line = None
    for c in range(chunk_count):
        mine = payload[c * chunk : (c + 1) * chunk]
        if line is not None:
            mine = after(mine, line)
        line = jnp.concatenate([mine] + [send(mine, "z", k) for k in range(1, depth)], axis=0)
        first = [line] + [send(line, "first", k) for k in range(1, side)]
        blocks = list(first)
        for k in range(1, side):
            blocks += [send(part, "last", k) for part in first]
        gathered.append(blocks + [send(part, "role") for part in blocks])

    finished = []
    summed = None
    for c in range(chunk_count):
        results = []
        for at in range(0, len(gathered[c]), 8):
            group = gathered[c][at : at + 8]
            if summed is not None:
                group = [after(group[0], summed)] + group[1:]
            results += expert_blocks(group, w_gate[0], w_up[0], w_down[0], own_lane)
        half = len(results) // 2
        whole = [
            (mine.astype(jnp.float32) + send(yours, "role").astype(jnp.float32))
            for mine, yours in zip(results[:half], results[half:])
        ]
        whole = [whole[k * side : (k + 1) * side] for k in range(side)]
        sent = [[part.astype(jnp.bfloat16) for part in row] for row in whole]
        summed = sent[side - 1][side - 1]
        kept = {}
        for a in reversed(range(side)):
            total = whole[0][a]
            for k in range(1, side):
                total = total + send(sent[k][a], "last", -k).astype(jnp.float32)
            kept[a] = total
        total = kept[0]
        for k in range(1, side):
            total = total + send(kept[k].astype(jnp.bfloat16), "first", -k).astype(jnp.float32)
        line = total.astype(jnp.bfloat16).reshape(depth, chunk, width)
        total = line[0].astype(jnp.float32)
        for k in range(1, depth):
            total = total + send(line[k], "z", -k).astype(jnp.float32)
        finished.append(total.astype(jnp.bfloat16))
    moe_out = jnp.concatenate(finished, axis=0)
    attended = jax.vmap(attend_row)(q_latent, q_rope, latent_cache, rope_cache, lengths)
    return (moe_out, attended)


def solution(mesh):
    placed = (
        P(("role", "dev"), None),
        P(("role", "dev"), None),
        P(("role", "dev"), None),
        P("dev", None, "role"),
        P("dev", None, "role"),
        P("dev", None, "role"),
        P(("role", "dev"), None, None),
        P(("role", "dev"), None),
        P(("role", "dev"), None, None),
        P(("role", "dev"), None, None),
        P(("role", "dev")),
    )
    return jax.shard_map(
        per_device,
        mesh=mesh,
        in_specs=placed,
        out_specs=(P(("role", "dev"), None), P(("role", "dev"), None, None)),
        check_vma=False,
    )
```

time: 283 us -> 135 us (0.48)
  the two profiles are of different devices: /device:TPU:14 before, /device:TPU:0 now
where the time goes in v1:
time: 135 us; the launch traced here: 134 us
  starting transfers between devices  43.8 us (32%)
  waiting for transfers between devices  39.9 us (30%)
  Pallas kernels  22 us (16%)
  matrix products  17.2 us (13%)
  local copies, waits for them, and re-layouts  7.57 us (6%)
  other arithmetic  2.98 us (2%)
    ppermute x40, starting transfers between devices, send(): return lax.ppermute(value, both_axes, shift_pairs(kind, step, depth, side))  43.8 us
    ppermute x40, waiting for transfers between devices, send(): return lax.ppermute(value, both_axes, shift_pairs(kind, step, depth, side))  39.9 us
    pallas_call x2, Pallas kernels, expert_blocks(): pl.pallas_call(functools.partial(expert_kernel, count), out_shape=[jax.Sh...  22 us
    dot_general x1, matrix products, attend_row(): lax.dot_general(query_lat, cache_lat, (((1,), (1,)), ((), ())), preferred...  7.44 us
    unnamed x23, local copies, waits for them, and re-layouts  6.18 us
    dot_general x1, matrix products, attend_row(): jnp.dot(probs, cache_lat, preferred_element_type=jnp.float32)  5.86 us
    sub x1, matrix products, attend_row(): weights = jnp.where(valid, jnp.exp(scores - highest), jnp.float32(0.0))  3.87 us
  transfers between devices with their start and end apart: 40, of which 10 were waited for; matrix products, arithmetic and copies ran while one was open for 14% of the time, Pallas kernels for 16%

profile of v1, /device:TPU:0, one launch (start us, length us, event | category | flops | bytes accessed | tf_op | source)
XLA Modules:
  0.0 134.2 jit_solution(12382845019108310547)
XLA Ops:
  2.7 3.1 %collective-permute-start = (bf16[16,3712]{1,0:T(8,128)(2,1)S(1)}, bf16[16,3712]{1,0:T(8,128)(2,1)S(1)}, u32[]{:S(2)}, u32[]{:S(2)}) collective-permute-start(bf16[16,3712]{1,0:T(8,128)(2,1)S(1)} %get-tuple-element.44), channel_id=1, source_target_pairs={{0,4},{1,5},{2,6},{3,7},{4,8},{5,9},{6,10},{7,11},{8,12},{9,13},{1... | collective-permute-start | bytes 356360 | tf_op jit(solution)/shard_map/ppermute | solution.py:161
  5.8 2.6 %collective-permute-start.1 = (bf16[16,3712]{1,0:T(8,128)(2,1)S(1)}, bf16[16,3712]{1,0:T(8,128)(2,1)S(1)}, u32[]{:S(2)}, u32[]{:S(2)}) collective-permute-start(bf16[16,3712]{1,0:T(8,128)(2,1)S(1)} %get-tuple-element.44), channel_id=1, source_target_pairs={{0,8},{1,9},{2,10},{3,11},{4,12},{5,13},{6,14},{7,15},{8,0},{9,1},... | collective-permute-start | bytes 356360 | tf_op jit(solution)/shard_map/ppermute | solution.py:161
  8.4 1.3 %collective-permute-start.2 = (bf16[16,3712]{1,0:T(8,128)(2,1)S(1)}, bf16[16,3712]{1,0:T(8,128)(2,1)S(1)}, u32[]{:S(2)}, u32[]{:S(2)}) collective-permute-start(bf16[16,3712]{1,0:T(8,128)(2,1)S(1)} %get-tuple-element.44), channel_id=1, source_target_pairs={{0,12},{1,13},{2,14},{3,15},{4,0},{5,1},{6,2},{7,3},{8,4},{9,5},{1... | collective-permute-start | bytes 356360 | tf_op jit(solution)/shard_map/ppermute | solution.py:161
  9.7 7.4 %fusion.11 = f32[4,64,2048]{2,1,0:T(8,128)} fusion(bf16[4,64,512]{2,1,0:T(8,128)(2,1)} %param.17, bf16[4,2048,512]{2,1,0:T(8,128)(2,1)} %param.19), kind=kOutput, calls=%fused_computation.35 | convolution fusion | flops 536870912 | bytes 10747904 | tf_op jit(solution)/shard_map/vmap()/dot_general | solution.py:39
  17.2 1.6 %collective-permute-start.3 = (bf16[64,3712]{1,0:T(8,128)(2,1)S(1)}, bf16[64,3712]{1,0:T(8,128)(2,1)S(1)}, u32[]{:S(2)}, u32[]{:S(2)}) collective-permute-start(bf16[64,3712]{1,0:T(8,128)(2,1)S(1)} %pad_maximum_fusion.refs_0_), channel_id=1, source_target_pairs={{0,2},{1,3},{2,0},{3,1},{4,6},{5,7},{6,4},{7,5},{8,10},{9,11},{10,... | collective-permute-start | bytes 1425416 | tf_op jit(solution)/shard_map/ppermute | solution.py:161
  18.8 1.5 %collective-permute-start.4 = (bf16[64,3712]{1,0:T(8,128)(2,1)S(1)}, bf16[64,3712]{1,0:T(8,128)(2,1)S(1)}, u32[]{:S(2)}, u32[]{:S(2)}) collective-permute-start(bf16[64,3712]{1,0:T(8,128)(2,1)S(1)} %pad_maximum_fusion.refs_0_), channel_id=1, source_target_pairs={{0,1},{1,0},{2,3},{3,2},{4,5},{5,4},{6,7},{7,6},{8,9},{9,8},{10,11... | collective-permute-start | bytes 1425416 | tf_op jit(solution)/shard_map/ppermute | solution.py:161
  20.3 2.1 %collective-permute-start.20 = (bf16[16,3712]{1,0:T(8,128)(2,1)S(1)}, bf16[16,3712]{1,0:T(8,128)(2,1)S(1)}, u32[]{:S(2)}, u32[]{:S(2)}) collective-permute-start(bf16[16,3712]{1,0:T(8,128)(2,1)S(1)} %get-tuple-element.28), channel_id=1, source_target_pairs={{0,4},{1,5},{2,6},{3,7},{4,8},{5,9},{6,10},{7,11},{8,12},{9,13},{1... | collective-permute-start | bytes 356360 | tf_op jit(solution)/shard_map/ppermute | solution.py:161
  22.4 1.7 %collective-permute-start.21 = (bf16[16,3712]{1,0:T(8,128)(2,1)S(1)}, bf16[16,3712]{1,0:T(8,128)(2,1)S(1)}, u32[]{:S(2)}, u32[]{:S(2)}) collective-permute-start(bf16[16,3712]{1,0:T(8,128)(2,1)S(1)} %get-tuple-element.28), channel_id=1, source_target_pairs={{0,8},{1,9},{2,10},{3,11},{4,12},{5,13},{6,14},{7,15},{8,0},{9,1},... | collective-permute-start | bytes 356360 | tf_op jit(solution)/shard_map/ppermute | solution.py:161
  24.1 4.2 %collective-permute-done.20 = bf16[16,3712]{1,0:T(8,128)(2,1)S(1)} collective-permute-done((bf16[16,3712]{1,0:T(8,128)(2,1)S(1)}, bf16[16,3712]{1,0:T(8,128)(2,1)S(1)}, u32[]{:S(2)}, u32[]{:S(2)}) %collective-permute-start.20) | collective-permute-done | bytes 118816 | tf_op jit(solution)/shard_map/ppermute | solution.py:161
  28.2 2.1 %collective-permute-start.22 = (bf16[16,3712]{1,0:T(8,128)(2,1)S(1)}, bf16[16,3712]{1,0:T(8,128)(2,1)S(1)}, u32[]{:S(2)}, u32[]{:S(2)}) collective-permute-start(bf16[16,3712]{1,0:T(8,128)(2,1)S(1)} %get-tuple-element.28), channel_id=1, source_target_pairs={{0,12},{1,13},{2,14},{3,15},{4,0},{5,1},{6,2},{7,3},{8,4},{9,5},{1... | collective-permute-start | bytes 356360 | tf_op jit(solution)/shard_map/ppermute | solution.py:161
  31.0 2.0 %collective-permute-done.21 = bf16[16,3712]{1,0:T(8,128)(2,1)S(1)} collective-permute-done((bf16[16,3712]{1,0:T(8,128)(2,1)S(1)}, bf16[16,3712]{1,0:T(8,128)(2,1)S(1)}, u32[]{:S(2)}, u32[]{:S(2)}) %collective-permute-start.21) | collective-permute-done | bytes 118816 | tf_op jit(solution)/shard_map/ppermute | solution.py:161
  33.0 2.1 %collective-permute-done.22 = bf16[16,3712]{1,0:T(8,128)(2,1)S(1)} collective-permute-done((bf16[16,3712]{1,0:T(8,128)(2,1)S(1)}, bf16[16,3712]{1,0:T(8,128)(2,1)S(1)}, u32[]{:S(2)}, u32[]{:S(2)}) %collective-permute-start.22) | collective-permute-done | bytes 118816 | tf_op jit(solution)/shard_map/ppermute | solution.py:161
  36.2 4.6 %collective-permute-done.5.refs_3_ = bf16[64,3712]{1,0:T(8,128)(2,1)} collective-permute-done((bf16[64,3712]{1,0:T(8,128)(2,1)S(1)}, bf16[64,3712]{1,0:T(8,128)(2,1)}, u32[]{:S(2)}, u32[]{:S(2)}) %collective-permute-start.5) | collective-permute-done | bytes 475168 | tf_op jit(solution)/shard_map/ppermute | solution.py:161
  41.1 3.9 %fusion.10 = (f32[4,64]{1,0:T(4,128)S(1)}, f32[4,64,2048]{2,1,0:T(8,128)}) fusion(pred[4,2048]{1,0:T(4,128)(4,1)S(1)} %iota_compare_fusion.1, f32[4,64,2048]{2,1,0:T(8,128)} %fusion.11, bf16[4,64,64]{2,1,0:T(8,128)(2,1)S(1)} %reshape.65, bf16[4,64,2048]{2,1,0:T(8,128)(2,1)S(1)} %copy-done), kind=kOutput, calls=%fused_computation.34 | convolution fusion | flops 70256640 | bytes 5284864 | tf_op jit(solution)/shard_map/vmap()/sub | solution.py:50
  45.5 1.5 %collective-permute-start.25 = (bf16[64,3712]{1,0:T(8,128)(2,1)S(1)}, bf16[64,3712]{1,0:T(8,128)(2,1)S(1)}, u32[]{:S(2)}, u32[]{:S(2)}) collective-permute-start(bf16[64,3712]{1,0:T(8,128)(2,1)S(1)} %collective-permute-done.23.refs_1_), channel_id=1, source_target_pairs={{0,1},{1,0},{2,3},{3,2},{4,5},{5,4},{6,7},{7,6},{8,9},{9,8},{10,11... | collective-permute-start | bytes 1425416 | tf_op jit(solution)/shard_map/ppermute | solution.py:161
  47.0 2.0 %copy-done.1 = bf16[1,3584,512]{2,1,0:T(8,128)(2,1)S(1)} copy-done((bf16[1,3584,512]{2,1,0:T(8,128)(2,1)S(1)}, bf16[1,3584,512]{2,1,0:T(8,128)(2,1)}, u32[]{:S(2)}) %copy-start.1) | copy-done | bytes 3670040
  49.0 2.0 %copy-done.3 = bf16[1,3584,512]{2,1,0:T(8,128)(2,1)S(1)} copy-done((bf16[1,3584,512]{2,1,0:T(8,128)(2,1)S(1)}, bf16[1,3584,512]{2,1,0:T(8,128)(2,1)}, u32[]{:S(2)}) %copy-start.3) | copy-done | bytes 3670040
  51.0 2.0 %copy-done.5 = bf16[1,3584,512]{2,1,0:T(8,128)(2,1)S(1)} copy-done((bf16[1,3584,512]{2,1,0:T(8,128)(2,1)S(1)}, bf16[1,3584,512]{2,1,0:T(8,128)(2,1)}, u32[]{:S(2)}) %copy-start.5) | copy-done | bytes 3670040
  53.1 10.6 %expert_blocks.2 = (bf16[64,3584]{1,0:T(8,128)(2,1)S(1)}, bf16[64,3584]{1,0:T(8,128)(2,1)S(1)}, bf16[64,3584]{1,0:T(8,128)(2,1)S(1)}, bf16[64,3584]{1,0:T(8,128)...) custom-call(f32[1,128]{1,0:T(1,128)S(1)} %or_convert_fusion.lane_ref, ...), custom_call_target="tpu_custom_call" | custom-call | flops 5637144576 | bytes 18350080 | tf_op jit(solution)/shard_map/expert_blocks/pallas_call | solution.py:112
  64.4 5.9 %convolution_convert_fusion = bf16[4,64,512]{2,1,0:T(8,128)(2,1)} fusion(bf16[4,2048,512]{2,1,0:T(8,128)(2,1)} %param.19, f32[4,64,2048]{2,1,0:T(8,128)S(1)} %copy-done.9, f32[4,64]{1,0:T(4,128)S(1)} %get-tuple-element.48), kind=kOutput, calls=%fused_computation.8 | convolution fusion | flops 538050560 | bytes 10748928 | tf_op jit(solution)/shard_map/vmap()/dot_general | solution.py:52
  71.5 3.3 %collective-permute-done.11 = bf16[64,3584]{1,0:T(8,128)(2,1)S(1)} collective-permute-done((bf16[64,3584]{1,0:T(8,128)(2,1)S(1)}, bf16[64,3584]{1,0:T(8,128)(2,1)S(1)}, u32[]{:S(2)}, u32[]{:S(2)}) %collective-permute-start.11) | collective-permute-done | bytes 458784 | tf_op jit(solution)/shard_map/ppermute | solution.py:161
  76.0 1.5 %collective-permute-start.12 = (bf16[64,3584]{1,0:T(8,128)(2,1)S(1)}, bf16[64,3584]{1,0:T(8,128)(2,1)S(1)}, u32[]{:S(2)}, u32[]{:S(2)}) collective-permute-start(bf16[64,3584]{1,0:T(8,128)(2,1)S(1)} %add_convert_fusion.7), channel_id=1, source_target_pairs={{0,1},{1,0},{2,3},{3,2},{4,5},{5,4},{6,7},{7,6},{8,9},{9,8},{10,11... | collective-permute-start | bytes 1376264 | tf_op jit(solution)/shard_map/ppermute | solution.py:161
  77.5 11.3 %expert_blocks.3 = (bf16[64,3584]{1,0:T(8,128)(2,1)S(1)}, bf16[64,3584]{1,0:T(8,128)(2,1)S(1)}, bf16[64,3584]{1,0:T(8,128)(2,1)S(1)}, bf16[64,3584]{1,0:T(8,128)...) custom-call(f32[1,128]{1,0:T(1,128)S(1)} %or_convert_fusion.lane_ref, ...), custom_call_target="tpu_custom_call" | custom-call | flops 5637144576 | bytes 18350080 | tf_op jit(solution)/shard_map/expert_blocks/pallas_call | solution.py:112
  89.7 1.7 %collective-permute-done.34 = bf16[64,3584]{1,0:T(8,128)(2,1)S(1)} collective-permute-done((bf16[64,3584]{1,0:T(8,128)(2,1)S(1)}, bf16[64,3584]{1,0:T(8,128)(2,1)S(1)}, u32[]{:S(2)}, u32[]{:S(2)}) %collective-permute-start.34) | collective-permute-done | bytes 458784 | tf_op jit(solution)/shard_map/ppermute | solution.py:161
  92.4 1.9 %collective-permute-start.16 = (bf16[64,3584]{1,0:T(8,128)(2,1)S(1)}, bf16[64,3584]{1,0:T(8,128)(2,1)S(1)}, u32[]{:S(2)}, u32[]{:S(2)}) collective-permute-start(bf16[64,3584]{1,0:T(8,128)(2,1)S(1)} %add_convert_fusion.5), channel_id=1, source_target_pairs={{0,2},{1,3},{2,0},{3,1},{4,6},{5,7},{6,4},{7,5},{8,10},{9,11},{10,... | collective-permute-start | bytes 1376264 | tf_op jit(solution)/shard_map/ppermute | solution.py:161
  94.3 9.6 %collective-permute-done.35 = bf16[64,3584]{1,0:T(8,128)(2,1)S(1)} collective-permute-done((bf16[64,3584]{1,0:T(8,128)(2,1)S(1)}, bf16[64,3584]{1,0:T(8,128)(2,1)S(1)}, u32[]{:S(2)}, u32[]{:S(2)}) %collective-permute-start.35) | collective-permute-done | bytes 458784 | tf_op jit(solution)/shard_map/ppermute | solution.py:161
  104.6 2.7 %collective-permute-start.36 = (bf16[64,3584]{1,0:T(8,128)(2,1)S(1)}, bf16[64,3584]{1,0:T(8,128)(2,1)S(1)}, u32[]{:S(2)}, u32[]{:S(2)}) collective-permute-start(bf16[64,3584]{1,0:T(8,128)(2,1)S(1)} %add_convert_fusion.1), channel_id=1, source_target_pairs={{0,2},{1,3},{2,0},{3,1},{4,6},{5,7},{6,4},{7,5},{8,10},{9,11},{10,... | collective-permute-start | bytes 1376264 | tf_op jit(solution)/shard_map/ppermute | solution.py:161
  107.6 5.2 %collective-permute-start.17 = (bf16[16,3584]{1,0:T(8,128)(2,1)S(1)}, bf16[16,3584]{1,0:T(8,128)(2,1)S(1)}, u32[]{:S(2)}, u32[]{:S(2)}) collective-permute-start(bf16[16,3584]{1,0:T(8,128)(2,1)S(1)} %get-tuple-element.38), channel_id=1, source_target_pairs={{0,12},{1,13},{2,14},{3,15},{4,0},{5,1},{6,2},{7,3},{8,4},{9,5},{1... | collective-permute-start | bytes 344072 | tf_op jit(solution)/shard_map/ppermute | solution.py:161
  114.1 3.0 %collective-permute-done.32 = bf16[64,3584]{1,0:T(8,128)(2,1)S(1)} collective-permute-done((bf16[64,3584]{1,0:T(8,128)(2,1)S(1)}, bf16[64,3584]{1,0:T(8,128)(2,1)S(1)}, u32[]{:S(2)}, u32[]{:S(2)}) %collective-permute-start.32) | collective-permute-done | bytes 458784 | tf_op jit(solution)/shard_map/ppermute | solution.py:161
  117.4 6.0 %collective-permute-start.37 = (bf16[16,3584]{1,0:T(8,128)(2,1)S(1)}, bf16[16,3584]{1,0:T(8,128)(2,1)S(1)}, u32[]{:S(2)}, u32[]{:S(2)}) collective-permute-start(bf16[16,3584]{1,0:T(8,128)(2,1)S(1)} %get-tuple-element.41), channel_id=1, source_target_pairs={{0,12},{1,13},{2,14},{3,15},{4,0},{5,1},{6,2},{7,3},{8,4},{9,5},{1... | collective-permute-start | bytes 344072 | tf_op jit(solution)/shard_map/ppermute | solution.py:161
  124.1 2.5 %collective-permute-done.37 = bf16[16,3584]{1,0:T(8,128)(2,1)S(1)} collective-permute-done((bf16[16,3584]{1,0:T(8,128)(2,1)S(1)}, bf16[16,3584]{1,0:T(8,128)(2,1)S(1)}, u32[]{:S(2)}, u32[]{:S(2)}) %collective-permute-start.37) | collective-permute-done | bytes 114720 | tf_op jit(solution)/shard_map/ppermute | solution.py:161
  126.6 6.9 %collective-permute-done.38 = bf16[16,3584]{1,0:T(8,128)(2,1)S(1)} collective-permute-done((bf16[16,3584]{1,0:T(8,128)(2,1)S(1)}, bf16[16,3584]{1,0:T(8,128)(2,1)S(1)}, u32[]{:S(2)}, u32[]{:S(2)}) %collective-permute-start.38) | collective-permute-done | bytes 114720 | tf_op jit(solution)/shard_map/ppermute | solution.py:161
  (102 shorter events, 13.4 us)
Async XLA Ops:
  2.7 14.5 %collective-permute-start = (bf16[16,3712]{1,0:T(8,128)(2,1)S(1)}, bf16[16,3712]{1,0:T(8,128)(2,1)S(1)}, u32[]{:S(2)}, u32[]{:S(2)}) collective-permute-start(bf16[16,3712]{1,0:T(8,128)(2,1)S(1)} %get-tuple-element.44), channel_id=1, source_target_pairs={{0,4},{1,5},{2,6},{3,7},{4,8},{5,9},{6,10},{7,11},{8,12},{9,13},{1... | collective-permute-start | bytes 356360 | tf_op jit(solution)/shard_map/ppermute | solution.py:161
  5.8 11.4 %collective-permute-start.1 = (bf16[16,3712]{1,0:T(8,128)(2,1)S(1)}, bf16[16,3712]{1,0:T(8,128)(2,1)S(1)}, u32[]{:S(2)}, u32[]{:S(2)}) collective-permute-start(bf16[16,3712]{1,0:T(8,128)(2,1)S(1)} %get-tuple-element.44), channel_id=1, source_target_pairs={{0,8},{1,9},{2,10},{3,11},{4,12},{5,13},{6,14},{7,15},{8,0},{9,1},... | collective-permute-start | bytes 356360 | tf_op jit(solution)/shard_map/ppermute | solution.py:161
  8.4 8.8 %collective-permute-start.2 = (bf16[16,3712]{1,0:T(8,128)(2,1)S(1)}, bf16[16,3712]{1,0:T(8,128)(2,1)S(1)}, u32[]{:S(2)}, u32[]{:S(2)}) collective-permute-start(bf16[16,3712]{1,0:T(8,128)(2,1)S(1)} %get-tuple-element.44), channel_id=1, source_target_pairs={{0,12},{1,13},{2,14},{3,15},{4,0},{5,1},{6,2},{7,3},{8,4},{9,5},{1... | collective-permute-start | bytes 356360 | tf_op jit(solution)/shard_map/ppermute | solution.py:161
  17.2 13.2 %collective-permute-start.3 = (bf16[64,3712]{1,0:T(8,128)(2,1)S(1)}, bf16[64,3712]{1,0:T(8,128)(2,1)S(1)}, u32[]{:S(2)}, u32[]{:S(2)}) collective-permute-start(bf16[64,3712]{1,0:T(8,128)(2,1)S(1)} %pad_maximum_fusion.refs_0_), channel_id=1, source_target_pairs={{0,2},{1,3},{2,0},{3,1},{4,6},{5,7},{6,4},{7,5},{8,10},{9,11},{10,... | collective-permute-start | bytes 1425416 | tf_op jit(solution)/shard_map/ppermute | solution.py:161
  18.8 16.8 %collective-permute-start.4 = (bf16[64,3712]{1,0:T(8,128)(2,1)S(1)}, bf16[64,3712]{1,0:T(8,128)(2,1)S(1)}, u32[]{:S(2)}, u32[]{:S(2)}) collective-permute-start(bf16[64,3712]{1,0:T(8,128)(2,1)S(1)} %pad_maximum_fusion.refs_0_), channel_id=1, source_target_pairs={{0,1},{1,0},{2,3},{3,2},{4,5},{5,4},{6,7},{7,6},{8,9},{9,8},{10,11... | collective-permute-start | bytes 1425416 | tf_op jit(solution)/shard_map/ppermute | solution.py:161
  20.3 24.6 %collective-permute-start.6 = (bf16[64,3712]{1,0:T(8,128)(2,1)S(1)}, bf16[64,3712]{1,0:T(8,128)(2,1)}, u32[]{:S(2)}, u32[]{:S(2)}) collective-permute-start(bf16[64,3712]{1,0:T(8,128)(2,1)S(1)} %pad_maximum_fusion.refs_0_), channel_id=1, source_target_pairs={{0,16},{1,17},{2,18},{3,19},{4,20},{5,21},{6,22},{7,23},{8,24},{9,... | collective-permute-start | bytes 1425416 | tf_op jit(solution)/shard_map/ppermute | solution.py:161
  20.3 7.9 %collective-permute-start.20 = (bf16[16,3712]{1,0:T(8,128)(2,1)S(1)}, bf16[16,3712]{1,0:T(8,128)(2,1)S(1)}, u32[]{:S(2)}, u32[]{:S(2)}) collective-permute-start(bf16[16,3712]{1,0:T(8,128)(2,1)S(1)} %get-tuple-element.28), channel_id=1, source_target_pairs={{0,4},{1,5},{2,6},{3,7},{4,8},{5,9},{6,10},{7,11},{8,12},{9,13},{1... | collective-permute-start | bytes 356360 | tf_op jit(solution)/shard_map/ppermute | solution.py:161
  22.4 10.5 %collective-permute-start.21 = (bf16[16,3712]{1,0:T(8,128)(2,1)S(1)}, bf16[16,3712]{1,0:T(8,128)(2,1)S(1)}, u32[]{:S(2)}, u32[]{:S(2)}) collective-permute-start(bf16[16,3712]{1,0:T(8,128)(2,1)S(1)} %get-tuple-element.28), channel_id=1, source_target_pairs={{0,8},{1,9},{2,10},{3,11},{4,12},{5,13},{6,14},{7,15},{8,0},{9,1},... | collective-permute-start | bytes 356360 | tf_op jit(solution)/shard_map/ppermute | solution.py:161
  28.2 6.8 %collective-permute-start.22 = (bf16[16,3712]{1,0:T(8,128)(2,1)S(1)}, bf16[16,3712]{1,0:T(8,128)(2,1)S(1)}, u32[]{:S(2)}, u32[]{:S(2)}) collective-permute-start(bf16[16,3712]{1,0:T(8,128)(2,1)S(1)} %get-tuple-element.28), channel_id=1, source_target_pairs={{0,12},{1,13},{2,14},{3,15},{4,0},{5,1},{6,2},{7,3},{8,4},{9,5},{1... | collective-permute-start | bytes 356360 | tf_op jit(solution)/shard_map/ppermute | solution.py:161
  30.4 10.4 %collective-permute-start.5 = (bf16[64,3712]{1,0:T(8,128)(2,1)S(1)}, bf16[64,3712]{1,0:T(8,128)(2,1)}, u32[]{:S(2)}, u32[]{:S(2)}) collective-permute-start(bf16[64,3712]{1,0:T(8,128)(2,1)S(1)} %collective-permute-done.3.refs_1_), channel_id=1, source_target_pairs={{0,1},{1,0},{2,3},{3,2},{4,5},{5,4},{6,7},{7,6},{8,9},{9,8},{10,11... | collective-permute-start | bytes 1425416 | tf_op jit(solution)/shard_map/ppermute | solution.py:161
  35.1 10.4 %collective-permute-start.23 = (bf16[64,3712]{1,0:T(8,128)(2,1)S(1)}, bf16[64,3712]{1,0:T(8,128)(2,1)S(1)}, u32[]{:S(2)}, u32[]{:S(2)}) collective-permute-start(bf16[64,3712]{1,0:T(8,128)(2,1)S(1)} %constant_dynamic-update-slice_fusion.refs_0_), channel_id=1, source_target_pairs={{0,2},{1,3},{2,0},{3,1},{4,6},{5,7},{6,4},{7,5},{8,10},{9,11},{10,... | collective-permute-start | bytes 1425416 | tf_op jit(solution)/shard_map/ppermute | solution.py:161
  35.7 11.3 %collective-permute-start.7 = (bf16[64,3712]{1,0:T(8,128)(2,1)S(1)}, bf16[64,3712]{1,0:T(8,128)(2,1)}, u32[]{:S(2)}, u32[]{:S(2)}) collective-permute-start(bf16[64,3712]{1,0:T(8,128)(2,1)S(1)} %collective-permute-done.3.refs_1_), channel_id=1, source_target_pairs={{0,16},{1,17},{2,18},{3,19},{4,20},{5,21},{6,22},{7,23},{8,24},{9,... | collective-permute-start | bytes 1425416 | tf_op jit(solution)/shard_map/ppermute | solution.py:161
  35.7 11.3 %collective-permute-start.8 = (bf16[64,3712]{1,0:T(8,128)(2,1)S(1)}, bf16[64,3712]{1,0:T(8,128)(2,1)}, u32[]{:S(2)}, u32[]{:S(2)}) collective-permute-start(bf16[64,3712]{1,0:T(8,128)(2,1)S(1)} %collective-permute-done.4.refs_2_), channel_id=1, source_target_pairs={{0,16},{1,17},{2,18},{3,19},{4,20},{5,21},{6,22},{7,23},{8,24},{9,... | collective-permute-start | bytes 1425416 | tf_op jit(solution)/shard_map/ppermute | solution.py:161
  44.9 25.8 %collective-permute-start.24 = (bf16[64,3712]{1,0:T(8,128)(2,1)S(1)}, bf16[64,3712]{1,0:T(8,128)(2,1)S(1)}, u32[]{:S(2)}, u32[]{:S(2)}) collective-permute-start(bf16[64,3712]{1,0:T(8,128)(2,1)S(1)} %constant_dynamic-update-slice_fusion.refs_0_), channel_id=1, source_target_pairs={{0,1},{1,0},{2,3},{3,2},{4,5},{5,4},{6,7},{7,6},{8,9},{9,8},{10,11... | collective-permute-start | bytes 1425416 | tf_op jit(solution)/shard_map/ppermute | solution.py:161
  45.5 25.3 %collective-permute-start.25 = (bf16[64,3712]{1,0:T(8,128)(2,1)S(1)}, bf16[64,3712]{1,0:T(8,128)(2,1)S(1)}, u32[]{:S(2)}, u32[]{:S(2)}) collective-permute-start(bf16[64,3712]{1,0:T(8,128)(2,1)S(1)} %collective-permute-done.23.refs_1_), channel_id=1, source_target_pairs={{0,1},{1,0},{2,3},{3,2},{4,5},{5,4},{6,7},{7,6},{8,9},{9,8},{10,11... | collective-permute-start | bytes 1425416 | tf_op jit(solution)/shard_map/ppermute | solution.py:161
  63.7 7.5 %collective-permute-start.14 = (bf16[64,3584]{1,0:T(8,128)(2,1)S(1)}, bf16[64,3584]{1,0:T(8,128)(2,1)S(1)}, u32[]{:S(2)}, u32[]{:S(2)}) collective-permute-start(bf16[64,3584]{1,0:T(8,128)(2,1)S(1)} %get-tuple-element.27), channel_id=1, source_target_pairs={{0,16},{1,17},{2,18},{3,19},{4,20},{5,21},{6,22},{7,23},{8,24},{9,... | collective-permute-start | bytes 1376264 | tf_op jit(solution)/shard_map/ppermute | solution.py:161
  70.8 6.7 %collective-permute-start.29 = (bf16[64,3712]{1,0:T(8,128)(2,1)S(1)}, bf16[64,3712]{1,0:T(8,128)(2,1)S(1)}, u32[]{:S(2)}, u32[]{:S(2)}) collective-permute-start(bf16[64,3712]{1,0:T(8,128)(2,1)S(1)} %collective-permute-done.25.refs_3_), channel_id=1, source_target_pairs={{0,16},{1,17},{2,18},{3,19},{4,20},{5,21},{6,22},{7,23},{8,24},{9,... | collective-permute-start | bytes 1425416 | tf_op jit(solution)/shard_map/ppermute | solution.py:161
  74.8 14.2 %collective-permute-start.13 = (bf16[64,3584]{1,0:T(8,128)(2,1)S(1)}, bf16[64,3584]{1,0:T(8,128)(2,1)S(1)}, u32[]{:S(2)}, u32[]{:S(2)}) collective-permute-start(bf16[64,3584]{1,0:T(8,128)(2,1)S(1)} %get-tuple-element.25), channel_id=1, source_target_pairs={{0,16},{1,17},{2,18},{3,19},{4,20},{5,21},{6,22},{7,23},{8,24},{9,... | collective-permute-start | bytes 1376264 | tf_op jit(solution)/shard_map/ppermute | solution.py:161
  75.0 29.6 %collective-permute-start.10 = (bf16[64,3584]{1,0:T(8,128)(2,1)S(1)}, bf16[64,3584]{1,0:T(8,128)(2,1)S(1)}, u32[]{:S(2)}, u32[]{:S(2)}) collective-permute-start(bf16[64,3584]{1,0:T(8,128)(2,1)S(1)} %get-tuple-element.21), channel_id=1, source_target_pairs={{0,16},{1,17},{2,18},{3,19},{4,20},{5,21},{6,22},{7,23},{8,24},{9,... | collective-permute-start | bytes 1376264 | tf_op jit(solution)/shard_map/ppermute | solution.py:161
  75.5 14.0 %collective-permute-start.15 = (bf16[64,3584]{1,0:T(8,128)(2,1)S(1)}, bf16[64,3584]{1,0:T(8,128)(2,1)S(1)}, u32[]{:S(2)}, u32[]{:S(2)}) collective-permute-start(bf16[64,3584]{1,0:T(8,128)(2,1)S(1)} %add_convert_fusion.6), channel_id=1, source_target_pairs={{0,1},{1,0},{2,3},{3,2},{4,5},{5,4},{6,7},{7,6},{8,9},{9,8},{10,11... | collective-permute-start | bytes 1376264 | tf_op jit(solution)/shard_map/ppermute | solution.py:161
  76.0 31.4 %collective-permute-start.12 = (bf16[64,3584]{1,0:T(8,128)(2,1)S(1)}, bf16[64,3584]{1,0:T(8,128)(2,1)S(1)}, u32[]{:S(2)}, u32[]{:S(2)}) collective-permute-start(bf16[64,3584]{1,0:T(8,128)(2,1)S(1)} %add_convert_fusion.7), channel_id=1, source_target_pairs={{0,1},{1,0},{2,3},{3,2},{4,5},{5,4},{6,7},{7,6},{8,9},{9,8},{10,11... | collective-permute-start | bytes 1376264 | tf_op jit(solution)/shard_map/ppermute | solution.py:161
  91.4 22.7 %collective-permute-start.30 = (bf16[64,3584]{1,0:T(8,128)(2,1)S(1)}, bf16[64,3584]{1,0:T(8,128)(2,1)S(1)}, u32[]{:S(2)}, u32[]{:S(2)}) collective-permute-start(bf16[64,3584]{1,0:T(8,128)(2,1)S(1)} %get-tuple-element.31), channel_id=1, source_target_pairs={{0,16},{1,17},{2,18},{3,19},{4,20},{5,21},{6,22},{7,23},{8,24},{9,... | collective-permute-start | bytes 1376264 | tf_op jit(solution)/shard_map/ppermute | solution.py:161
  91.7 12.3 %collective-permute-start.35 = (bf16[64,3584]{1,0:T(8,128)(2,1)S(1)}, bf16[64,3584]{1,0:T(8,128)(2,1)S(1)}, u32[]{:S(2)}, u32[]{:S(2)}) collective-permute-start(bf16[64,3584]{1,0:T(8,128)(2,1)S(1)} %add_convert_fusion.2), channel_id=1, source_target_pairs={{0,1},{1,0},{2,3},{3,2},{4,5},{5,4},{6,7},{7,6},{8,9},{9,8},{10,11... | collective-permute-start | bytes 1376264 | tf_op jit(solution)/shard_map/ppermute | solution.py:161
  92.4 15.0 %collective-permute-start.16 = (bf16[64,3584]{1,0:T(8,128)(2,1)S(1)}, bf16[64,3584]{1,0:T(8,128)(2,1)S(1)}, u32[]{:S(2)}, u32[]{:S(2)}) collective-permute-start(bf16[64,3584]{1,0:T(8,128)(2,1)S(1)} %add_convert_fusion.5), channel_id=1, source_target_pairs={{0,2},{1,3},{2,0},{3,1},{4,6},{5,7},{6,4},{7,5},{8,10},{9,11},{10,... | collective-permute-start | bytes 1376264 | tf_op jit(solution)/shard_map/ppermute | solution.py:161
  103.9 13.2 %collective-permute-start.32 = (bf16[64,3584]{1,0:T(8,128)(2,1)S(1)}, bf16[64,3584]{1,0:T(8,128)(2,1)S(1)}, u32[]{:S(2)}, u32[]{:S(2)}) collective-permute-start(bf16[64,3584]{1,0:T(8,128)(2,1)S(1)} %add_convert_fusion.3), channel_id=1, source_target_pairs={{0,1},{1,0},{2,3},{3,2},{4,5},{5,4},{6,7},{7,6},{8,9},{9,8},{10,11... | collective-permute-start | bytes 1376264 | tf_op jit(solution)/shard_map/ppermute | solution.py:161
  104.6 12.5 %collective-permute-start.36 = (bf16[64,3584]{1,0:T(8,128)(2,1)S(1)}, bf16[64,3584]{1,0:T(8,128)(2,1)S(1)}, u32[]{:S(2)}, u32[]{:S(2)}) collective-permute-start(bf16[64,3584]{1,0:T(8,128)(2,1)S(1)} %add_convert_fusion.1), channel_id=1, source_target_pairs={{0,2},{1,3},{2,0},{3,1},{4,6},{5,7},{6,4},{7,5},{8,10},{9,11},{10,... | collective-permute-start | bytes 1376264 | tf_op jit(solution)/shard_map/ppermute | solution.py:161
  107.6 15.8 %collective-permute-start.17 = (bf16[16,3584]{1,0:T(8,128)(2,1)S(1)}, bf16[16,3584]{1,0:T(8,128)(2,1)S(1)}, u32[]{:S(2)}, u32[]{:S(2)}) collective-permute-start(bf16[16,3584]{1,0:T(8,128)(2,1)S(1)} %get-tuple-element.38), channel_id=1, source_target_pairs={{0,12},{1,13},{2,14},{3,15},{4,0},{5,1},{6,2},{7,3},{8,4},{9,5},{1... | collective-permute-start | bytes 344072 | tf_op jit(solution)/shard_map/ppermute | solution.py:161
  112.9 11.2 %collective-permute-start.18 = (bf16[16,3584]{1,0:T(8,128)(2,1)S(1)}, bf16[16,3584]{1,0:T(8,128)(2,1)S(1)}, u32[]{:S(2)}, u32[]{:S(2)}) collective-permute-start(bf16[16,3584]{1,0:T(8,128)(2,1)S(1)} %get-tuple-element.40), channel_id=1, source_target_pairs={{0,8},{1,9},{2,10},{3,11},{4,12},{5,13},{6,14},{7,15},{8,0},{9,1},... | collective-permute-start | bytes 344072 | tf_op jit(solution)/shard_map/ppermute | solution.py:161
  114.1 9.9 %collective-permute-start.19 = (bf16[16,3584]{1,0:T(8,128)(2,1)S(1)}, bf16[16,3584]{1,0:T(8,128)(2,1)S(1)}, u32[]{:S(2)}, u32[]{:S(2)}) collective-permute-start(bf16[16,3584]{1,0:T(8,128)(2,1)S(1)} %get-tuple-element.39), channel_id=1, source_target_pairs={{0,4},{1,5},{2,6},{3,7},{4,8},{5,9},{6,10},{7,11},{8,12},{9,13},{1... | collective-permute-start | bytes 344072 | tf_op jit(solution)/shard_map/ppermute | solution.py:161
  117.4 9.2 %collective-permute-start.37 = (bf16[16,3584]{1,0:T(8,128)(2,1)S(1)}, bf16[16,3584]{1,0:T(8,128)(2,1)S(1)}, u32[]{:S(2)}, u32[]{:S(2)}) collective-permute-start(bf16[16,3584]{1,0:T(8,128)(2,1)S(1)} %get-tuple-element.41), channel_id=1, source_target_pairs={{0,12},{1,13},{2,14},{3,15},{4,0},{5,1},{6,2},{7,3},{8,4},{9,5},{1... | collective-permute-start | bytes 344072 | tf_op jit(solution)/shard_map/ppermute | solution.py:161
  123.4 10.1 %collective-permute-start.38 = (bf16[16,3584]{1,0:T(8,128)(2,1)S(1)}, bf16[16,3584]{1,0:T(8,128)(2,1)S(1)}, u32[]{:S(2)}, u32[]{:S(2)}) collective-permute-start(bf16[16,3584]{1,0:T(8,128)(2,1)S(1)} %get-tuple-element.43), channel_id=1, source_target_pairs={{0,8},{1,9},{2,10},{3,11},{4,12},{5,13},{6,14},{7,15},{8,0},{9,1},... | collective-permute-start | bytes 344072 | tf_op jit(solution)/shard_map/ppermute | solution.py:161
  123.4 10.0 %collective-permute-start.39 = (bf16[16,3584]{1,0:T(8,128)(2,1)S(1)}, bf16[16,3584]{1,0:T(8,128)(2,1)S(1)}, u32[]{:S(2)}, u32[]{:S(2)}) collective-permute-start(bf16[16,3584]{1,0:T(8,128)(2,1)S(1)} %get-tuple-element.42), channel_id=1, source_target_pairs={{0,4},{1,5},{2,6},{3,7},{4,8},{5,9},{6,10},{7,11},{8,12},{9,13},{1... | collective-permute-start | bytes 344072 | tf_op jit(solution)/shard_map/ppermute | solution.py:161
  (18 other events, 206.6 us)

commit v2 on v1

v2 whole, which is shorter than its diff:
```python
import functools

import jax
import jax.numpy as jnp
from jax import lax
from jax.experimental import pallas as pl
from jax.experimental.pallas import tpu as pltpu
from jax.sharding import PartitionSpec as P

score_scale = 192.0 ** (-0.5)
both_axes = ("role", "dev")
chunk_count = 2


def shift_pairs(kind, step, depth, side):
    pairs = []
    for r in range(2):
        for z in range(depth):
            for y in range(side):
                for x in range(side):
                    to_r, to_z, to_y, to_x = r, z, y, x
                    if kind == "role":
                        to_r = 1 - r
                    elif kind == "z":
                        to_z = (z + step) % depth
                    elif (kind == "first") == (r == 0):
                        to_y = (y + step) % side
                    else:
                        to_x = (x + step) % side
                    here = ((r * depth + z) * side + y) * side + x
                    there = ((to_r * depth + to_z) * side + to_y) * side + to_x
                    pairs.append((here, there))
    return pairs


def attend_kernel(lengths_ref, lat_ref, rope_ref, cache_ref, keys_ref, *refs):
    out_ref = refs[-1]
    length = lengths_ref[pl.program_id(0)]
    cache = cache_ref[0]
    scores = lax.dot_general(
        lat_ref[0], cache, (((1,), (1,)), ((), ())), preferred_element_type=jnp.float32
    )
    scores = scores + jnp.dot(rope_ref[0], keys_ref[0], preferred_element_type=jnp.float32)
    scores = scores * score_scale
    valid = lax.broadcasted_iota(jnp.int32, scores.shape, 1) < length
    scores = jnp.where(valid, scores, jnp.float32(-1e30))
    highest = jnp.max(scores, axis=1, keepdims=True)
    weights = jnp.where(valid, jnp.exp(scores - highest), jnp.float32(0.0))
    probs = weights * (1.0 / jnp.sum(weights, axis=1, keepdims=True))
    out_ref[0] = jnp.dot(
        probs.astype(jnp.bfloat16), cache, preferred_element_type=jnp.float32
    ).astype(jnp.bfloat16)


def attend_rows(q_latent, q_rope, latent_cache, rope_cache, lengths, start, count, resident=()):
    heads, latent = q_latent.shape[1:]
    cached = latent_cache.shape[1]
    rope = rope_cache.shape[1]

    def spec(*shape):
        return pl.BlockSpec((1, *shape), lambda at, lengths_ref: (start + at, 0, 0))

    return pl.pallas_call(
        attend_kernel,
        out_shape=jax.ShapeDtypeStruct((count, heads, latent), jnp.bfloat16),
        grid_spec=pltpu.PrefetchScalarGridSpec(
            num_scalar_prefetch=1,
            grid=(count,),
            in_specs=[
                spec(heads, latent),
                spec(heads, rope),
                spec(cached, latent),
                spec(rope, cached),
            ]
            + [pl.BlockSpec(memory_space=pltpu.VMEM)] * len(resident),
            out_specs=pl.BlockSpec((1, heads, latent), lambda at, lengths_ref: (at, 0, 0)),
        ),
        compiler_params=pltpu.CompilerParams(vmem_limit_bytes=(46 if resident else 48) * 1024 * 1024),
        cost_estimate=pl.CostEstimate(
            flops=2 * count * heads * cached * (2 * latent + rope),
            bytes_accessed=2 * count * cached * (latent + rope),
            transcendentals=count * heads * cached,
        ),
        name="attend_rows",
    )(lengths[start : start + count], q_latent, q_rope, latent_cache, rope_cache, *resident)


def expert_kernel(count, lane_ref, *refs):
    blocks, refs = refs[:count], refs[count:]
    (gate_mat, up_mat, down_mat), refs = refs[:3], refs[3:]
    results, (hidden,) = refs[:count], refs[count:]
    block = blocks[0].shape[0]
    width, units = gate_mat.shape
    tile, slab = units // 2, width // 2
    chosen = jnp.concatenate([rows[:, :width] for rows in blocks], axis=0)
    tails = jnp.concatenate([rows[:, width:] for rows in blocks], axis=0)
    row_gates = jnp.sum(tails.astype(jnp.float32) * lane_ref[...], axis=1, keepdims=True)
    for piece in range(2):
        lanes = pl.ds(piece * tile, tile)
        gate_part = jnp.dot(chosen, gate_mat[:, lanes], preferred_element_type=jnp.float32)
        up_part = jnp.dot(chosen, up_mat[:, lanes], preferred_element_type=jnp.float32)
        silu = gate_part / (1.0 + jnp.exp(-gate_part))
        hidden[:, lanes] = (silu * up_part).astype(jnp.bfloat16)
    for piece in range(2):
        lanes = pl.ds(piece * slab, slab)
        result = lax.dot_general(
            hidden[...],
            down_mat[lanes, :],
            (((1,), (1,)), ((), ())),
            preferred_element_type=jnp.float32,
        )
        result = (result * row_gates).astype(jnp.bfloat16)
        for at in range(count):
            results[at][:, lanes] = result[at * block : (at + 1) * block]


def expert_blocks(blocks, gate_matrix, up_matrix, down_matrix, own_lane):
    count = len(blocks)
    block = blocks[0].shape[0]
    width, units = gate_matrix.shape
    total = count * block
    inside = pl.BlockSpec(memory_space=pltpu.VMEM)
    return pl.pallas_call(
        functools.partial(expert_kernel, count),
        out_shape=[jax.ShapeDtypeStruct((block, width), jnp.bfloat16)] * count,
        in_specs=[inside] * (count + 4),
        out_specs=[inside] * count,
        scratch_shapes=[pltpu.VMEM((total, units), jnp.bfloat16)],
        compiler_params=pltpu.CompilerParams(vmem_limit_bytes=10 * 1024 * 1024),
        cost_estimate=pl.CostEstimate(
            flops=6 * total * width * units,
            bytes_accessed=6 * width * units + 4 * total * width,
            transcendentals=total * units,
        ),
        name="expert_blocks",
    )(own_lane, *blocks, gate_matrix, up_matrix, down_matrix)


def after(value, *earlier):
    return lax.optimization_barrier((value, *earlier))[0]


def per_device(
    moe_rows,
    expert_ids,
    gate_weights,
    w_gate,
    w_up,
    w_down,
    q_latent,
    q_rope,
    latent_cache,
    rope_cache,
    lengths,
):
    tok_count, width = moe_rows.shape
    experts = lax.axis_size("dev")
    side = 1
    while experts % (4 * side * side) == 0 and (2 * side) ** 2 * 4 <= experts:
        side *= 2
    depth = experts // (side * side)
    chunk = tok_count // chunk_count
    block = depth * chunk

    def send(value, kind, step=1):
        return lax.ppermute(value, both_axes, shift_pairs(kind, step, depth, side))

    place = lax.axis_index("dev")
    named = expert_ids[:, :, None] == jnp.arange(experts, dtype=jnp.int32)[None, None, :]
    dense_gates = jnp.sum(jnp.where(named, gate_weights[:, :, None], 0.0), axis=1)
    kept_part = lax.reduce_precision(dense_gates, exponent_bits=8, mantissa_bits=7)
    upper = kept_part.astype(jnp.bfloat16)
    lower = (dense_gates - kept_part).astype(jnp.bfloat16)
    spare = -(2 * experts) % 128
    tail = jnp.concatenate([upper, lower, jnp.zeros((tok_count, spare), jnp.bfloat16)], axis=1)
    tail_width = tail.shape[1]
    payload = jnp.concatenate([moe_rows, tail], axis=1)
    lane = jnp.arange(tail_width, dtype=jnp.int32)
    own_lane = ((lane == place) | (lane == place + experts)).astype(jnp.float32)[None, :]
    payload = after(payload, own_lane)

    att_rows = lengths.shape[0]
    rope_rows = q_rope.reshape(att_rows, q_latent.shape[1], rope_cache.shape[1])
    att_half = att_rows // 2

    matrices = (w_gate[0], w_up[0], w_down[0])

    def attend(start, key, resident=()):
        return attend_rows(
            q_latent, key, latent_cache, rope_cache, lengths, start, att_half, resident
        )

    def pieces(c):
        return payload[c * chunk : (c + 1) * chunk]

    def along(mine):
        return [mine] + [send(mine, "z", k) for k in range(1, depth)]

    early = attend(0, rope_rows)
    gathered = []
    coming = along(pieces(0))
    coming[1] = after(coming[1], early)
    last = None
    for c in range(chunk_count):
        line = jnp.concatenate(coming, axis=0)
        if last is not None:
            line = after(line, last)
        if c + 1 < chunk_count:
            coming = along(after(pieces(c + 1), line))
        first = [line] + [send(line, "first", k) for k in range(1, side)]
        if c == 0:
            late = attend(att_half, after(rope_rows, line))
            first[1] = after(first[1], late, *coming)
        blocks = list(first)
        for k in range(1, side):
            blocks += [send(part, "last", k) for part in first]
        last = blocks[-1]
        gathered.append(blocks + [send(part, "role") for part in blocks])

    finished = []
    summed = None
    for c in range(chunk_count):
        half = len(gathered[c]) // 2
        own, other = gathered[c][:half], gathered[c][half:]
        if summed is not None:
            other = [after(other[0], summed)] + other[1:]

        def expert(blocks):
            results = []
            for at in range(0, half, 4):
                results += expert_blocks(blocks[at : at + 4], *matrices, own_lane)
            return results

        theirs = [send(part, "role") for part in expert(other)]
        if c + 1 < chunk_count:
            following = gathered[c + 1]
            own = [after(own[0], following[1], following[side])] + own[1:]
        mine = expert(own)
        whole = [a.astype(jnp.float32) + b.astype(jnp.float32) for a, b in zip(mine, theirs)]
        whole = [whole[k * side : (k + 1) * side] for k in range(side)]
        sent = [[part.astype(jnp.bfloat16) for part in row] for row in whole]
        summed = sent[side - 1][side - 1]
        kept = {}
        for a in reversed(range(side)):
            total = whole[0][a]
            for k in range(1, side):
                total = total + send(sent[k][a], "last", -k).astype(jnp.float32)
            kept[a] = total
        total = kept[0]
        for k in range(1, side):
            total = total + send(kept[k].astype(jnp.bfloat16), "first", -k).astype(jnp.float32)
        line = total.astype(jnp.bfloat16).reshape(depth, chunk, width)
        total = line[0].astype(jnp.float32)
        for k in range(1, depth):
            total = total + send(line[k], "z", -k).astype(jnp.float32)
        finished.append(total.astype(jnp.bfloat16))
    moe_out = jnp.concatenate(finished, axis=0)
    attended = jnp.concatenate([early, late], axis=0)
    return (moe_out, attended)


def solution(mesh):
    placed = (
        P(("role", "dev"), None),
        P(("role", "dev"), None),
        P(("role", "dev"), None),
        P("dev", None, "role"),
        P("dev", None, "role"),
        P("dev", None, "role"),
        P(("role", "dev"), None, None),
        P(("role", "dev"), None),
        P(("role", "dev"), None, None),
        P(("role", "dev"), None, None),
        P(("role", "dev")),
    )
    return jax.shard_map(
        per_device,
        mesh=mesh,
        in_specs=placed,
        out_specs=(P(("role", "dev"), None), P(("role", "dev"), None, None)),
        check_vma=False,
    )
```

time: 135 us -> 116 us (0.86)
  matrix products: 17.2 us -> 0 us
  starting transfers between devices: 43.8 us -> 37.9 us
  waiting for transfers between devices: 39.9 us -> 45.2 us
  local copies, waits for them, and re-layouts: 7.57 us -> 5.11 us
    dot_general x2 -> x0, matrix products: 13.3 us -> none  [the longest x1 7.44 us: attend_row(): lax.dot_general(query_lat, cache_lat, (((1,), (1,)), ((), ())), preferred...]
    pallas_call x0 -> x2, Pallas kernels: none -> 10.7 us  [attend_rows(): pl.pallas_call(attend_kernel, out_shape=jax.ShapeDtypeStruct((count, head...]
    pallas_call x2 -> x4, Pallas kernels: 22 us -> 12.3 us  [expert_blocks(): pl.pallas_call(functools.partial(expert_kernel, count), out_shape=[jax.Sh...]
    ppermute x40, starting transfers between devices: 43.8 us -> 37.9 us  [send(): return lax.ppermute(value, both_axes, shift_pairs(kind, step, depth, side))]
    ppermute x40, waiting for transfers between devices: 39.9 us -> 45.2 us  [send(): return lax.ppermute(value, both_axes, shift_pairs(kind, step, depth, side))]
    unnamed x23 -> x14, local copies, waits for them, and re-layouts: 6.18 us -> 2.19 us
    sub x1 -> x0, matrix products: 3.87 us -> none  [attend_row(): weights = jnp.where(valid, jnp.exp(scores - highest), jnp.float32(0.0))]
  transfers between devices with their start and end apart: 40 -> 40, of which waited for: 10 -> 12; matrix products, arithmetic and copies ran while one was open for 14% -> 3% of each run, Pallas kernels for 16% -> 20%
where the time goes in v2:
time: 116 us
  waiting for transfers between devices  45.2 us (39%)
  starting transfers between devices  37.9 us (33%)
  Pallas kernels  23 us (20%)
  local copies, waits for them, and re-layouts  5.11 us (4%)
  other arithmetic  3.59 us (3%)
    ppermute x40, waiting for transfers between devices, send(): return lax.ppermute(value, both_axes, shift_pairs(kind, step, depth, side))  45.2 us
    ppermute x40, starting transfers between devices, send(): return lax.ppermute(value, both_axes, shift_pairs(kind, step, depth, side))  37.9 us
    pallas_call x4, Pallas kernels, expert_blocks(): pl.pallas_call(functools.partial(expert_kernel, count), out_shape=[jax.Sh...  12.3 us
    pallas_call x2, Pallas kernels, attend_rows(): pl.pallas_call(attend_kernel, out_shape=jax.ShapeDtypeStruct((count, head...  10.7 us
  transfers between devices with their start and end apart: 40, of which 12 were waited for; matrix products, arithmetic and copies ran while one was open for 3% of the time, Pallas kernels for 20%

profile of v2, /device:TPU:0, one launch (start us, length us, event | category | flops | bytes accessed | tf_op | source)
XLA Modules:
  0.0 115.8 jit_solution(17150452706374266364)
XLA Ops:
  2.6 3.1 %collective-permute-start = (bf16[16,3712]{1,0:T(8,128)(2,1)S(1)}, bf16[16,3712]{1,0:T(8,128)(2,1)S(1)}, u32[]{:S(2)}, u32[]{:S(2)}) collective-permute-start(bf16[16,3712]{1,0:T(8,128)(2,1)S(1)} %get-tuple-element.56), channel_id=1, source_target_pairs={{0,4},{1,5},{2,6},{3,7},{4,8},{5,9},{6,10},{7,11},{8,12},{9,13},{1... | collective-permute-start | bytes 356360 | tf_op jit(solution)/shard_map/ppermute | solution.py:166
  5.7 2.6 %collective-permute-start.1 = (bf16[16,3712]{1,0:T(8,128)(2,1)S(1)}, bf16[16,3712]{1,0:T(8,128)(2,1)S(1)}, u32[]{:S(2)}, u32[]{:S(2)}) collective-permute-start(bf16[16,3712]{1,0:T(8,128)(2,1)S(1)} %get-tuple-element.56), channel_id=1, source_target_pairs={{0,8},{1,9},{2,10},{3,11},{4,12},{5,13},{6,14},{7,15},{8,0},{9,1},... | collective-permute-start | bytes 356360 | tf_op jit(solution)/shard_map/ppermute | solution.py:166
  8.3 1.3 %collective-permute-start.2 = (bf16[16,3712]{1,0:T(8,128)(2,1)S(1)}, bf16[16,3712]{1,0:T(8,128)(2,1)S(1)}, u32[]{:S(2)}, u32[]{:S(2)}) collective-permute-start(bf16[16,3712]{1,0:T(8,128)(2,1)S(1)} %get-tuple-element.56), channel_id=1, source_target_pairs={{0,12},{1,13},{2,14},{3,15},{4,0},{5,1},{6,2},{7,3},{8,4},{9,5},{1... | collective-permute-start | bytes 356360 | tf_op jit(solution)/shard_map/ppermute | solution.py:166
  11.3 1.2 %copy-done.3 = bf16[4,64,2048]{2,1,0:T(8,128)(2,1)S(1)} copy-done((bf16[4,64,2048]{2,1,0:T(8,128)(2,1)S(1)}, bf16[4,64,2048]{2,1,0:T(8,128)(2,1)}, u32[]{:S(2)}) %copy-start.3) | copy-done | bytes 1048600
  13.5 5.1 %attend_rows.2 = bf16[2,64,512]{2,1,0:T(8,128)(2,1)S(1)} custom-call(s32[2]{0:T(128)S(1)} %get-tuple-element.61.lengths_ref, bf16[4,64,512]{2,1,0:T(8,128)(2,1)S(1)} %copy-done.5, bf16[4,64,64]{2,1,0:T(8,128)(2,1)S(1)} %reshape.46.rope_ref, bf16[4,2048,512]{2,1,0:T(8,128)(2,1)} %cache_ref.3, bf16[4,64,2048]{2,1,0:T(8,128)(2,1)S(1)} %copy-done.3), custom_call_target="tpu_custom_call" | custom-call | flops 570425344 | bytes 4718592 | tf_op jit(solution)/shard_map/attend_rows/pallas_call | solution.py:63
  18.7 1.6 %collective-permute-start.6 = (bf16[64,3712]{1,0:T(8,128)(2,1)S(1)}, bf16[64,3712]{1,0:T(8,128)(2,1)S(1)}, u32[]{:S(2)}, u32[]{:S(2)}) collective-permute-start(bf16[64,3712]{1,0:T(8,128)(2,1)S(1)} %pad_maximum_fusion.refs_0_), channel_id=1, source_target_pairs={{0,2},{1,3},{2,0},{3,1},{4,6},{5,7},{6,4},{7,5},{8,10},{9,11},{10,... | collective-permute-start | bytes 1425416 | tf_op jit(solution)/shard_map/ppermute | solution.py:166
  21.0 1.4 %collective-permute-start.4 = (bf16[16,3712]{1,0:T(8,128)(2,1)S(1)}, bf16[16,3712]{1,0:T(8,128)(2,1)S(1)}, u32[]{:S(2)}, u32[]{:S(2)}) collective-permute-start(bf16[16,3712]{1,0:T(8,128)(2,1)S(1)} %get-tuple-element.28), channel_id=1, source_target_pairs={{0,8},{1,9},{2,10},{3,11},{4,12},{5,13},{6,14},{7,15},{8,0},{9,1},... | collective-permute-start | bytes 356360 | tf_op jit(solution)/shard_map/ppermute | solution.py:166
  22.4 1.7 %collective-permute-start.5 = (bf16[16,3712]{1,0:T(8,128)(2,1)S(1)}, bf16[16,3712]{1,0:T(8,128)(2,1)S(1)}, u32[]{:S(2)}, u32[]{:S(2)}) collective-permute-start(bf16[16,3712]{1,0:T(8,128)(2,1)S(1)} %get-tuple-element.28), channel_id=1, source_target_pairs={{0,12},{1,13},{2,14},{3,15},{4,0},{5,1},{6,2},{7,3},{8,4},{9,5},{1... | collective-permute-start | bytes 356360 | tf_op jit(solution)/shard_map/ppermute | solution.py:166
  24.1 1.5 %collective-permute-start.10 = (bf16[64,3712]{1,0:T(8,128)(2,1)S(1)}, bf16[64,3712]{1,0:T(8,128)(2,1)S(1)}, u32[]{:S(2)}, u32[]{:S(2)}) collective-permute-start(bf16[64,3712]{1,0:T(8,128)(2,1)S(1)} %pad_maximum_fusion.refs_0_), channel_id=1, source_target_pairs={{0,1},{1,0},{2,3},{3,2},{4,5},{5,4},{6,7},{7,6},{8,9},{9,8},{10,11... | collective-permute-start | bytes 1425416 | tf_op jit(solution)/shard_map/ppermute | solution.py:166
  25.6 5.6 %attend_rows.3 = bf16[2,64,512]{2,1,0:T(8,128)(2,1)S(1)} custom-call(s32[2]{0:T(128)S(1)} %get-tuple-element.60.lengths_ref, bf16[4,64,512]{2,1,0:T(8,128)(2,1)S(1)} %copy-done.6, bf16[4,64,64]{2,1,0:T(8,128)(2,1)S(1)} %reshape.46.rope_ref, bf16[4,2048,512]{2,1,0:T(8,128)(2,1)} %cache_ref.3, bf16[4,64,2048]{2,1,0:T(8,128)(2,1)S(1)} %copy-done.4), custom_call_target="tpu_custom_call" | custom-call | flops 570425344 | bytes 4718592 | tf_op jit(solution)/shard_map/attend_rows/pallas_call | solution.py:63
  32.9 7.1 %collective-permute-done.7.refs_3_ = bf16[64,3712]{1,0:T(8,128)(2,1)S(1)} collective-permute-done((bf16[64,3712]{1,0:T(8,128)(2,1)S(1)}, bf16[64,3712]{1,0:T(8,128)(2,1)S(1)}, u32[]{:S(2)}, u32[]{:S(2)}) %collective-permute-start.7) | collective-permute-done | bytes 475168 | tf_op jit(solution)/shard_map/ppermute | solution.py:166
  40.0 1.4 %collective-permute-start.8 = (bf16[64,3712]{1,0:T(8,128)(2,1)S(1)}, bf16[64,3712]{1,0:T(8,128)(2,1)S(1)}, u32[]{:S(2)}, u32[]{:S(2)}) collective-permute-start(bf16[64,3712]{1,0:T(8,128)(2,1)S(1)} %pad_maximum_fusion.1.refs_0_), channel_id=1, source_target_pairs={{0,2},{1,3},{2,0},{3,1},{4,6},{5,7},{6,4},{7,5},{8,10},{9,11},{10,... | collective-permute-start | bytes 1425416 | tf_op jit(solution)/shard_map/ppermute | solution.py:166
  41.4 1.2 %collective-permute-start.9 = (bf16[64,3712]{1,0:T(8,128)(2,1)S(1)}, bf16[64,3712]{1,0:T(8,128)(2,1)S(1)}, u32[]{:S(2)}, u32[]{:S(2)}) collective-permute-start(bf16[64,3712]{1,0:T(8,128)(2,1)S(1)} %pad_maximum_fusion.1.refs_0_), channel_id=1, source_target_pairs={{0,1},{1,0},{2,3},{3,2},{4,5},{5,4},{6,7},{7,6},{8,9},{9,8},{10,11... | collective-permute-start | bytes 1425416 | tf_op jit(solution)/shard_map/ppermute | solution.py:166
  42.6 3.1 %expert_blocks.5 = (bf16[64,3584]{1,0:T(8,128)(2,1)S(1)}, bf16[64,3584]{1,0:T(8,128)(2,1)S(1)}, bf16[64,3584]{1,0:T(8,128)(2,1)S(1)}, bf16[64,3584]{1,0:T(8,128)(2,1)S(1)}) custom-call(f32[1,128]{1,0:T(1,128)S(1)} %or_convert_fusion.lane_ref, bf16[64,3712]{1,0:T(8,128)(2,1)S(1)} %collective-permute-done.11.refs_0_, ...), custom_call_target="tpu_custom_call" | custom-call | flops 2818572288 | bytes 14680064 | tf_op jit(solution)/shard_map/expert_blocks/pallas_call | solution.py:123
  47.0 6.5 %collective-permute-done.8.refs_1_ = bf16[64,3712]{1,0:T(8,128)(2,1)S(1)} collective-permute-done((bf16[64,3712]{1,0:T(8,128)(2,1)S(1)}, bf16[64,3712]{1,0:T(8,128)(2,1)S(1)}, u32[]{:S(2)}, u32[]{:S(2)}) %collective-permute-start.8) | collective-permute-done | bytes 475168 | tf_op jit(solution)/shard_map/ppermute | solution.py:166
  54.2 3.1 %expert_blocks.4 = (bf16[64,3584]{1,0:T(8,128)(2,1)S(1)}, bf16[64,3584]{1,0:T(8,128)(2,1)S(1)}, bf16[64,3584]{1,0:T(8,128)(2,1)S(1)}, bf16[64,3584]{1,0:T(8,128)(2,1)S(1)}) custom-call(f32[1,128]{1,0:T(1,128)S(1)} %or_convert_fusion.lane_ref, bf16[64,3712]{1,0:T(8,128)(2,1)S(1)} %pad_maximum_fusion.refs_0_, ...), custom_call_target="tpu_custom_call" | custom-call | flops 2818572288 | bytes 14680064 | tf_op jit(solution)/shard_map/expert_blocks/pallas_call | solution.py:123
  60.2 5.7 %collective-permute-done.25.refs_3_ = bf16[64,3712]{1,0:T(8,128)(2,1)S(1)} collective-permute-done((bf16[64,3712]{1,0:T(8,128)(2,1)S(1)}, bf16[64,3712]{1,0:T(8,128)(2,1)S(1)}, u32[]{:S(2)}, u32[]{:S(2)}) %collective-permute-start.25) | collective-permute-done | bytes 475168 | tf_op jit(solution)/shard_map/ppermute | solution.py:166
  67.0 3.8 %collective-permute-done.20 = bf16[64,3584]{1,0:T(8,128)(2,1)S(1)} collective-permute-done((bf16[64,3584]{1,0:T(8,128)(2,1)S(1)}, bf16[64,3584]{1,0:T(8,128)(2,1)S(1)}, u32[]{:S(2)}, u32[]{:S(2)}) %collective-permute-start.20) | collective-permute-done | bytes 458784 | tf_op jit(solution)/shard_map/ppermute | solution.py:166
  71.0 1.4 %collective-permute-start.21 = (bf16[64,3584]{1,0:T(8,128)(2,1)S(1)}, bf16[64,3584]{1,0:T(8,128)(2,1)S(1)}, u32[]{:S(2)}, u32[]{:S(2)}) collective-permute-start(bf16[64,3584]{1,0:T(8,128)(2,1)S(1)} %add_convert_fusion.5), channel_id=1, source_target_pairs={{0,2},{1,3},{2,0},{3,1},{4,6},{5,7},{6,4},{7,5},{8,10},{9,11},{10,... | collective-permute-start | bytes 1376264 | tf_op jit(solution)/shard_map/ppermute | solution.py:166
  72.4 3.1 %expert_blocks.6 = (bf16[64,3584]{1,0:T(8,128)(2,1)S(1)}, bf16[64,3584]{1,0:T(8,128)(2,1)S(1)}, bf16[64,3584]{1,0:T(8,128)(2,1)S(1)}, bf16[64,3584]{1,0:T(8,128)(2,1)S(1)}) custom-call(f32[1,128]{1,0:T(1,128)S(1)} %or_convert_fusion.lane_ref, bf16[64,3712]{1,0:T(8,128)(2,1)S(1)} %pad_maximum_fusion.1.refs_0_, ...), custom_call_target="tpu_custom_call" | custom-call | flops 2818572288 | bytes 14680064 | tf_op jit(solution)/shard_map/expert_blocks/pallas_call | solution.py:123
  75.5 3.1 %expert_blocks.7 = (bf16[64,3584]{1,0:T(8,128)(2,1)S(1)}, bf16[64,3584]{1,0:T(8,128)(2,1)S(1)}, bf16[64,3584]{1,0:T(8,128)(2,1)S(1)}, bf16[64,3584]{1,0:T(8,128)(2,1)S(1)}) custom-call(f32[1,128]{1,0:T(1,128)S(1)} %or_convert_fusion.lane_ref, bf16[64,3712]{1,0:T(8,128)(2,1)S(1)} %collective-permute-done.26.refs_0_, ...), custom_call_target="tpu_custom_call" | custom-call | flops 2818572288 | bytes 14680064 | tf_op jit(solution)/shard_map/expert_blocks/pallas_call | solution.py:123
  81.3 1.5 %collective-permute-start.35 = (bf16[64,3584]{1,0:T(8,128)(2,1)S(1)}, bf16[64,3584]{1,0:T(8,128)(2,1)S(1)}, u32[]{:S(2)}, u32[]{:S(2)}) collective-permute-start(bf16[64,3584]{1,0:T(8,128)(2,1)S(1)} %add_convert_fusion.2), channel_id=1, source_target_pairs={{0,1},{1,0},{2,3},{3,2},{4,5},{5,4},{6,7},{7,6},{8,9},{9,8},{10,11... | collective-permute-start | bytes 1376264 | tf_op jit(solution)/shard_map/ppermute | solution.py:166
  83.5 6.3 %collective-permute-done.35 = bf16[64,3584]{1,0:T(8,128)(2,1)S(1)} collective-permute-done((bf16[64,3584]{1,0:T(8,128)(2,1)S(1)}, bf16[64,3584]{1,0:T(8,128)(2,1)S(1)}, u32[]{:S(2)}, u32[]{:S(2)}) %collective-permute-start.35) | collective-permute-done | bytes 458784 | tf_op jit(solution)/shard_map/ppermute | solution.py:166
  90.0 1.4 %collective-permute-start.36 = (bf16[64,3584]{1,0:T(8,128)(2,1)S(1)}, bf16[64,3584]{1,0:T(8,128)(2,1)S(1)}, u32[]{:S(2)}, u32[]{:S(2)}) collective-permute-start(bf16[64,3584]{1,0:T(8,128)(2,1)S(1)} %add_convert_fusion.1), channel_id=1, source_target_pairs={{0,2},{1,3},{2,0},{3,1},{4,6},{5,7},{6,4},{7,5},{8,10},{9,11},{10,... | collective-permute-start | bytes 1376264 | tf_op jit(solution)/shard_map/ppermute | solution.py:166
  91.4 2.2 %collective-permute-start.22 = (bf16[16,3584]{1,0:T(8,128)(2,1)S(1)}, bf16[16,3584]{1,0:T(8,128)(2,1)S(1)}, u32[]{:S(2)}, u32[]{:S(2)}) collective-permute-start(bf16[16,3584]{1,0:T(8,128)(2,1)S(1)} %get-tuple-element.50), channel_id=1, source_target_pairs={{0,12},{1,13},{2,14},{3,15},{4,0},{5,1},{6,2},{7,3},{8,4},{9,5},{1... | collective-permute-start | bytes 344072 | tf_op jit(solution)/shard_map/ppermute | solution.py:166
  93.6 1.7 %collective-permute-start.23 = (bf16[16,3584]{1,0:T(8,128)(2,1)S(1)}, bf16[16,3584]{1,0:T(8,128)(2,1)S(1)}, u32[]{:S(2)}, u32[]{:S(2)}) collective-permute-start(bf16[16,3584]{1,0:T(8,128)(2,1)S(1)} %get-tuple-element.52), channel_id=1, source_target_pairs={{0,8},{1,9},{2,10},{3,11},{4,12},{5,13},{6,14},{7,15},{8,0},{9,1},... | collective-permute-start | bytes 344072 | tf_op jit(solution)/shard_map/ppermute | solution.py:166
  95.3 2.2 %collective-permute-done.32 = bf16[64,3584]{1,0:T(8,128)(2,1)S(1)} collective-permute-done((bf16[64,3584]{1,0:T(8,128)(2,1)S(1)}, bf16[64,3584]{1,0:T(8,128)(2,1)S(1)}, u32[]{:S(2)}, u32[]{:S(2)}) %collective-permute-start.32) | collective-permute-done | bytes 458784 | tf_op jit(solution)/shard_map/ppermute | solution.py:166
  97.4 1.3 %collective-permute-done.36 = bf16[64,3584]{1,0:T(8,128)(2,1)S(1)} collective-permute-done((bf16[64,3584]{1,0:T(8,128)(2,1)S(1)}, bf16[64,3584]{1,0:T(8,128)(2,1)S(1)}, u32[]{:S(2)}, u32[]{:S(2)}) %collective-permute-start.36) | collective-permute-done | bytes 458784 | tf_op jit(solution)/shard_map/ppermute | solution.py:166
  99.1 3.0 %collective-permute-start.37 = (bf16[16,3584]{1,0:T(8,128)(2,1)S(1)}, bf16[16,3584]{1,0:T(8,128)(2,1)S(1)}, u32[]{:S(2)}, u32[]{:S(2)}) collective-permute-start(bf16[16,3584]{1,0:T(8,128)(2,1)S(1)} %get-tuple-element.53), channel_id=1, source_target_pairs={{0,12},{1,13},{2,14},{3,15},{4,0},{5,1},{6,2},{7,3},{8,4},{9,5},{1... | collective-permute-start | bytes 344072 | tf_op jit(solution)/shard_map/ppermute | solution.py:166
  102.1 1.6 %collective-permute-start.38 = (bf16[16,3584]{1,0:T(8,128)(2,1)S(1)}, bf16[16,3584]{1,0:T(8,128)(2,1)S(1)}, u32[]{:S(2)}, u32[]{:S(2)}) collective-permute-start(bf16[16,3584]{1,0:T(8,128)(2,1)S(1)} %get-tuple-element.55), channel_id=1, source_target_pairs={{0,8},{1,9},{2,10},{3,11},{4,12},{5,13},{6,14},{7,15},{8,0},{9,1},... | collective-permute-start | bytes 344072 | tf_op jit(solution)/shard_map/ppermute | solution.py:166
  104.8 2.3 %collective-permute-done.37 = bf16[16,3584]{1,0:T(8,128)(2,1)S(1)} collective-permute-done((bf16[16,3584]{1,0:T(8,128)(2,1)S(1)}, bf16[16,3584]{1,0:T(8,128)(2,1)S(1)}, u32[]{:S(2)}, u32[]{:S(2)}) %collective-permute-start.37) | collective-permute-done | bytes 114720 | tf_op jit(solution)/shard_map/ppermute | solution.py:166
  107.0 8.0 %collective-permute-done.38 = bf16[16,3584]{1,0:T(8,128)(2,1)S(1)} collective-permute-done((bf16[16,3584]{1,0:T(8,128)(2,1)S(1)}, bf16[16,3584]{1,0:T(8,128)(2,1)S(1)}, u32[]{:S(2)}, u32[]{:S(2)}) %collective-permute-start.38) | collective-permute-done | bytes 114720 | tf_op jit(solution)/shard_map/ppermute | solution.py:166
  (95 shorter events, 18.9 us)
Async XLA Ops:
  2.6 16.0 %collective-permute-start = (bf16[16,3712]{1,0:T(8,128)(2,1)S(1)}, bf16[16,3712]{1,0:T(8,128)(2,1)S(1)}, u32[]{:S(2)}, u32[]{:S(2)}) collective-permute-start(bf16[16,3712]{1,0:T(8,128)(2,1)S(1)} %get-tuple-element.56), channel_id=1, source_target_pairs={{0,4},{1,5},{2,6},{3,7},{4,8},{5,9},{6,10},{7,11},{8,12},{9,13},{1... | collective-permute-start | bytes 356360 | tf_op jit(solution)/shard_map/ppermute | solution.py:166
  5.7 12.9 %collective-permute-start.1 = (bf16[16,3712]{1,0:T(8,128)(2,1)S(1)}, bf16[16,3712]{1,0:T(8,128)(2,1)S(1)}, u32[]{:S(2)}, u32[]{:S(2)}) collective-permute-start(bf16[16,3712]{1,0:T(8,128)(2,1)S(1)} %get-tuple-element.56), channel_id=1, source_target_pairs={{0,8},{1,9},{2,10},{3,11},{4,12},{5,13},{6,14},{7,15},{8,0},{9,1},... | collective-permute-start | bytes 356360 | tf_op jit(solution)/shard_map/ppermute | solution.py:166
  8.3 10.4 %collective-permute-start.2 = (bf16[16,3712]{1,0:T(8,128)(2,1)S(1)}, bf16[16,3712]{1,0:T(8,128)(2,1)S(1)}, u32[]{:S(2)}, u32[]{:S(2)}) collective-permute-start(bf16[16,3712]{1,0:T(8,128)(2,1)S(1)} %get-tuple-element.56), channel_id=1, source_target_pairs={{0,12},{1,13},{2,14},{3,15},{4,0},{5,1},{6,2},{7,3},{8,4},{9,5},{1... | collective-permute-start | bytes 356360 | tf_op jit(solution)/shard_map/ppermute | solution.py:166
  18.7 12.5 %collective-permute-start.6 = (bf16[64,3712]{1,0:T(8,128)(2,1)S(1)}, bf16[64,3712]{1,0:T(8,128)(2,1)S(1)}, u32[]{:S(2)}, u32[]{:S(2)}) collective-permute-start(bf16[64,3712]{1,0:T(8,128)(2,1)S(1)} %pad_maximum_fusion.refs_0_), channel_id=1, source_target_pairs={{0,2},{1,3},{2,0},{3,1},{4,6},{5,7},{6,4},{7,5},{8,10},{9,11},{10,... | collective-permute-start | bytes 1425416 | tf_op jit(solution)/shard_map/ppermute | solution.py:166
  20.3 10.9 %collective-permute-start.3 = (bf16[16,3712]{1,0:T(8,128)(2,1)S(1)}, bf16[16,3712]{1,0:T(8,128)(2,1)S(1)}, u32[]{:S(2)}, u32[]{:S(2)}) collective-permute-start(bf16[16,3712]{1,0:T(8,128)(2,1)S(1)} %get-tuple-element.28), channel_id=1, source_target_pairs={{0,4},{1,5},{2,6},{3,7},{4,8},{5,9},{6,10},{7,11},{8,12},{9,13},{1... | collective-permute-start | bytes 356360 | tf_op jit(solution)/shard_map/ppermute | solution.py:166
  21.0 10.2 %collective-permute-start.4 = (bf16[16,3712]{1,0:T(8,128)(2,1)S(1)}, bf16[16,3712]{1,0:T(8,128)(2,1)S(1)}, u32[]{:S(2)}, u32[]{:S(2)}) collective-permute-start(bf16[16,3712]{1,0:T(8,128)(2,1)S(1)} %get-tuple-element.28), channel_id=1, source_target_pairs={{0,8},{1,9},{2,10},{3,11},{4,12},{5,13},{6,14},{7,15},{8,0},{9,1},... | collective-permute-start | bytes 356360 | tf_op jit(solution)/shard_map/ppermute | solution.py:166
  22.4 8.8 %collective-permute-start.5 = (bf16[16,3712]{1,0:T(8,128)(2,1)S(1)}, bf16[16,3712]{1,0:T(8,128)(2,1)S(1)}, u32[]{:S(2)}, u32[]{:S(2)}) collective-permute-start(bf16[16,3712]{1,0:T(8,128)(2,1)S(1)} %get-tuple-element.28), channel_id=1, source_target_pairs={{0,12},{1,13},{2,14},{3,15},{4,0},{5,1},{6,2},{7,3},{8,4},{9,5},{1... | collective-permute-start | bytes 356360 | tf_op jit(solution)/shard_map/ppermute | solution.py:166
  24.1 8.7 %collective-permute-start.10 = (bf16[64,3712]{1,0:T(8,128)(2,1)S(1)}, bf16[64,3712]{1,0:T(8,128)(2,1)S(1)}, u32[]{:S(2)}, u32[]{:S(2)}) collective-permute-start(bf16[64,3712]{1,0:T(8,128)(2,1)S(1)} %pad_maximum_fusion.refs_0_), channel_id=1, source_target_pairs={{0,1},{1,0},{2,3},{3,2},{4,5},{5,4},{6,7},{7,6},{8,9},{9,8},{10,11... | collective-permute-start | bytes 1425416 | tf_op jit(solution)/shard_map/ppermute | solution.py:166
  31.2 8.7 %collective-permute-start.7 = (bf16[64,3712]{1,0:T(8,128)(2,1)S(1)}, bf16[64,3712]{1,0:T(8,128)(2,1)S(1)}, u32[]{:S(2)}, u32[]{:S(2)}) collective-permute-start(bf16[64,3712]{1,0:T(8,128)(2,1)S(1)} %collective-permute-done.6.refs_1_), channel_id=1, source_target_pairs={{0,1},{1,0},{2,3},{3,2},{4,5},{5,4},{6,7},{7,6},{8,9},{9,8},{10,11... | collective-permute-start | bytes 1425416 | tf_op jit(solution)/shard_map/ppermute | solution.py:166
  32.4 9.0 %collective-permute-start.11 = (bf16[64,3712]{1,0:T(8,128)(2,1)S(1)}, bf16[64,3712]{1,0:T(8,128)(2,1)S(1)}, u32[]{:S(2)}, u32[]{:S(2)}) collective-permute-start(bf16[64,3712]{1,0:T(8,128)(2,1)S(1)} %pad_maximum_fusion.refs_0_), channel_id=1, source_target_pairs={{0,16},{1,17},{2,18},{3,19},{4,20},{5,21},{6,22},{7,23},{8,24},{9,... | collective-permute-start | bytes 1425416 | tf_op jit(solution)/shard_map/ppermute | solution.py:166
  32.4 10.2 %collective-permute-start.12 = (bf16[64,3712]{1,0:T(8,128)(2,1)S(1)}, bf16[64,3712]{1,0:T(8,128)(2,1)S(1)}, u32[]{:S(2)}, u32[]{:S(2)}) collective-permute-start(bf16[64,3712]{1,0:T(8,128)(2,1)S(1)} %collective-permute-done.6.refs_1_), channel_id=1, source_target_pairs={{0,16},{1,17},{2,18},{3,19},{4,20},{5,21},{6,22},{7,23},{8,24},{9,... | collective-permute-start | bytes 1425416 | tf_op jit(solution)/shard_map/ppermute | solution.py:166
  32.9 9.7 %collective-permute-start.13 = (bf16[64,3712]{1,0:T(8,128)(2,1)S(1)}, bf16[64,3712]{1,0:T(8,128)(2,1)S(1)}, u32[]{:S(2)}, u32[]{:S(2)}) collective-permute-start(bf16[64,3712]{1,0:T(8,128)(2,1)S(1)} %collective-permute-done.10.refs_2_), channel_id=1, source_target_pairs={{0,16},{1,17},{2,18},{3,19},{4,20},{5,21},{6,22},{7,23},{8,24},{9,... | collective-permute-start | bytes 1425416 | tf_op jit(solution)/shard_map/ppermute | solution.py:166
  40.0 13.5 %collective-permute-start.8 = (bf16[64,3712]{1,0:T(8,128)(2,1)S(1)}, bf16[64,3712]{1,0:T(8,128)(2,1)S(1)}, u32[]{:S(2)}, u32[]{:S(2)}) collective-permute-start(bf16[64,3712]{1,0:T(8,128)(2,1)S(1)} %pad_maximum_fusion.1.refs_0_), channel_id=1, source_target_pairs={{0,2},{1,3},{2,0},{3,1},{4,6},{5,7},{6,4},{7,5},{8,10},{9,11},{10,... | collective-permute-start | bytes 1425416 | tf_op jit(solution)/shard_map/ppermute | solution.py:166
  41.4 12.2 %collective-permute-start.9 = (bf16[64,3712]{1,0:T(8,128)(2,1)S(1)}, bf16[64,3712]{1,0:T(8,128)(2,1)S(1)}, u32[]{:S(2)}, u32[]{:S(2)}) collective-permute-start(bf16[64,3712]{1,0:T(8,128)(2,1)S(1)} %pad_maximum_fusion.1.refs_0_), channel_id=1, source_target_pairs={{0,1},{1,0},{2,3},{3,2},{4,5},{5,4},{6,7},{7,6},{8,9},{9,8},{10,11... | collective-permute-start | bytes 1425416 | tf_op jit(solution)/shard_map/ppermute | solution.py:166
  45.7 11.5 %collective-permute-start.19 = (bf16[64,3584]{1,0:T(8,128)(2,1)S(1)}, bf16[64,3584]{1,0:T(8,128)(2,1)S(1)}, u32[]{:S(2)}, u32[]{:S(2)}) collective-permute-start(bf16[64,3584]{1,0:T(8,128)(2,1)S(1)} %get-tuple-element.40), channel_id=1, source_target_pairs={{0,16},{1,17},{2,18},{3,19},{4,20},{5,21},{6,22},{7,23},{8,24},{9,... | collective-permute-start | bytes 1376264 | tf_op jit(solution)/shard_map/ppermute | solution.py:166
  46.5 13.1 %collective-permute-start.26 = (bf16[64,3712]{1,0:T(8,128)(2,1)S(1)}, bf16[64,3712]{1,0:T(8,128)(2,1)S(1)}, u32[]{:S(2)}, u32[]{:S(2)}) collective-permute-start(bf16[64,3712]{1,0:T(8,128)(2,1)S(1)} %pad_maximum_fusion.1.refs_0_), channel_id=1, source_target_pairs={{0,16},{1,17},{2,18},{3,19},{4,20},{5,21},{6,22},{7,23},{8,24},{9,... | collective-permute-start | bytes 1425416 | tf_op jit(solution)/shard_map/ppermute | solution.py:166
  54.0 25.1 %collective-permute-start.15 = (bf16[64,3584]{1,0:T(8,128)(2,1)S(1)}, bf16[64,3584]{1,0:T(8,128)(2,1)S(1)}, u32[]{:S(2)}, u32[]{:S(2)}) collective-permute-start(bf16[64,3584]{1,0:T(8,128)(2,1)S(1)} %get-tuple-element.34), channel_id=1, source_target_pairs={{0,16},{1,17},{2,18},{3,19},{4,20},{5,21},{6,22},{7,23},{8,24},{9,... | collective-permute-start | bytes 1376264 | tf_op jit(solution)/shard_map/ppermute | solution.py:166
  57.2 8.7 %collective-permute-start.25 = (bf16[64,3712]{1,0:T(8,128)(2,1)S(1)}, bf16[64,3712]{1,0:T(8,128)(2,1)S(1)}, u32[]{:S(2)}, u32[]{:S(2)}) collective-permute-start(bf16[64,3712]{1,0:T(8,128)(2,1)S(1)} %collective-permute-done.8.refs_1_), channel_id=1, source_target_pairs={{0,1},{1,0},{2,3},{3,2},{4,5},{5,4},{6,7},{7,6},{8,9},{9,8},{10,11... | collective-permute-start | bytes 1425416 | tf_op jit(solution)/shard_map/ppermute | solution.py:166
  58.5 12.4 %collective-permute-start.20 = (bf16[64,3584]{1,0:T(8,128)(2,1)S(1)}, bf16[64,3584]{1,0:T(8,128)(2,1)S(1)}, u32[]{:S(2)}, u32[]{:S(2)}) collective-permute-start(bf16[64,3584]{1,0:T(8,128)(2,1)S(1)} %add_convert_fusion.6), channel_id=1, source_target_pairs={{0,1},{1,0},{2,3},{3,2},{4,5},{5,4},{6,7},{7,6},{8,9},{9,8},{10,11... | collective-permute-start | bytes 1376264 | tf_op jit(solution)/shard_map/ppermute | solution.py:166
  59.6 11.4 %collective-permute-start.27 = (bf16[64,3712]{1,0:T(8,128)(2,1)S(1)}, bf16[64,3712]{1,0:T(8,128)(2,1)S(1)}, u32[]{:S(2)}, u32[]{:S(2)}) collective-permute-start(bf16[64,3712]{1,0:T(8,128)(2,1)S(1)} %collective-permute-done.8.refs_1_), channel_id=1, source_target_pairs={{0,16},{1,17},{2,18},{3,19},{4,20},{5,21},{6,22},{7,23},{8,24},{9,... | collective-permute-start | bytes 1425416 | tf_op jit(solution)/shard_map/ppermute | solution.py:166
  59.7 15.8 %collective-permute-start.28 = (bf16[64,3712]{1,0:T(8,128)(2,1)S(1)}, bf16[64,3712]{1,0:T(8,128)(2,1)S(1)}, u32[]{:S(2)}, u32[]{:S(2)}) collective-permute-start(bf16[64,3712]{1,0:T(8,128)(2,1)S(1)} %collective-permute-done.9.refs_2_), channel_id=1, source_target_pairs={{0,16},{1,17},{2,18},{3,19},{4,20},{5,21},{6,22},{7,23},{8,24},{9,... | collective-permute-start | bytes 1425416 | tf_op jit(solution)/shard_map/ppermute | solution.py:166
  65.9 13.3 %collective-permute-start.17 = (bf16[64,3584]{1,0:T(8,128)(2,1)S(1)}, bf16[64,3584]{1,0:T(8,128)(2,1)S(1)}, u32[]{:S(2)}, u32[]{:S(2)}) collective-permute-start(bf16[64,3584]{1,0:T(8,128)(2,1)S(1)} %add_convert_fusion.7), channel_id=1, source_target_pairs={{0,1},{1,0},{2,3},{3,2},{4,5},{5,4},{6,7},{7,6},{8,9},{9,8},{10,11... | collective-permute-start | bytes 1376264 | tf_op jit(solution)/shard_map/ppermute | solution.py:166
  71.0 9.1 %collective-permute-start.21 = (bf16[64,3584]{1,0:T(8,128)(2,1)S(1)}, bf16[64,3584]{1,0:T(8,128)(2,1)S(1)}, u32[]{:S(2)}, u32[]{:S(2)}) collective-permute-start(bf16[64,3584]{1,0:T(8,128)(2,1)S(1)} %add_convert_fusion.5), channel_id=1, source_target_pairs={{0,2},{1,3},{2,0},{3,1},{4,6},{5,7},{6,4},{7,5},{8,10},{9,11},{10,... | collective-permute-start | bytes 1376264 | tf_op jit(solution)/shard_map/ppermute | solution.py:166
  79.3 16.0 %collective-permute-start.30 = (bf16[64,3584]{1,0:T(8,128)(2,1)S(1)}, bf16[64,3584]{1,0:T(8,128)(2,1)S(1)}, u32[]{:S(2)}, u32[]{:S(2)}) collective-permute-start(bf16[64,3584]{1,0:T(8,128)(2,1)S(1)} %get-tuple-element.43), channel_id=1, source_target_pairs={{0,16},{1,17},{2,18},{3,19},{4,20},{5,21},{6,22},{7,23},{8,24},{9,... | collective-permute-start | bytes 1376264 | tf_op jit(solution)/shard_map/ppermute | solution.py:166
  81.3 8.5 %collective-permute-start.35 = (bf16[64,3584]{1,0:T(8,128)(2,1)S(1)}, bf16[64,3584]{1,0:T(8,128)(2,1)S(1)}, u32[]{:S(2)}, u32[]{:S(2)}) collective-permute-start(bf16[64,3584]{1,0:T(8,128)(2,1)S(1)} %add_convert_fusion.2), channel_id=1, source_target_pairs={{0,1},{1,0},{2,3},{3,2},{4,5},{5,4},{6,7},{7,6},{8,9},{9,8},{10,11... | collective-permute-start | bytes 1376264 | tf_op jit(solution)/shard_map/ppermute | solution.py:166
  82.9 14.6 %collective-permute-start.32 = (bf16[64,3584]{1,0:T(8,128)(2,1)S(1)}, bf16[64,3584]{1,0:T(8,128)(2,1)S(1)}, u32[]{:S(2)}, u32[]{:S(2)}) collective-permute-start(bf16[64,3584]{1,0:T(8,128)(2,1)S(1)} %add_convert_fusion.3), channel_id=1, source_target_pairs={{0,1},{1,0},{2,3},{3,2},{4,5},{5,4},{6,7},{7,6},{8,9},{9,8},{10,11... | collective-permute-start | bytes 1376264 | tf_op jit(solution)/shard_map/ppermute | solution.py:166
  90.0 8.8 %collective-permute-start.36 = (bf16[64,3584]{1,0:T(8,128)(2,1)S(1)}, bf16[64,3584]{1,0:T(8,128)(2,1)S(1)}, u32[]{:S(2)}, u32[]{:S(2)}) collective-permute-start(bf16[64,3584]{1,0:T(8,128)(2,1)S(1)} %add_convert_fusion.1), channel_id=1, source_target_pairs={{0,2},{1,3},{2,0},{3,1},{4,6},{5,7},{6,4},{7,5},{8,10},{9,11},{10,... | collective-permute-start | bytes 1376264 | tf_op jit(solution)/shard_map/ppermute | solution.py:166
  91.4 12.3 %collective-permute-start.22 = (bf16[16,3584]{1,0:T(8,128)(2,1)S(1)}, bf16[16,3584]{1,0:T(8,128)(2,1)S(1)}, u32[]{:S(2)}, u32[]{:S(2)}) collective-permute-start(bf16[16,3584]{1,0:T(8,128)(2,1)S(1)} %get-tuple-element.50), channel_id=1, source_target_pairs={{0,12},{1,13},{2,14},{3,15},{4,0},{5,1},{6,2},{7,3},{8,4},{9,5},{1... | collective-permute-start | bytes 344072 | tf_op jit(solution)/shard_map/ppermute | solution.py:166
  93.6 11.1 %collective-permute-start.23 = (bf16[16,3584]{1,0:T(8,128)(2,1)S(1)}, bf16[16,3584]{1,0:T(8,128)(2,1)S(1)}, u32[]{:S(2)}, u32[]{:S(2)}) collective-permute-start(bf16[16,3584]{1,0:T(8,128)(2,1)S(1)} %get-tuple-element.52), channel_id=1, source_target_pairs={{0,8},{1,9},{2,10},{3,11},{4,12},{5,13},{6,14},{7,15},{8,0},{9,1},... | collective-permute-start | bytes 344072 | tf_op jit(solution)/shard_map/ppermute | solution.py:166
  95.3 9.4 %collective-permute-start.24 = (bf16[16,3584]{1,0:T(8,128)(2,1)S(1)}, bf16[16,3584]{1,0:T(8,128)(2,1)S(1)}, u32[]{:S(2)}, u32[]{:S(2)}) collective-permute-start(bf16[16,3584]{1,0:T(8,128)(2,1)S(1)} %get-tuple-element.51), channel_id=1, source_target_pairs={{0,4},{1,5},{2,6},{3,7},{4,8},{5,9},{6,10},{7,11},{8,12},{9,13},{1... | collective-permute-start | bytes 344072 | tf_op jit(solution)/shard_map/ppermute | solution.py:166
  102.1 12.9 %collective-permute-start.38 = (bf16[16,3584]{1,0:T(8,128)(2,1)S(1)}, bf16[16,3584]{1,0:T(8,128)(2,1)S(1)}, u32[]{:S(2)}, u32[]{:S(2)}) collective-permute-start(bf16[16,3584]{1,0:T(8,128)(2,1)S(1)} %get-tuple-element.55), channel_id=1, source_target_pairs={{0,8},{1,9},{2,10},{3,11},{4,12},{5,13},{6,14},{7,15},{8,0},{9,1},... | collective-permute-start | bytes 344072 | tf_op jit(solution)/shard_map/ppermute | solution.py:166
  103.6 11.3 %collective-permute-start.39 = (bf16[16,3584]{1,0:T(8,128)(2,1)S(1)}, bf16[16,3584]{1,0:T(8,128)(2,1)S(1)}, u32[]{:S(2)}, u32[]{:S(2)}) collective-permute-start(bf16[16,3584]{1,0:T(8,128)(2,1)S(1)} %get-tuple-element.54), channel_id=1, source_target_pairs={{0,4},{1,5},{2,6},{3,7},{4,8},{5,9},{6,10},{7,11},{8,12},{9,13},{1... | collective-permute-start | bytes 344072 | tf_op jit(solution)/shard_map/ppermute | solution.py:166
  (15 other events, 121.7 us)

commit v3 on v2

--- a/solution.py
+++ b/solution.py
@@ -22,19 +22,18 @@
                     if kind == "role":
                         to_r = 1 - r
                     elif kind == "z":
-                        to_z = (z + step) % depth
+                        to_z = z ^ step
                     elif (kind == "first") == (r == 0):
-                        to_y = (y + step) % side
+                        to_y = y ^ step
                     else:
-                        to_x = (x + step) % side
+                        to_x = x ^ step
                     here = ((r * depth + z) * side + y) * side + x
                     there = ((to_r * depth + to_z) * side + to_y) * side + to_x
                     pairs.append((here, there))
     return pairs
 
 
-def attend_kernel(lengths_ref, lat_ref, rope_ref, cache_ref, keys_ref, *refs):
-    out_ref = refs[-1]
+def attend_kernel(lengths_ref, lat_ref, rope_ref, cache_ref, keys_ref, out_ref):
     length = lengths_ref[pl.program_id(0)]
     cache = cache_ref[0]
     scores = lax.dot_general(
@@ -52,7 +51,7 @@
     ).astype(jnp.bfloat16)
 
 
-def attend_rows(q_latent, q_rope, latent_cache, rope_cache, lengths, start, count, resident=()):
+def attend_rows(q_latent, q_rope, latent_cache, rope_cache, lengths, start, count):
     heads, latent = q_latent.shape[1:]
     cached = latent_cache.shape[1]
     rope = rope_cache.shape[1]
@@ -71,18 +70,17 @@
                 spec(heads, rope),
                 spec(cached, latent),
                 spec(rope, cached),
-            ]
-            + [pl.BlockSpec(memory_space=pltpu.VMEM)] * len(resident),
+            ],
             out_specs=pl.BlockSpec((1, heads, latent), lambda at, lengths_ref: (at, 0, 0)),
         ),
-        compiler_params=pltpu.CompilerParams(vmem_limit_bytes=(46 if resident else 48) * 1024 * 1024),
+        compiler_params=pltpu.CompilerParams(vmem_limit_bytes=48 * 1024 * 1024),
         cost_estimate=pl.CostEstimate(
             flops=2 * count * heads * cached * (2 * latent + rope),
             bytes_accessed=2 * count * cached * (latent + rope),
             transcendentals=count * heads * cached,
         ),
         name="attend_rows",
-    )(lengths[start : start + count], q_latent, q_rope, latent_cache, rope_cache, *resident)
+    )(lengths[start : start + count], q_latent, q_rope, latent_cache, rope_cache)
 
 
 def expert_kernel(count, lane_ref, *refs):
@@ -185,10 +183,8 @@
 
     matrices = (w_gate[0], w_up[0], w_down[0])
 
-    def attend(start, key, resident=()):
-        return attend_rows(
-            q_latent, key, latent_cache, rope_cache, lengths, start, att_half, resident
-        )
+    def attend(start, count, key):
+        return attend_rows(q_latent, key, latent_cache, rope_cache, lengths, start, count)
 
     def pieces(c):
         return payload[c * chunk : (c + 1) * chunk]
@@ -196,20 +192,18 @@
     def along(mine):
         return [mine] + [send(mine, "z", k) for k in range(1, depth)]
 
-    early = attend(0, rope_rows)
+    early = attend(0, att_half, rope_rows)
     gathered = []
     coming = along(pieces(0))
     coming[1] = after(coming[1], early)
     last = None
     for c in range(chunk_count):
         line = jnp.concatenate(coming, axis=0)
-        if last is not None:
-            line = after(line, last)
         if c + 1 < chunk_count:
             coming = along(after(pieces(c + 1), line))
         first = [line] + [send(line, "first", k) for k in range(1, side)]
         if c == 0:
-            late = attend(att_half, after(rope_rows, line))
+            late = attend(att_half, att_half, after(rope_rows, line))
             first[1] = after(first[1], late, *coming)
         blocks = list(first)
         for k in range(1, side):
@@ -223,7 +217,7 @@
         half = len(gathered[c]) // 2
         own, other = gathered[c][:half], gathered[c][half:]
         if summed is not None:
-            other = [after(other[0], summed)] + other[1:]
+            other = [after(other[0], *summed)] + other[1:]
 
         def expert(blocks):
             results = []
@@ -231,28 +225,31 @@
                 results += expert_blocks(blocks[at : at + 4], *matrices, own_lane)
             return results
 
-        theirs = [send(part, "role") for part in expert(other)]
+        other_results = expert(other)
+        theirs = [send(part, "role") for part in other_results]
+        if summed is not None:
+            own = [after(own[0], other_results[-1])] + own[1:]
         if c + 1 < chunk_count:
             following = gathered[c + 1]
-            own = [after(own[0], following[1], following[side])] + own[1:]
+            own = [after(own[0], following[1], following[side], *theirs)] + own[1:]
         mine = expert(own)
         whole = [a.astype(jnp.float32) + b.astype(jnp.float32) for a, b in zip(mine, theirs)]
         whole = [whole[k * side : (k + 1) * side] for k in range(side)]
         sent = [[part.astype(jnp.bfloat16) for part in row] for row in whole]
-        summed = sent[side - 1][side - 1]
+        summed = sum(sent, [])
         kept = {}
         for a in reversed(range(side)):
             total = whole[0][a]
             for k in range(1, side):
-                total = total + send(sent[k][a], "last", -k).astype(jnp.float32)
+                total = total + send(sent[k][a], "last", k).astype(jnp.float32)
             kept[a] = total
         total = kept[0]
         for k in range(1, side):
-            total = total + send(kept[k].astype(jnp.bfloat16), "first", -k).astype(jnp.float32)
+            total = total + send(kept[k].astype(jnp.bfloat16), "first", k).astype(jnp.float32)
         line = total.astype(jnp.bfloat16).reshape(depth, chunk, width)
         total = line[0].astype(jnp.float32)
         for k in range(1, depth):
-            total = total + send(line[k], "z", -k).astype(jnp.float32)
+            total = total + send(line[k], "z", k).astype(jnp.float32)
         finished.append(total.astype(jnp.bfloat16))
     moe_out = jnp.concatenate(finished, axis=0)
     attended = jnp.concatenate([early, late], axis=0)

time: 116 us -> 111 us (0.957)
  waiting for transfers between devices: 45.2 us -> 40.2 us
    ppermute x40, waiting for transfers between devices: 45.2 us -> 40.2 us  [send(): return lax.ppermute(value, both_axes, shift_pairs(kind, step, depth, side))]
  transfers between devices with their start and end apart: 40 -> 40, of which waited for: 12 -> 10; matrix products, arithmetic and copies ran while one was open for 3% -> 3% of each run, Pallas kernels for 20% -> 21%
where the time goes in v3:
time: 111 us; the launch traced here: 110 us
  waiting for transfers between devices  40.2 us (36%)
  starting transfers between devices  37.6 us (34%)
  Pallas kernels  23 us (21%)
  local copies, waits for them, and re-layouts  5.17 us (5%)
  other arithmetic  3.54 us (3%)
    ppermute x40, waiting for transfers between devices, send(): return lax.ppermute(value, both_axes, shift_pairs(kind, step, depth, side))  40.2 us
    ppermute x40, starting transfers between devices, send(): return lax.ppermute(value, both_axes, shift_pairs(kind, step, depth, side))  37.6 us
    pallas_call x4, Pallas kernels, expert_blocks(): pl.pallas_call(functools.partial(expert_kernel, count), out_shape=[jax.Sh...  12.2 us
    pallas_call x2, Pallas kernels, attend_rows(): pl.pallas_call(attend_kernel, out_shape=jax.ShapeDtypeStruct((count, head...  10.7 us
    unnamed x17, local copies, waits for them, and re-layouts  2.23 us
  transfers between devices with their start and end apart: 40, of which 10 were waited for; matrix products, arithmetic and copies ran while one was open for 3% of the time, Pallas kernels for 21%

profile of v3, /device:TPU:0, one launch (start us, length us, event | category | flops | bytes accessed | tf_op | source)
XLA Modules:
  0.0 110.5 jit_solution(15097023963635388759)
XLA Ops:
  1.5 1.0 concatenate.15
  2.6 3.1 %collective-permute-start = (bf16[16,3712]{1,0:T(8,128)(2,1)S(1)}, bf16[16,3712]{1,0:T(8,128)(2,1)S(1)}, u32[]{:S(2)}, u32[]{:S(2)}) collective-permute-start(bf16[16,3712]{1,0:T(8,128)(2,1)S(1)} %get-tuple-element.56), channel_id=1, source_target_pairs={{0,4},{1,5},{2,6},{3,7},{4,0},{5,1},{6,2},{7,3},{8,12},{9,13},{10,... | collective-permute-start | bytes 356360 | tf_op jit(solution)/shard_map/ppermute | solution.py:164
  5.7 2.6 %collective-permute-start.1 = (bf16[16,3712]{1,0:T(8,128)(2,1)S(1)}, bf16[16,3712]{1,0:T(8,128)(2,1)S(1)}, u32[]{:S(2)}, u32[]{:S(2)}) collective-permute-start(bf16[16,3712]{1,0:T(8,128)(2,1)S(1)} %get-tuple-element.56), channel_id=1, source_target_pairs={{0,8},{1,9},{2,10},{3,11},{4,12},{5,13},{6,14},{7,15},{8,0},{9,1},... | collective-permute-start | bytes 356360 | tf_op jit(solution)/shard_map/ppermute | solution.py:164
  10.0 1.2 %copy-done.3 = bf16[4,64,2048]{2,1,0:T(8,128)(2,1)S(1)} copy-done((bf16[4,64,2048]{2,1,0:T(8,128)(2,1)S(1)}, bf16[4,64,2048]{2,1,0:T(8,128)(2,1)}, u32[]{:S(2)}) %copy-start.3) | copy-done | bytes 1048600
  12.1 5.1 %attend_rows.2 = bf16[2,64,512]{2,1,0:T(8,128)(2,1)S(1)} custom-call(s32[2]{0:T(128)S(1)} %get-tuple-element.61.lengths_ref, bf16[4,64,512]{2,1,0:T(8,128)(2,1)S(1)} %copy-done.5, bf16[4,64,64]{2,1,0:T(8,128)(2,1)S(1)} %reshape.46.rope_ref, bf16[4,2048,512]{2,1,0:T(8,128)(2,1)} %cache_ref.3, bf16[4,64,2048]{2,1,0:T(8,128)(2,1)S(1)} %copy-done.3), custom_call_target="tpu_custom_call" | custom-call | flops 570425344 | bytes 4718592 | tf_op jit(solution)/shard_map/attend_rows/pallas_call | solution.py:62
  17.7 1.9 %collective-permute-start.3 = (bf16[16,3712]{1,0:T(8,128)(2,1)S(1)}, bf16[16,3712]{1,0:T(8,128)(2,1)S(1)}, u32[]{:S(2)}, u32[]{:S(2)}) collective-permute-start(bf16[16,3712]{1,0:T(8,128)(2,1)S(1)} %get-tuple-element.28), channel_id=1, source_target_pairs={{0,4},{1,5},{2,6},{3,7},{4,0},{5,1},{6,2},{7,3},{8,12},{9,13},{10,... | collective-permute-start | bytes 356360 | tf_op jit(solution)/shard_map/ppermute | solution.py:164
  19.6 2.2 %collective-permute-start.4 = (bf16[16,3712]{1,0:T(8,128)(2,1)S(1)}, bf16[16,3712]{1,0:T(8,128)(2,1)S(1)}, u32[]{:S(2)}, u32[]{:S(2)}) collective-permute-start(bf16[16,3712]{1,0:T(8,128)(2,1)S(1)} %get-tuple-element.28), channel_id=1, source_target_pairs={{0,8},{1,9},{2,10},{3,11},{4,12},{5,13},{6,14},{7,15},{8,0},{9,1},... | collective-permute-start | bytes 356360 | tf_op jit(solution)/shard_map/ppermute | solution.py:164
  22.2 1.5 %collective-permute-start.9 = (bf16[64,3712]{1,0:T(8,128)(2,1)S(1)}, bf16[64,3712]{1,0:T(8,128)(2,1)S(1)}, u32[]{:S(2)}, u32[]{:S(2)}) collective-permute-start(bf16[64,3712]{1,0:T(8,128)(2,1)S(1)} %pad_maximum_fusion.refs_0_), channel_id=1, source_target_pairs={{0,2},{1,3},{2,0},{3,1},{4,6},{5,7},{6,4},{7,5},{8,10},{9,11},{10,... | collective-permute-start | bytes 1425416 | tf_op jit(solution)/shard_map/ppermute | solution.py:164
  23.7 1.5 %collective-permute-start.11 = (bf16[64,3712]{1,0:T(8,128)(2,1)S(1)}, bf16[64,3712]{1,0:T(8,128)(2,1)S(1)}, u32[]{:S(2)}, u32[]{:S(2)}) collective-permute-start(bf16[64,3712]{1,0:T(8,128)(2,1)S(1)} %pad_maximum_fusion.refs_0_), channel_id=1, source_target_pairs={{0,1},{1,0},{2,3},{3,2},{4,5},{5,4},{6,7},{7,6},{8,9},{9,8},{10,11... | collective-permute-start | bytes 1425416 | tf_op jit(solution)/shard_map/ppermute | solution.py:164
  25.3 5.6 %attend_rows.3 = bf16[2,64,512]{2,1,0:T(8,128)(2,1)S(1)} custom-call(s32[2]{0:T(128)S(1)} %get-tuple-element.60.lengths_ref, bf16[4,64,512]{2,1,0:T(8,128)(2,1)S(1)} %copy-done.6, bf16[4,64,64]{2,1,0:T(8,128)(2,1)S(1)} %reshape.46.rope_ref, bf16[4,2048,512]{2,1,0:T(8,128)(2,1)} %cache_ref.3, bf16[4,64,2048]{2,1,0:T(8,128)(2,1)S(1)} %copy-done.4), custom_call_target="tpu_custom_call" | custom-call | flops 570425344 | bytes 4718592 | tf_op jit(solution)/shard_map/attend_rows/pallas_call | solution.py:62
  31.0 3.7 %collective-permute-done.9.refs_1_ = bf16[64,3712]{1,0:T(8,128)(2,1)S(1)} collective-permute-done((bf16[64,3712]{1,0:T(8,128)(2,1)S(1)}, bf16[64,3712]{1,0:T(8,128)(2,1)S(1)}, u32[]{:S(2)}, u32[]{:S(2)}) %collective-permute-start.9) | collective-permute-done | bytes 475168 | tf_op jit(solution)/shard_map/ppermute | solution.py:164
  35.2 2.2 %collective-permute-start.6 = (bf16[64,3712]{1,0:T(8,128)(2,1)S(1)}, bf16[64,3712]{1,0:T(8,128)(2,1)S(1)}, u32[]{:S(2)}, u32[]{:S(2)}) collective-permute-start(bf16[64,3712]{1,0:T(8,128)(2,1)S(1)} %constant_dynamic-update-slice_fusion.refs_0_), channel_id=1, source_target_pairs={{0,2},{1,3},{2,0},{3,1},{4,6},{5,7},{6,4},{7,5},{8,10},{9,11},{10,... | collective-permute-start | bytes 1425416 | tf_op jit(solution)/shard_map/ppermute | solution.py:164
  37.9 6.8 %collective-permute-done.13.refs_3_ = bf16[64,3712]{1,0:T(8,128)(2,1)S(1)} collective-permute-done((bf16[64,3712]{1,0:T(8,128)(2,1)S(1)}, bf16[64,3712]{1,0:T(8,128)(2,1)S(1)}, u32[]{:S(2)}, u32[]{:S(2)}) %collective-permute-start.13) | collective-permute-done | bytes 475168 | tf_op jit(solution)/shard_map/ppermute | solution.py:164
  45.6 1.1 collective-permute-start.28
  46.7 3.0 %expert_blocks.4 = (bf16[64,3584]{1,0:T(8,128)(2,1)S(1)}, bf16[64,3584]{1,0:T(8,128)(2,1)S(1)}, bf16[64,3584]{1,0:T(8,128)(2,1)S(1)}, bf16[64,3584]{1,0:T(8,128)(2,1)S(1)}) custom-call(f32[1,128]{1,0:T(1,128)S(1)} %or_convert_fusion.lane_ref, bf16[64,3712]{1,0:T(8,128)(2,1)S(1)} %collective-permute-done.8.refs_0_, ...), custom_call_target="tpu_custom_call" | custom-call | flops 2818572288 | bytes 14680064 | tf_op jit(solution)/shard_map/expert_blocks/pallas_call | solution.py:121
  50.4 2.9 %collective-permute-done.7.refs_2_ = bf16[64,3712]{1,0:T(8,128)(2,1)S(1)} collective-permute-done((bf16[64,3712]{1,0:T(8,128)(2,1)S(1)}, bf16[64,3712]{1,0:T(8,128)(2,1)S(1)}, u32[]{:S(2)}, u32[]{:S(2)}) %collective-permute-start.7) | collective-permute-done | bytes 475168 | tf_op jit(solution)/shard_map/ppermute | solution.py:164
  54.0 4.4 %collective-permute-done.28.refs_3_ = bf16[64,3712]{1,0:T(8,128)(2,1)S(1)} collective-permute-done((bf16[64,3712]{1,0:T(8,128)(2,1)S(1)}, bf16[64,3712]{1,0:T(8,128)(2,1)S(1)}, u32[]{:S(2)}, u32[]{:S(2)}) %collective-permute-start.28) | collective-permute-done | bytes 475168 | tf_op jit(solution)/shard_map/ppermute | solution.py:164
  59.4 3.0 %expert_blocks.5 = (bf16[64,3584]{1,0:T(8,128)(2,1)S(1)}, bf16[64,3584]{1,0:T(8,128)(2,1)S(1)}, bf16[64,3584]{1,0:T(8,128)(2,1)S(1)}, bf16[64,3584]{1,0:T(8,128)(2,1)S(1)}) custom-call(f32[1,128]{1,0:T(1,128)S(1)} %or_convert_fusion.lane_ref, bf16[64,3712]{1,0:T(8,128)(2,1)S(1)} %pad_maximum_fusion.refs_0_, ...), custom_call_target="tpu_custom_call" | custom-call | flops 2818572288 | bytes 14680064 | tf_op jit(solution)/shard_map/expert_blocks/pallas_call | solution.py:121
  62.6 1.0 collective-permute-start.20
  63.8 1.1 %collective-permute-start.19 = (bf16[64,3584]{1,0:T(8,128)(2,1)S(1)}, bf16[64,3584]{1,0:T(8,128)(2,1)S(1)}, u32[]{:S(2)}, u32[]{:S(2)}) collective-permute-start(bf16[64,3584]{1,0:T(8,128)(2,1)S(1)} %add_convert_fusion.7), channel_id=1, source_target_pairs={{0,1},{1,0},{2,3},{3,2},{4,5},{5,4},{6,7},{7,6},{8,9},{9,8},{10,11... | collective-permute-start | bytes 1376264 | tf_op jit(solution)/shard_map/ppermute | solution.py:164
  64.9 3.1 %expert_blocks.6 = (bf16[64,3584]{1,0:T(8,128)(2,1)S(1)}, bf16[64,3584]{1,0:T(8,128)(2,1)S(1)}, bf16[64,3584]{1,0:T(8,128)(2,1)S(1)}, bf16[64,3584]{1,0:T(8,128)(2,1)S(1)}) custom-call(f32[1,128]{1,0:T(1,128)S(1)} %or_convert_fusion.lane_ref, bf16[64,3712]{1,0:T(8,128)(2,1)S(1)} %collective-permute-done.25.refs_0_, ...), custom_call_target="tpu_custom_call" | custom-call | flops 2818572288 | bytes 14680064 | tf_op jit(solution)/shard_map/expert_blocks/pallas_call | solution.py:121
  68.7 3.1 %expert_blocks.7 = (bf16[64,3584]{1,0:T(8,128)(2,1)S(1)}, bf16[64,3584]{1,0:T(8,128)(2,1)S(1)}, bf16[64,3584]{1,0:T(8,128)(2,1)S(1)}, bf16[64,3584]{1,0:T(8,128)(2,1)S(1)}) custom-call(f32[1,128]{1,0:T(1,128)S(1)} %or_convert_fusion.lane_ref, bf16[64,3712]{1,0:T(8,128)(2,1)S(1)} %constant_dynamic-update-slice_fusion.refs_0_, ...), custom_call_target="tpu_custom_call" | custom-call | flops 2818572288 | bytes 14680064 | tf_op jit(solution)/shard_map/expert_blocks/pallas_call | solution.py:121
  72.4 1.6 %collective-permute-start.21 = (bf16[64,3584]{1,0:T(8,128)(2,1)S(1)}, bf16[64,3584]{1,0:T(8,128)(2,1)S(1)}, u32[]{:S(2)}, u32[]{:S(2)}) collective-permute-start(bf16[64,3584]{1,0:T(8,128)(2,1)S(1)} %add_convert_fusion.5), channel_id=1, source_target_pairs={{0,2},{1,3},{2,0},{3,1},{4,6},{5,7},{6,4},{7,5},{8,10},{9,11},{10,... | collective-permute-start | bytes 1376264 | tf_op jit(solution)/shard_map/ppermute | solution.py:164
  74.8 1.6 %collective-permute-start.32 = (bf16[64,3584]{1,0:T(8,128)(2,1)S(1)}, bf16[64,3584]{1,0:T(8,128)(2,1)S(1)}, u32[]{:S(2)}, u32[]{:S(2)}) collective-permute-start(bf16[64,3584]{1,0:T(8,128)(2,1)S(1)} %add_convert_fusion.3), channel_id=1, source_target_pairs={{0,1},{1,0},{2,3},{3,2},{4,5},{5,4},{6,7},{7,6},{8,9},{9,8},{10,11... | collective-permute-start | bytes 1376264 | tf_op jit(solution)/shard_map/ppermute | solution.py:164
  76.4 9.5 %collective-permute-done.35 = bf16[64,3584]{1,0:T(8,128)(2,1)S(1)} collective-permute-done((bf16[64,3584]{1,0:T(8,128)(2,1)S(1)}, bf16[64,3584]{1,0:T(8,128)(2,1)S(1)}, u32[]{:S(2)}, u32[]{:S(2)}) %collective-permute-start.35) | collective-permute-done | bytes 458784 | tf_op jit(solution)/shard_map/ppermute | solution.py:164
  86.1 1.6 %collective-permute-start.36 = (bf16[64,3584]{1,0:T(8,128)(2,1)S(1)}, bf16[64,3584]{1,0:T(8,128)(2,1)S(1)}, u32[]{:S(2)}, u32[]{:S(2)}) collective-permute-start(bf16[64,3584]{1,0:T(8,128)(2,1)S(1)} %add_convert_fusion.1), channel_id=1, source_target_pairs={{0,2},{1,3},{2,0},{3,1},{4,6},{5,7},{6,4},{7,5},{8,10},{9,11},{10,... | collective-permute-start | bytes 1376264 | tf_op jit(solution)/shard_map/ppermute | solution.py:164
  88.9 3.1 %collective-permute-start.23 = (bf16[16,3584]{1,0:T(8,128)(2,1)S(1)}, bf16[16,3584]{1,0:T(8,128)(2,1)S(1)}, u32[]{:S(2)}, u32[]{:S(2)}) collective-permute-start(bf16[16,3584]{1,0:T(8,128)(2,1)S(1)} %get-tuple-element.52), channel_id=1, source_target_pairs={{0,8},{1,9},{2,10},{3,11},{4,12},{5,13},{6,14},{7,15},{8,0},{9,1},... | collective-permute-start | bytes 344072 | tf_op jit(solution)/shard_map/ppermute | solution.py:164
  92.8 2.9 %collective-permute-done.36 = bf16[64,3584]{1,0:T(8,128)(2,1)S(1)} collective-permute-done((bf16[64,3584]{1,0:T(8,128)(2,1)S(1)}, bf16[64,3584]{1,0:T(8,128)(2,1)S(1)}, u32[]{:S(2)}, u32[]{:S(2)}) %collective-permute-start.36) | collective-permute-done | bytes 458784 | tf_op jit(solution)/shard_map/ppermute | solution.py:164
  95.9 1.0 collective-permute-start.37
  96.9 2.9 %collective-permute-start.38 = (bf16[16,3584]{1,0:T(8,128)(2,1)S(1)}, bf16[16,3584]{1,0:T(8,128)(2,1)S(1)}, u32[]{:S(2)}, u32[]{:S(2)}) collective-permute-start(bf16[16,3584]{1,0:T(8,128)(2,1)S(1)} %get-tuple-element.55), channel_id=1, source_target_pairs={{0,8},{1,9},{2,10},{3,11},{4,12},{5,13},{6,14},{7,15},{8,0},{9,1},... | collective-permute-start | bytes 344072 | tf_op jit(solution)/shard_map/ppermute | solution.py:164
  100.5 2.6 %collective-permute-done.37 = bf16[16,3584]{1,0:T(8,128)(2,1)S(1)} collective-permute-done((bf16[16,3584]{1,0:T(8,128)(2,1)S(1)}, bf16[16,3584]{1,0:T(8,128)(2,1)S(1)}, u32[]{:S(2)}, u32[]{:S(2)}) %collective-permute-start.37) | collective-permute-done | bytes 114720 | tf_op jit(solution)/shard_map/ppermute | solution.py:164
  103.1 6.7 %collective-permute-done.38 = bf16[16,3584]{1,0:T(8,128)(2,1)S(1)} collective-permute-done((bf16[16,3584]{1,0:T(8,128)(2,1)S(1)}, bf16[16,3584]{1,0:T(8,128)(2,1)S(1)}, u32[]{:S(2)}, u32[]{:S(2)}) %collective-permute-start.38) | collective-permute-done | bytes 114720 | tf_op jit(solution)/shard_map/ppermute | solution.py:164
  (98 shorter events, 15.1 us)
Async XLA Ops:
  2.6 14.7 %collective-permute-start = (bf16[16,3712]{1,0:T(8,128)(2,1)S(1)}, bf16[16,3712]{1,0:T(8,128)(2,1)S(1)}, u32[]{:S(2)}, u32[]{:S(2)}) collective-permute-start(bf16[16,3712]{1,0:T(8,128)(2,1)S(1)} %get-tuple-element.56), channel_id=1, source_target_pairs={{0,4},{1,5},{2,6},{3,7},{4,0},{5,1},{6,2},{7,3},{8,12},{9,13},{10,... | collective-permute-start | bytes 356360 | tf_op jit(solution)/shard_map/ppermute | solution.py:164
  5.7 12.0 %collective-permute-start.1 = (bf16[16,3712]{1,0:T(8,128)(2,1)S(1)}, bf16[16,3712]{1,0:T(8,128)(2,1)S(1)}, u32[]{:S(2)}, u32[]{:S(2)}) collective-permute-start(bf16[16,3712]{1,0:T(8,128)(2,1)S(1)} %get-tuple-element.56), channel_id=1, source_target_pairs={{0,8},{1,9},{2,10},{3,11},{4,12},{5,13},{6,14},{7,15},{8,0},{9,1},... | collective-permute-start | bytes 356360 | tf_op jit(solution)/shard_map/ppermute | solution.py:164
  8.3 9.4 %collective-permute-start.2 = (bf16[16,3712]{1,0:T(8,128)(2,1)S(1)}, bf16[16,3712]{1,0:T(8,128)(2,1)S(1)}, u32[]{:S(2)}, u32[]{:S(2)}) collective-permute-start(bf16[16,3712]{1,0:T(8,128)(2,1)S(1)} %get-tuple-element.56), channel_id=1, source_target_pairs={{0,12},{1,13},{2,14},{3,15},{4,8},{5,9},{6,10},{7,11},{8,4},{9,5},... | collective-permute-start | bytes 356360 | tf_op jit(solution)/shard_map/ppermute | solution.py:164
  17.7 13.1 %collective-permute-start.3 = (bf16[16,3712]{1,0:T(8,128)(2,1)S(1)}, bf16[16,3712]{1,0:T(8,128)(2,1)S(1)}, u32[]{:S(2)}, u32[]{:S(2)}) collective-permute-start(bf16[16,3712]{1,0:T(8,128)(2,1)S(1)} %get-tuple-element.28), channel_id=1, source_target_pairs={{0,4},{1,5},{2,6},{3,7},{4,0},{5,1},{6,2},{7,3},{8,12},{9,13},{10,... | collective-permute-start | bytes 356360 | tf_op jit(solution)/shard_map/ppermute | solution.py:164
  19.6 11.3 %collective-permute-start.4 = (bf16[16,3712]{1,0:T(8,128)(2,1)S(1)}, bf16[16,3712]{1,0:T(8,128)(2,1)S(1)}, u32[]{:S(2)}, u32[]{:S(2)}) collective-permute-start(bf16[16,3712]{1,0:T(8,128)(2,1)S(1)} %get-tuple-element.28), channel_id=1, source_target_pairs={{0,8},{1,9},{2,10},{3,11},{4,12},{5,13},{6,14},{7,15},{8,0},{9,1},... | collective-permute-start | bytes 356360 | tf_op jit(solution)/shard_map/ppermute | solution.py:164
  21.8 9.2 %collective-permute-start.5 = (bf16[16,3712]{1,0:T(8,128)(2,1)S(1)}, bf16[16,3712]{1,0:T(8,128)(2,1)S(1)}, u32[]{:S(2)}, u32[]{:S(2)}) collective-permute-start(bf16[16,3712]{1,0:T(8,128)(2,1)S(1)} %get-tuple-element.28), channel_id=1, source_target_pairs={{0,12},{1,13},{2,14},{3,15},{4,8},{5,9},{6,10},{7,11},{8,4},{9,5},... | collective-permute-start | bytes 356360 | tf_op jit(solution)/shard_map/ppermute | solution.py:164
  22.2 12.5 %collective-permute-start.9 = (bf16[64,3712]{1,0:T(8,128)(2,1)S(1)}, bf16[64,3712]{1,0:T(8,128)(2,1)S(1)}, u32[]{:S(2)}, u32[]{:S(2)}) collective-permute-start(bf16[64,3712]{1,0:T(8,128)(2,1)S(1)} %pad_maximum_fusion.refs_0_), channel_id=1, source_target_pairs={{0,2},{1,3},{2,0},{3,1},{4,6},{5,7},{6,4},{7,5},{8,10},{9,11},{10,... | collective-permute-start | bytes 1425416 | tf_op jit(solution)/shard_map/ppermute | solution.py:164
  23.7 13.7 %collective-permute-start.11 = (bf16[64,3712]{1,0:T(8,128)(2,1)S(1)}, bf16[64,3712]{1,0:T(8,128)(2,1)S(1)}, u32[]{:S(2)}, u32[]{:S(2)}) collective-permute-start(bf16[64,3712]{1,0:T(8,128)(2,1)S(1)} %pad_maximum_fusion.refs_0_), channel_id=1, source_target_pairs={{0,1},{1,0},{2,3},{3,2},{4,5},{5,4},{6,7},{7,6},{8,9},{9,8},{10,11... | collective-permute-start | bytes 1425416 | tf_op jit(solution)/shard_map/ppermute | solution.py:164
  30.9 13.8 %collective-permute-start.8 = (bf16[64,3712]{1,0:T(8,128)(2,1)S(1)}, bf16[64,3712]{1,0:T(8,128)(2,1)S(1)}, u32[]{:S(2)}, u32[]{:S(2)}) collective-permute-start(bf16[64,3712]{1,0:T(8,128)(2,1)S(1)} %pad_maximum_fusion.refs_0_), channel_id=1, source_target_pairs={{0,16},{1,17},{2,18},{3,19},{4,20},{5,21},{6,22},{7,23},{8,24},{9,... | collective-permute-start | bytes 1425416 | tf_op jit(solution)/shard_map/ppermute | solution.py:164
  34.7 10.0 %collective-permute-start.13 = (bf16[64,3712]{1,0:T(8,128)(2,1)S(1)}, bf16[64,3712]{1,0:T(8,128)(2,1)S(1)}, u32[]{:S(2)}, u32[]{:S(2)}) collective-permute-start(bf16[64,3712]{1,0:T(8,128)(2,1)S(1)} %collective-permute-done.9.refs_1_), channel_id=1, source_target_pairs={{0,1},{1,0},{2,3},{3,2},{4,5},{5,4},{6,7},{7,6},{8,9},{9,8},{10,11... | collective-permute-start | bytes 1425416 | tf_op jit(solution)/shard_map/ppermute | solution.py:164
  35.2 10.4 %collective-permute-start.6 = (bf16[64,3712]{1,0:T(8,128)(2,1)S(1)}, bf16[64,3712]{1,0:T(8,128)(2,1)S(1)}, u32[]{:S(2)}, u32[]{:S(2)}) collective-permute-start(bf16[64,3712]{1,0:T(8,128)(2,1)S(1)} %constant_dynamic-update-slice_fusion.refs_0_), channel_id=1, source_target_pairs={{0,2},{1,3},{2,0},{3,1},{4,6},{5,7},{6,4},{7,5},{8,10},{9,11},{10,... | collective-permute-start | bytes 1425416 | tf_op jit(solution)/shard_map/ppermute | solution.py:164
  37.4 9.3 %collective-permute-start.10 = (bf16[64,3712]{1,0:T(8,128)(2,1)S(1)}, bf16[64,3712]{1,0:T(8,128)(2,1)S(1)}, u32[]{:S(2)}, u32[]{:S(2)}) collective-permute-start(bf16[64,3712]{1,0:T(8,128)(2,1)S(1)} %collective-permute-done.9.refs_1_), channel_id=1, source_target_pairs={{0,16},{1,17},{2,18},{3,19},{4,20},{5,21},{6,22},{7,23},{8,24},{9,... | collective-permute-start | bytes 1425416 | tf_op jit(solution)/shard_map/ppermute | solution.py:164
  37.4 9.3 %collective-permute-start.12 = (bf16[64,3712]{1,0:T(8,128)(2,1)S(1)}, bf16[64,3712]{1,0:T(8,128)(2,1)S(1)}, u32[]{:S(2)}, u32[]{:S(2)}) collective-permute-start(bf16[64,3712]{1,0:T(8,128)(2,1)S(1)} %collective-permute-done.11.refs_2_), channel_id=1, source_target_pairs={{0,16},{1,17},{2,18},{3,19},{4,20},{5,21},{6,22},{7,23},{8,24},{9,... | collective-permute-start | bytes 1425416 | tf_op jit(solution)/shard_map/ppermute | solution.py:164
  44.7 8.7 %collective-permute-start.7 = (bf16[64,3712]{1,0:T(8,128)(2,1)S(1)}, bf16[64,3712]{1,0:T(8,128)(2,1)S(1)}, u32[]{:S(2)}, u32[]{:S(2)}) collective-permute-start(bf16[64,3712]{1,0:T(8,128)(2,1)S(1)} %constant_dynamic-update-slice_fusion.refs_0_), channel_id=1, source_target_pairs={{0,1},{1,0},{2,3},{3,2},{4,5},{5,4},{6,7},{7,6},{8,9},{9,8},{10,11... | collective-permute-start | bytes 1425416 | tf_op jit(solution)/shard_map/ppermute | solution.py:164
  45.6 12.8 %collective-permute-start.28 = (bf16[64,3712]{1,0:T(8,128)(2,1)S(1)}, bf16[64,3712]{1,0:T(8,128)(2,1)S(1)}, u32[]{:S(2)}, u32[]{:S(2)}) collective-permute-start(bf16[64,3712]{1,0:T(8,128)(2,1)S(1)} %collective-permute-done.6.refs_1_), channel_id=1, source_target_pairs={{0,1},{1,0},{2,3},{3,2},{4,5},{5,4},{6,7},{7,6},{8,9},{9,8},{10,11... | collective-permute-start | bytes 1425416 | tf_op jit(solution)/shard_map/ppermute | solution.py:164
  49.8 8.6 %collective-permute-start.15 = (bf16[64,3584]{1,0:T(8,128)(2,1)S(1)}, bf16[64,3584]{1,0:T(8,128)(2,1)S(1)}, u32[]{:S(2)}, u32[]{:S(2)}) collective-permute-start(bf16[64,3584]{1,0:T(8,128)(2,1)S(1)} %get-tuple-element.31), channel_id=1, source_target_pairs={{0,16},{1,17},{2,18},{3,19},{4,20},{5,21},{6,22},{7,23},{8,24},{9,... | collective-permute-start | bytes 1376264 | tf_op jit(solution)/shard_map/ppermute | solution.py:164
  49.9 9.1 %collective-permute-start.16 = (bf16[64,3584]{1,0:T(8,128)(2,1)S(1)}, bf16[64,3584]{1,0:T(8,128)(2,1)S(1)}, u32[]{:S(2)}, u32[]{:S(2)}) collective-permute-start(bf16[64,3584]{1,0:T(8,128)(2,1)S(1)} %get-tuple-element.32), channel_id=1, source_target_pairs={{0,16},{1,17},{2,18},{3,19},{4,20},{5,21},{6,22},{7,23},{8,24},{9,... | collective-permute-start | bytes 1376264 | tf_op jit(solution)/shard_map/ppermute | solution.py:164
  50.4 8.6 %collective-permute-start.17 = (bf16[64,3584]{1,0:T(8,128)(2,1)S(1)}, bf16[64,3584]{1,0:T(8,128)(2,1)S(1)}, u32[]{:S(2)}, u32[]{:S(2)}) collective-permute-start(bf16[64,3584]{1,0:T(8,128)(2,1)S(1)} %get-tuple-element.33), channel_id=1, source_target_pairs={{0,16},{1,17},{2,18},{3,19},{4,20},{5,21},{6,22},{7,23},{8,24},{9,... | collective-permute-start | bytes 1376264 | tf_op jit(solution)/shard_map/ppermute | solution.py:164
  58.4 6.5 %collective-permute-start.26 = (bf16[64,3712]{1,0:T(8,128)(2,1)S(1)}, bf16[64,3712]{1,0:T(8,128)(2,1)S(1)}, u32[]{:S(2)}, u32[]{:S(2)}) collective-permute-start(bf16[64,3712]{1,0:T(8,128)(2,1)S(1)} %collective-permute-done.6.refs_1_), channel_id=1, source_target_pairs={{0,16},{1,17},{2,18},{3,19},{4,20},{5,21},{6,22},{7,23},{8,24},{9,... | collective-permute-start | bytes 1425416 | tf_op jit(solution)/shard_map/ppermute | solution.py:164
  62.6 9.1 %collective-permute-start.20 = (bf16[64,3584]{1,0:T(8,128)(2,1)S(1)}, bf16[64,3584]{1,0:T(8,128)(2,1)S(1)}, u32[]{:S(2)}, u32[]{:S(2)}) collective-permute-start(bf16[64,3584]{1,0:T(8,128)(2,1)S(1)} %add_convert_fusion.6), channel_id=1, source_target_pairs={{0,1},{1,0},{2,3},{3,2},{4,5},{5,4},{6,7},{7,6},{8,9},{9,8},{10,11... | collective-permute-start | bytes 1376264 | tf_op jit(solution)/shard_map/ppermute | solution.py:164
  63.8 23.9 %collective-permute-start.19 = (bf16[64,3584]{1,0:T(8,128)(2,1)S(1)}, bf16[64,3584]{1,0:T(8,128)(2,1)S(1)}, u32[]{:S(2)}, u32[]{:S(2)}) collective-permute-start(bf16[64,3584]{1,0:T(8,128)(2,1)S(1)} %add_convert_fusion.7), channel_id=1, source_target_pairs={{0,1},{1,0},{2,3},{3,2},{4,5},{5,4},{6,7},{7,6},{8,9},{9,8},{10,11... | collective-permute-start | bytes 1376264 | tf_op jit(solution)/shard_map/ppermute | solution.py:164
  71.7 20.3 %collective-permute-start.30 = (bf16[64,3584]{1,0:T(8,128)(2,1)S(1)}, bf16[64,3584]{1,0:T(8,128)(2,1)S(1)}, u32[]{:S(2)}, u32[]{:S(2)}) collective-permute-start(bf16[64,3584]{1,0:T(8,128)(2,1)S(1)} %get-tuple-element.44), channel_id=1, source_target_pairs={{0,16},{1,17},{2,18},{3,19},{4,20},{5,21},{6,22},{7,23},{8,24},{9,... | collective-permute-start | bytes 1376264 | tf_op jit(solution)/shard_map/ppermute | solution.py:164
  72.4 15.3 %collective-permute-start.21 = (bf16[64,3584]{1,0:T(8,128)(2,1)S(1)}, bf16[64,3584]{1,0:T(8,128)(2,1)S(1)}, u32[]{:S(2)}, u32[]{:S(2)}) collective-permute-start(bf16[64,3584]{1,0:T(8,128)(2,1)S(1)} %add_convert_fusion.5), channel_id=1, source_target_pairs={{0,2},{1,3},{2,0},{3,1},{4,6},{5,7},{6,4},{7,5},{8,10},{9,11},{10,... | collective-permute-start | bytes 1376264 | tf_op jit(solution)/shard_map/ppermute | solution.py:164
  74.1 11.8 %collective-permute-start.35 = (bf16[64,3584]{1,0:T(8,128)(2,1)S(1)}, bf16[64,3584]{1,0:T(8,128)(2,1)S(1)}, u32[]{:S(2)}, u32[]{:S(2)}) collective-permute-start(bf16[64,3584]{1,0:T(8,128)(2,1)S(1)} %add_convert_fusion.2), channel_id=1, source_target_pairs={{0,1},{1,0},{2,3},{3,2},{4,5},{5,4},{6,7},{7,6},{8,9},{9,8},{10,11... | collective-permute-start | bytes 1376264 | tf_op jit(solution)/shard_map/ppermute | solution.py:164
  74.8 18.0 %collective-permute-start.32 = (bf16[64,3584]{1,0:T(8,128)(2,1)S(1)}, bf16[64,3584]{1,0:T(8,128)(2,1)S(1)}, u32[]{:S(2)}, u32[]{:S(2)}) collective-permute-start(bf16[64,3584]{1,0:T(8,128)(2,1)S(1)} %add_convert_fusion.3), channel_id=1, source_target_pairs={{0,1},{1,0},{2,3},{3,2},{4,5},{5,4},{6,7},{7,6},{8,9},{9,8},{10,11... | collective-permute-start | bytes 1376264 | tf_op jit(solution)/shard_map/ppermute | solution.py:164
  86.1 9.6 %collective-permute-start.36 = (bf16[64,3584]{1,0:T(8,128)(2,1)S(1)}, bf16[64,3584]{1,0:T(8,128)(2,1)S(1)}, u32[]{:S(2)}, u32[]{:S(2)}) collective-permute-start(bf16[64,3584]{1,0:T(8,128)(2,1)S(1)} %add_convert_fusion.1), channel_id=1, source_target_pairs={{0,2},{1,3},{2,0},{3,1},{4,6},{5,7},{6,4},{7,5},{8,10},{9,11},{10,... | collective-permute-start | bytes 1376264 | tf_op jit(solution)/shard_map/ppermute | solution.py:164
  87.9 11.9 %collective-permute-start.22 = (bf16[16,3584]{1,0:T(8,128)(2,1)S(1)}, bf16[16,3584]{1,0:T(8,128)(2,1)S(1)}, u32[]{:S(2)}, u32[]{:S(2)}) collective-permute-start(bf16[16,3584]{1,0:T(8,128)(2,1)S(1)} %get-tuple-element.50), channel_id=1, source_target_pairs={{0,4},{1,5},{2,6},{3,7},{4,0},{5,1},{6,2},{7,3},{8,12},{9,13},{10,... | collective-permute-start | bytes 344072 | tf_op jit(solution)/shard_map/ppermute | solution.py:164
  88.9 11.5 %collective-permute-start.23 = (bf16[16,3584]{1,0:T(8,128)(2,1)S(1)}, bf16[16,3584]{1,0:T(8,128)(2,1)S(1)}, u32[]{:S(2)}, u32[]{:S(2)}) collective-permute-start(bf16[16,3584]{1,0:T(8,128)(2,1)S(1)} %get-tuple-element.52), channel_id=1, source_target_pairs={{0,8},{1,9},{2,10},{3,11},{4,12},{5,13},{6,14},{7,15},{8,0},{9,1},... | collective-permute-start | bytes 344072 | tf_op jit(solution)/shard_map/ppermute | solution.py:164
  92.0 8.4 %collective-permute-start.24 = (bf16[16,3584]{1,0:T(8,128)(2,1)S(1)}, bf16[16,3584]{1,0:T(8,128)(2,1)S(1)}, u32[]{:S(2)}, u32[]{:S(2)}) collective-permute-start(bf16[16,3584]{1,0:T(8,128)(2,1)S(1)} %get-tuple-element.51), channel_id=1, source_target_pairs={{0,12},{1,13},{2,14},{3,15},{4,8},{5,9},{6,10},{7,11},{8,4},{9,5},... | collective-permute-start | bytes 344072 | tf_op jit(solution)/shard_map/ppermute | solution.py:164
  95.9 7.1 %collective-permute-start.37 = (bf16[16,3584]{1,0:T(8,128)(2,1)S(1)}, bf16[16,3584]{1,0:T(8,128)(2,1)S(1)}, u32[]{:S(2)}, u32[]{:S(2)}) collective-permute-start(bf16[16,3584]{1,0:T(8,128)(2,1)S(1)} %get-tuple-element.53), channel_id=1, source_target_pairs={{0,4},{1,5},{2,6},{3,7},{4,0},{5,1},{6,2},{7,3},{8,12},{9,13},{10,... | collective-permute-start | bytes 344072 | tf_op jit(solution)/shard_map/ppermute | solution.py:164
  96.9 12.8 %collective-permute-start.38 = (bf16[16,3584]{1,0:T(8,128)(2,1)S(1)}, bf16[16,3584]{1,0:T(8,128)(2,1)S(1)}, u32[]{:S(2)}, u32[]{:S(2)}) collective-permute-start(bf16[16,3584]{1,0:T(8,128)(2,1)S(1)} %get-tuple-element.55), channel_id=1, source_target_pairs={{0,8},{1,9},{2,10},{3,11},{4,12},{5,13},{6,14},{7,15},{8,0},{9,1},... | collective-permute-start | bytes 344072 | tf_op jit(solution)/shard_map/ppermute | solution.py:164
  99.8 9.9 %collective-permute-start.39 = (bf16[16,3584]{1,0:T(8,128)(2,1)S(1)}, bf16[16,3584]{1,0:T(8,128)(2,1)S(1)}, u32[]{:S(2)}, u32[]{:S(2)}) collective-permute-start(bf16[16,3584]{1,0:T(8,128)(2,1)S(1)} %get-tuple-element.54), channel_id=1, source_target_pairs={{0,12},{1,13},{2,14},{3,15},{4,8},{5,9},{6,10},{7,11},{8,4},{9,5},... | collective-permute-start | bytes 344072 | tf_op jit(solution)/shard_map/ppermute | solution.py:164
  (15 other events, 142.4 us)

commit v4 on v3

--- a/solution.py
+++ b/solution.py
@@ -158,7 +158,6 @@
         side *= 2
     depth = experts // (side * side)
     chunk = tok_count // chunk_count
-    block = depth * chunk
 
     def send(value, kind, step=1):
         return lax.ppermute(value, both_axes, shift_pairs(kind, step, depth, side))
@@ -196,7 +195,6 @@
     gathered = []
     coming = along(pieces(0))
     coming[1] = after(coming[1], early)
-    last = None
     for c in range(chunk_count):
         line = jnp.concatenate(coming, axis=0)
         if c + 1 < chunk_count:
@@ -208,7 +206,6 @@
         blocks = list(first)
         for k in range(1, side):
             blocks += [send(part, "last", k) for part in first]
-        last = blocks[-1]
         gathered.append(blocks + [send(part, "role") for part in blocks])
 
     finished = []
@@ -228,7 +225,7 @@
         other_results = expert(other)
         theirs = [send(part, "role") for part in other_results]
         if summed is not None:
-            own = [after(own[0], other_results[-1])] + own[1:]
+            own = [after(own[0], theirs[-1])] + own[1:]
         if c + 1 < chunk_count:
             following = gathered[c + 1]
             own = [after(own[0], following[1], following[side], *theirs)] + own[1:]

time: 111 us -> 109 us (0.982)
    ppermute x40, waiting for transfers between devices: 40.2 us -> 39.1 us  [send(): return lax.ppermute(value, both_axes, shift_pairs(kind, step, depth, side))]
  transfers between devices with their start and end apart: 40 -> 40, of which waited for: 10 -> 11; matrix products, arithmetic and copies ran while one was open for 3% -> 3% of each run, Pallas kernels for 21% -> 21%
where the time goes in v4:
time: 109 us
  waiting for transfers between devices  39.1 us (36%)
  starting transfers between devices  37.1 us (34%)
  Pallas kernels  23 us (21%)
  local copies, waits for them, and re-layouts  5.17 us (5%)
  other arithmetic  3.55 us (3%)
    ppermute x40, waiting for transfers between devices, send(): return lax.ppermute(value, both_axes, shift_pairs(kind, step, depth, side))  39.1 us
    ppermute x40, starting transfers between devices, send(): return lax.ppermute(value, both_axes, shift_pairs(kind, step, depth, side))  37.1 us
    pallas_call x4, Pallas kernels, expert_blocks(): pl.pallas_call(functools.partial(expert_kernel, count), out_shape=[jax.Sh...  12.2 us
    pallas_call x2, Pallas kernels, attend_rows(): pl.pallas_call(attend_kernel, out_shape=jax.ShapeDtypeStruct((count, head...  10.7 us
    unnamed x17, local copies, waits for them, and re-layouts  2.23 us
  transfers between devices with their start and end apart: 40, of which 11 were waited for; matrix products, arithmetic and copies ran while one was open for 3% of the time, Pallas kernels for 21%

profile of v4, /device:TPU:0, one launch (start us, length us, event | category | flops | bytes accessed | tf_op | source)
XLA Modules:
  0.0 108.9 jit_solution(15080572978902862411)
XLA Ops:
  2.6 3.1 %collective-permute-start = (bf16[16,3712]{1,0:T(8,128)(2,1)S(1)}, bf16[16,3712]{1,0:T(8,128)(2,1)S(1)}, u32[]{:S(2)}, u32[]{:S(2)}) collective-permute-start(bf16[16,3712]{1,0:T(8,128)(2,1)S(1)} %get-tuple-element.56), channel_id=1, source_target_pairs={{0,4},{1,5},{2,6},{3,7},{4,0},{5,1},{6,2},{7,3},{8,12},{9,13},{10,... | collective-permute-start | bytes 356360 | tf_op jit(solution)/shard_map/ppermute | solution.py:163
  5.7 2.6 %collective-permute-start.1 = (bf16[16,3712]{1,0:T(8,128)(2,1)S(1)}, bf16[16,3712]{1,0:T(8,128)(2,1)S(1)}, u32[]{:S(2)}, u32[]{:S(2)}) collective-permute-start(bf16[16,3712]{1,0:T(8,128)(2,1)S(1)} %get-tuple-element.56), channel_id=1, source_target_pairs={{0,8},{1,9},{2,10},{3,11},{4,12},{5,13},{6,14},{7,15},{8,0},{9,1},... | collective-permute-start | bytes 356360 | tf_op jit(solution)/shard_map/ppermute | solution.py:163
  10.0 1.2 %copy-done.3 = bf16[4,64,2048]{2,1,0:T(8,128)(2,1)S(1)} copy-done((bf16[4,64,2048]{2,1,0:T(8,128)(2,1)S(1)}, bf16[4,64,2048]{2,1,0:T(8,128)(2,1)}, u32[]{:S(2)}) %copy-start.3) | copy-done | bytes 1048600
  12.1 5.1 %attend_rows.2 = bf16[2,64,512]{2,1,0:T(8,128)(2,1)S(1)} custom-call(s32[2]{0:T(128)S(1)} %get-tuple-element.61.lengths_ref, bf16[4,64,512]{2,1,0:T(8,128)(2,1)S(1)} %copy-done.5, bf16[4,64,64]{2,1,0:T(8,128)(2,1)S(1)} %reshape.46.rope_ref, bf16[4,2048,512]{2,1,0:T(8,128)(2,1)} %cache_ref.3, bf16[4,64,2048]{2,1,0:T(8,128)(2,1)S(1)} %copy-done.3), custom_call_target="tpu_custom_call" | custom-call | flops 570425344 | bytes 4718592 | tf_op jit(solution)/shard_map/attend_rows/pallas_call | solution.py:62
  17.7 1.9 %collective-permute-start.3 = (bf16[16,3712]{1,0:T(8,128)(2,1)S(1)}, bf16[16,3712]{1,0:T(8,128)(2,1)S(1)}, u32[]{:S(2)}, u32[]{:S(2)}) collective-permute-start(bf16[16,3712]{1,0:T(8,128)(2,1)S(1)} %get-tuple-element.28), channel_id=1, source_target_pairs={{0,4},{1,5},{2,6},{3,7},{4,0},{5,1},{6,2},{7,3},{8,12},{9,13},{10,... | collective-permute-start | bytes 356360 | tf_op jit(solution)/shard_map/ppermute | solution.py:163
  19.6 2.2 %collective-permute-start.4 = (bf16[16,3712]{1,0:T(8,128)(2,1)S(1)}, bf16[16,3712]{1,0:T(8,128)(2,1)S(1)}, u32[]{:S(2)}, u32[]{:S(2)}) collective-permute-start(bf16[16,3712]{1,0:T(8,128)(2,1)S(1)} %get-tuple-element.28), channel_id=1, source_target_pairs={{0,8},{1,9},{2,10},{3,11},{4,12},{5,13},{6,14},{7,15},{8,0},{9,1},... | collective-permute-start | bytes 356360 | tf_op jit(solution)/shard_map/ppermute | solution.py:163
  22.2 1.5 %collective-permute-start.9 = (bf16[64,3712]{1,0:T(8,128)(2,1)S(1)}, bf16[64,3712]{1,0:T(8,128)(2,1)S(1)}, u32[]{:S(2)}, u32[]{:S(2)}) collective-permute-start(bf16[64,3712]{1,0:T(8,128)(2,1)S(1)} %pad_maximum_fusion.refs_0_), channel_id=1, source_target_pairs={{0,2},{1,3},{2,0},{3,1},{4,6},{5,7},{6,4},{7,5},{8,10},{9,11},{10,... | collective-permute-start | bytes 1425416 | tf_op jit(solution)/shard_map/ppermute | solution.py:163
  23.7 1.5 %collective-permute-start.11 = (bf16[64,3712]{1,0:T(8,128)(2,1)S(1)}, bf16[64,3712]{1,0:T(8,128)(2,1)S(1)}, u32[]{:S(2)}, u32[]{:S(2)}) collective-permute-start(bf16[64,3712]{1,0:T(8,128)(2,1)S(1)} %pad_maximum_fusion.refs_0_), channel_id=1, source_target_pairs={{0,1},{1,0},{2,3},{3,2},{4,5},{5,4},{6,7},{7,6},{8,9},{9,8},{10,11... | collective-permute-start | bytes 1425416 | tf_op jit(solution)/shard_map/ppermute | solution.py:163
  25.3 5.6 %attend_rows.3 = bf16[2,64,512]{2,1,0:T(8,128)(2,1)S(1)} custom-call(s32[2]{0:T(128)S(1)} %get-tuple-element.60.lengths_ref, bf16[4,64,512]{2,1,0:T(8,128)(2,1)S(1)} %copy-done.6, bf16[4,64,64]{2,1,0:T(8,128)(2,1)S(1)} %reshape.46.rope_ref, bf16[4,2048,512]{2,1,0:T(8,128)(2,1)} %cache_ref.3, bf16[4,64,2048]{2,1,0:T(8,128)(2,1)S(1)} %copy-done.4), custom_call_target="tpu_custom_call" | custom-call | flops 570425344 | bytes 4718592 | tf_op jit(solution)/shard_map/attend_rows/pallas_call | solution.py:62
  31.0 3.7 %collective-permute-done.9.refs_1_ = bf16[64,3712]{1,0:T(8,128)(2,1)S(1)} collective-permute-done((bf16[64,3712]{1,0:T(8,128)(2,1)S(1)}, bf16[64,3712]{1,0:T(8,128)(2,1)S(1)}, u32[]{:S(2)}, u32[]{:S(2)}) %collective-permute-start.9) | collective-permute-done | bytes 475168 | tf_op jit(solution)/shard_map/ppermute | solution.py:163
  35.2 2.2 %collective-permute-start.6 = (bf16[64,3712]{1,0:T(8,128)(2,1)S(1)}, bf16[64,3712]{1,0:T(8,128)(2,1)S(1)}, u32[]{:S(2)}, u32[]{:S(2)}) collective-permute-start(bf16[64,3712]{1,0:T(8,128)(2,1)S(1)} %constant_dynamic-update-slice_fusion.refs_0_), channel_id=1, source_target_pairs={{0,2},{1,3},{2,0},{3,1},{4,6},{5,7},{6,4},{7,5},{8,10},{9,11},{10,... | collective-permute-start | bytes 1425416 | tf_op jit(solution)/shard_map/ppermute | solution.py:163
  37.9 6.8 %collective-permute-done.13.refs_3_ = bf16[64,3712]{1,0:T(8,128)(2,1)S(1)} collective-permute-done((bf16[64,3712]{1,0:T(8,128)(2,1)S(1)}, bf16[64,3712]{1,0:T(8,128)(2,1)S(1)}, u32[]{:S(2)}, u32[]{:S(2)}) %collective-permute-start.13) | collective-permute-done | bytes 475168 | tf_op jit(solution)/shard_map/ppermute | solution.py:163
  45.6 1.1 collective-permute-start.28
  46.7 3.0 %expert_blocks.4 = (bf16[64,3584]{1,0:T(8,128)(2,1)S(1)}, bf16[64,3584]{1,0:T(8,128)(2,1)S(1)}, bf16[64,3584]{1,0:T(8,128)(2,1)S(1)}, bf16[64,3584]{1,0:T(8,128)(2,1)S(1)}) custom-call(f32[1,128]{1,0:T(1,128)S(1)} %or_convert_fusion.lane_ref, bf16[64,3712]{1,0:T(8,128)(2,1)S(1)} %collective-permute-done.8.refs_0_, ...), custom_call_target="tpu_custom_call" | custom-call | flops 2818572288 | bytes 14680064 | tf_op jit(solution)/shard_map/expert_blocks/pallas_call | solution.py:121
  50.4 2.9 %collective-permute-done.7.refs_2_ = bf16[64,3712]{1,0:T(8,128)(2,1)S(1)} collective-permute-done((bf16[64,3712]{1,0:T(8,128)(2,1)S(1)}, bf16[64,3712]{1,0:T(8,128)(2,1)S(1)}, u32[]{:S(2)}, u32[]{:S(2)}) %collective-permute-start.7) | collective-permute-done | bytes 475168 | tf_op jit(solution)/shard_map/ppermute | solution.py:163
  54.0 4.4 %collective-permute-done.28.refs_3_ = bf16[64,3712]{1,0:T(8,128)(2,1)S(1)} collective-permute-done((bf16[64,3712]{1,0:T(8,128)(2,1)S(1)}, bf16[64,3712]{1,0:T(8,128)(2,1)S(1)}, u32[]{:S(2)}, u32[]{:S(2)}) %collective-permute-start.28) | collective-permute-done | bytes 475168 | tf_op jit(solution)/shard_map/ppermute | solution.py:163
  59.4 3.0 %expert_blocks.5 = (bf16[64,3584]{1,0:T(8,128)(2,1)S(1)}, bf16[64,3584]{1,0:T(8,128)(2,1)S(1)}, bf16[64,3584]{1,0:T(8,128)(2,1)S(1)}, bf16[64,3584]{1,0:T(8,128)(2,1)S(1)}) custom-call(f32[1,128]{1,0:T(1,128)S(1)} %or_convert_fusion.lane_ref, bf16[64,3712]{1,0:T(8,128)(2,1)S(1)} %pad_maximum_fusion.refs_0_, ...), custom_call_target="tpu_custom_call" | custom-call | flops 2818572288 | bytes 14680064 | tf_op jit(solution)/shard_map/expert_blocks/pallas_call | solution.py:121
  62.6 1.0 collective-permute-start.20
  63.8 1.1 %collective-permute-start.19 = (bf16[64,3584]{1,0:T(8,128)(2,1)S(1)}, bf16[64,3584]{1,0:T(8,128)(2,1)S(1)}, u32[]{:S(2)}, u32[]{:S(2)}) collective-permute-start(bf16[64,3584]{1,0:T(8,128)(2,1)S(1)} %add_convert_fusion.7), channel_id=1, source_target_pairs={{0,1},{1,0},{2,3},{3,2},{4,5},{5,4},{6,7},{7,6},{8,9},{9,8},{10,11... | collective-permute-start | bytes 1376264 | tf_op jit(solution)/shard_map/ppermute | solution.py:163
  64.9 3.1 %expert_blocks.6 = (bf16[64,3584]{1,0:T(8,128)(2,1)S(1)}, bf16[64,3584]{1,0:T(8,128)(2,1)S(1)}, bf16[64,3584]{1,0:T(8,128)(2,1)S(1)}, bf16[64,3584]{1,0:T(8,128)(2,1)S(1)}) custom-call(f32[1,128]{1,0:T(1,128)S(1)} %or_convert_fusion.lane_ref, bf16[64,3712]{1,0:T(8,128)(2,1)S(1)} %collective-permute-done.25.refs_0_, ...), custom_call_target="tpu_custom_call" | custom-call | flops 2818572288 | bytes 14680064 | tf_op jit(solution)/shard_map/expert_blocks/pallas_call | solution.py:121
  68.7 2.5 %collective-permute-done.20 = bf16[64,3584]{1,0:T(8,128)(2,1)S(1)} collective-permute-done((bf16[64,3584]{1,0:T(8,128)(2,1)S(1)}, bf16[64,3584]{1,0:T(8,128)(2,1)S(1)}, u32[]{:S(2)}, u32[]{:S(2)}) %collective-permute-start.20) | collective-permute-done | bytes 458784 | tf_op jit(solution)/shard_map/ppermute | solution.py:163
  71.3 1.6 %collective-permute-start.21 = (bf16[64,3584]{1,0:T(8,128)(2,1)S(1)}, bf16[64,3584]{1,0:T(8,128)(2,1)S(1)}, u32[]{:S(2)}, u32[]{:S(2)}) collective-permute-start(bf16[64,3584]{1,0:T(8,128)(2,1)S(1)} %add_convert_fusion.5), channel_id=1, source_target_pairs={{0,2},{1,3},{2,0},{3,1},{4,6},{5,7},{6,4},{7,5},{8,10},{9,11},{10,... | collective-permute-start | bytes 1376264 | tf_op jit(solution)/shard_map/ppermute | solution.py:163
  72.9 3.1 %expert_blocks.7 = (bf16[64,3584]{1,0:T(8,128)(2,1)S(1)}, bf16[64,3584]{1,0:T(8,128)(2,1)S(1)}, bf16[64,3584]{1,0:T(8,128)(2,1)S(1)}, bf16[64,3584]{1,0:T(8,128)(2,1)S(1)}) custom-call(f32[1,128]{1,0:T(1,128)S(1)} %or_convert_fusion.lane_ref, bf16[64,3712]{1,0:T(8,128)(2,1)S(1)} %constant_dynamic-update-slice_fusion.refs_0_, ...), custom_call_target="tpu_custom_call" | custom-call | flops 2818572288 | bytes 14680064 | tf_op jit(solution)/shard_map/expert_blocks/pallas_call | solution.py:121
  76.8 1.6 %collective-permute-start.33 = (bf16[64,3584]{1,0:T(8,128)(2,1)S(1)}, bf16[64,3584]{1,0:T(8,128)(2,1)S(1)}, u32[]{:S(2)}, u32[]{:S(2)}) collective-permute-start(bf16[64,3584]{1,0:T(8,128)(2,1)S(1)} %add_convert_fusion.3), channel_id=1, source_target_pairs={{0,1},{1,0},{2,3},{3,2},{4,5},{5,4},{6,7},{7,6},{8,9},{9,8},{10,11... | collective-permute-start | bytes 1376264 | tf_op jit(solution)/shard_map/ppermute | solution.py:163
  78.4 7.5 %collective-permute-done.35 = bf16[64,3584]{1,0:T(8,128)(2,1)S(1)} collective-permute-done((bf16[64,3584]{1,0:T(8,128)(2,1)S(1)}, bf16[64,3584]{1,0:T(8,128)(2,1)S(1)}, u32[]{:S(2)}, u32[]{:S(2)}) %collective-permute-start.35) | collective-permute-done | bytes 458784 | tf_op jit(solution)/shard_map/ppermute | solution.py:163
  86.1 1.6 %collective-permute-start.36 = (bf16[64,3584]{1,0:T(8,128)(2,1)S(1)}, bf16[64,3584]{1,0:T(8,128)(2,1)S(1)}, u32[]{:S(2)}, u32[]{:S(2)}) collective-permute-start(bf16[64,3584]{1,0:T(8,128)(2,1)S(1)} %add_convert_fusion.1), channel_id=1, source_target_pairs={{0,2},{1,3},{2,0},{3,1},{4,6},{5,7},{6,4},{7,5},{8,10},{9,11},{10,... | collective-permute-start | bytes 1376264 | tf_op jit(solution)/shard_map/ppermute | solution.py:163
  88.9 3.1 %collective-permute-start.23 = (bf16[16,3584]{1,0:T(8,128)(2,1)S(1)}, bf16[16,3584]{1,0:T(8,128)(2,1)S(1)}, u32[]{:S(2)}, u32[]{:S(2)}) collective-permute-start(bf16[16,3584]{1,0:T(8,128)(2,1)S(1)} %get-tuple-element.52), channel_id=1, source_target_pairs={{0,8},{1,9},{2,10},{3,11},{4,12},{5,13},{6,14},{7,15},{8,0},{9,1},... | collective-permute-start | bytes 344072 | tf_op jit(solution)/shard_map/ppermute | solution.py:163
  92.4 1.2 %collective-permute-done.33 = bf16[64,3584]{1,0:T(8,128)(2,1)S(1)} collective-permute-done((bf16[64,3584]{1,0:T(8,128)(2,1)S(1)}, bf16[64,3584]{1,0:T(8,128)(2,1)S(1)}, u32[]{:S(2)}, u32[]{:S(2)}) %collective-permute-start.33) | collective-permute-done | bytes 458784 | tf_op jit(solution)/shard_map/ppermute | solution.py:163
  93.6 1.2 %collective-permute-done.36 = bf16[64,3584]{1,0:T(8,128)(2,1)S(1)} collective-permute-done((bf16[64,3584]{1,0:T(8,128)(2,1)S(1)}, bf16[64,3584]{1,0:T(8,128)(2,1)S(1)}, u32[]{:S(2)}, u32[]{:S(2)}) %collective-permute-start.36) | collective-permute-done | bytes 458784 | tf_op jit(solution)/shard_map/ppermute | solution.py:163
  96.1 3.1 %collective-permute-start.38 = (bf16[16,3584]{1,0:T(8,128)(2,1)S(1)}, bf16[16,3584]{1,0:T(8,128)(2,1)S(1)}, u32[]{:S(2)}, u32[]{:S(2)}) collective-permute-start(bf16[16,3584]{1,0:T(8,128)(2,1)S(1)} %get-tuple-element.55), channel_id=1, source_target_pairs={{0,8},{1,9},{2,10},{3,11},{4,12},{5,13},{6,14},{7,15},{8,0},{9,1},... | collective-permute-start | bytes 344072 | tf_op jit(solution)/shard_map/ppermute | solution.py:163
  99.6 4.0 %collective-permute-done.37 = bf16[16,3584]{1,0:T(8,128)(2,1)S(1)} collective-permute-done((bf16[16,3584]{1,0:T(8,128)(2,1)S(1)}, bf16[16,3584]{1,0:T(8,128)(2,1)S(1)}, u32[]{:S(2)}, u32[]{:S(2)}) %collective-permute-start.37) | collective-permute-done | bytes 114720 | tf_op jit(solution)/shard_map/ppermute | solution.py:163
  103.6 4.4 %collective-permute-done.38 = bf16[16,3584]{1,0:T(8,128)(2,1)S(1)} collective-permute-done((bf16[16,3584]{1,0:T(8,128)(2,1)S(1)}, bf16[16,3584]{1,0:T(8,128)(2,1)S(1)}, u32[]{:S(2)}, u32[]{:S(2)}) %collective-permute-start.38) | collective-permute-done | bytes 114720 | tf_op jit(solution)/shard_map/ppermute | solution.py:163
  (98 shorter events, 16.0 us)
Async XLA Ops:
  2.6 14.7 %collective-permute-start = (bf16[16,3712]{1,0:T(8,128)(2,1)S(1)}, bf16[16,3712]{1,0:T(8,128)(2,1)S(1)}, u32[]{:S(2)}, u32[]{:S(2)}) collective-permute-start(bf16[16,3712]{1,0:T(8,128)(2,1)S(1)} %get-tuple-element.56), channel_id=1, source_target_pairs={{0,4},{1,5},{2,6},{3,7},{4,0},{5,1},{6,2},{7,3},{8,12},{9,13},{10,... | collective-permute-start | bytes 356360 | tf_op jit(solution)/shard_map/ppermute | solution.py:163
  5.7 12.0 %collective-permute-start.1 = (bf16[16,3712]{1,0:T(8,128)(2,1)S(1)}, bf16[16,3712]{1,0:T(8,128)(2,1)S(1)}, u32[]{:S(2)}, u32[]{:S(2)}) collective-permute-start(bf16[16,3712]{1,0:T(8,128)(2,1)S(1)} %get-tuple-element.56), channel_id=1, source_target_pairs={{0,8},{1,9},{2,10},{3,11},{4,12},{5,13},{6,14},{7,15},{8,0},{9,1},... | collective-permute-start | bytes 356360 | tf_op jit(solution)/shard_map/ppermute | solution.py:163
  8.3 9.4 %collective-permute-start.2 = (bf16[16,3712]{1,0:T(8,128)(2,1)S(1)}, bf16[16,3712]{1,0:T(8,128)(2,1)S(1)}, u32[]{:S(2)}, u32[]{:S(2)}) collective-permute-start(bf16[16,3712]{1,0:T(8,128)(2,1)S(1)} %get-tuple-element.56), channel_id=1, source_target_pairs={{0,12},{1,13},{2,14},{3,15},{4,8},{5,9},{6,10},{7,11},{8,4},{9,5},... | collective-permute-start | bytes 356360 | tf_op jit(solution)/shard_map/ppermute | solution.py:163
  17.7 13.1 %collective-permute-start.3 = (bf16[16,3712]{1,0:T(8,128)(2,1)S(1)}, bf16[16,3712]{1,0:T(8,128)(2,1)S(1)}, u32[]{:S(2)}, u32[]{:S(2)}) collective-permute-start(bf16[16,3712]{1,0:T(8,128)(2,1)S(1)} %get-tuple-element.28), channel_id=1, source_target_pairs={{0,4},{1,5},{2,6},{3,7},{4,0},{5,1},{6,2},{7,3},{8,12},{9,13},{10,... | collective-permute-start | bytes 356360 | tf_op jit(solution)/shard_map/ppermute | solution.py:163
  19.6 11.3 %collective-permute-start.4 = (bf16[16,3712]{1,0:T(8,128)(2,1)S(1)}, bf16[16,3712]{1,0:T(8,128)(2,1)S(1)}, u32[]{:S(2)}, u32[]{:S(2)}) collective-permute-start(bf16[16,3712]{1,0:T(8,128)(2,1)S(1)} %get-tuple-element.28), channel_id=1, source_target_pairs={{0,8},{1,9},{2,10},{3,11},{4,12},{5,13},{6,14},{7,15},{8,0},{9,1},... | collective-permute-start | bytes 356360 | tf_op jit(solution)/shard_map/ppermute | solution.py:163
  21.8 9.2 %collective-permute-start.5 = (bf16[16,3712]{1,0:T(8,128)(2,1)S(1)}, bf16[16,3712]{1,0:T(8,128)(2,1)S(1)}, u32[]{:S(2)}, u32[]{:S(2)}) collective-permute-start(bf16[16,3712]{1,0:T(8,128)(2,1)S(1)} %get-tuple-element.28), channel_id=1, source_target_pairs={{0,12},{1,13},{2,14},{3,15},{4,8},{5,9},{6,10},{7,11},{8,4},{9,5},... | collective-permute-start | bytes 356360 | tf_op jit(solution)/shard_map/ppermute | solution.py:163
  22.2 12.5 %collective-permute-start.9 = (bf16[64,3712]{1,0:T(8,128)(2,1)S(1)}, bf16[64,3712]{1,0:T(8,128)(2,1)S(1)}, u32[]{:S(2)}, u32[]{:S(2)}) collective-permute-start(bf16[64,3712]{1,0:T(8,128)(2,1)S(1)} %pad_maximum_fusion.refs_0_), channel_id=1, source_target_pairs={{0,2},{1,3},{2,0},{3,1},{4,6},{5,7},{6,4},{7,5},{8,10},{9,11},{10,... | collective-permute-start | bytes 1425416 | tf_op jit(solution)/shard_map/ppermute | solution.py:163
  23.7 13.7 %collective-permute-start.11 = (bf16[64,3712]{1,0:T(8,128)(2,1)S(1)}, bf16[64,3712]{1,0:T(8,128)(2,1)S(1)}, u32[]{:S(2)}, u32[]{:S(2)}) collective-permute-start(bf16[64,3712]{1,0:T(8,128)(2,1)S(1)} %pad_maximum_fusion.refs_0_), channel_id=1, source_target_pairs={{0,1},{1,0},{2,3},{3,2},{4,5},{5,4},{6,7},{7,6},{8,9},{9,8},{10,11... | collective-permute-start | bytes 1425416 | tf_op jit(solution)/shard_map/ppermute | solution.py:163
  30.9 13.8 %collective-permute-start.8 = (bf16[64,3712]{1,0:T(8,128)(2,1)S(1)}, bf16[64,3712]{1,0:T(8,128)(2,1)S(1)}, u32[]{:S(2)}, u32[]{:S(2)}) collective-permute-start(bf16[64,3712]{1,0:T(8,128)(2,1)S(1)} %pad_maximum_fusion.refs_0_), channel_id=1, source_target_pairs={{0,16},{1,17},{2,18},{3,19},{4,20},{5,21},{6,22},{7,23},{8,24},{9,... | collective-permute-start | bytes 1425416 | tf_op jit(solution)/shard_map/ppermute | solution.py:163
  34.7 10.0 %collective-permute-start.13 = (bf16[64,3712]{1,0:T(8,128)(2,1)S(1)}, bf16[64,3712]{1,0:T(8,128)(2,1)S(1)}, u32[]{:S(2)}, u32[]{:S(2)}) collective-permute-start(bf16[64,3712]{1,0:T(8,128)(2,1)S(1)} %collective-permute-done.9.refs_1_), channel_id=1, source_target_pairs={{0,1},{1,0},{2,3},{3,2},{4,5},{5,4},{6,7},{7,6},{8,9},{9,8},{10,11... | collective-permute-start | bytes 1425416 | tf_op jit(solution)/shard_map/ppermute | solution.py:163
  35.2 10.4 %collective-permute-start.6 = (bf16[64,3712]{1,0:T(8,128)(2,1)S(1)}, bf16[64,3712]{1,0:T(8,128)(2,1)S(1)}, u32[]{:S(2)}, u32[]{:S(2)}) collective-permute-start(bf16[64,3712]{1,0:T(8,128)(2,1)S(1)} %constant_dynamic-update-slice_fusion.refs_0_), channel_id=1, source_target_pairs={{0,2},{1,3},{2,0},{3,1},{4,6},{5,7},{6,4},{7,5},{8,10},{9,11},{10,... | collective-permute-start | bytes 1425416 | tf_op jit(solution)/shard_map/ppermute | solution.py:163
  37.4 9.3 %collective-permute-start.10 = (bf16[64,3712]{1,0:T(8,128)(2,1)S(1)}, bf16[64,3712]{1,0:T(8,128)(2,1)S(1)}, u32[]{:S(2)}, u32[]{:S(2)}) collective-permute-start(bf16[64,3712]{1,0:T(8,128)(2,1)S(1)} %collective-permute-done.9.refs_1_), channel_id=1, source_target_pairs={{0,16},{1,17},{2,18},{3,19},{4,20},{5,21},{6,22},{7,23},{8,24},{9,... | collective-permute-start | bytes 1425416 | tf_op jit(solution)/shard_map/ppermute | solution.py:163
  37.4 9.3 %collective-permute-start.12 = (bf16[64,3712]{1,0:T(8,128)(2,1)S(1)}, bf16[64,3712]{1,0:T(8,128)(2,1)S(1)}, u32[]{:S(2)}, u32[]{:S(2)}) collective-permute-start(bf16[64,3712]{1,0:T(8,128)(2,1)S(1)} %collective-permute-done.11.refs_2_), channel_id=1, source_target_pairs={{0,16},{1,17},{2,18},{3,19},{4,20},{5,21},{6,22},{7,23},{8,24},{9,... | collective-permute-start | bytes 1425416 | tf_op jit(solution)/shard_map/ppermute | solution.py:163
  44.7 8.7 %collective-permute-start.7 = (bf16[64,3712]{1,0:T(8,128)(2,1)S(1)}, bf16[64,3712]{1,0:T(8,128)(2,1)S(1)}, u32[]{:S(2)}, u32[]{:S(2)}) collective-permute-start(bf16[64,3712]{1,0:T(8,128)(2,1)S(1)} %constant_dynamic-update-slice_fusion.refs_0_), channel_id=1, source_target_pairs={{0,1},{1,0},{2,3},{3,2},{4,5},{5,4},{6,7},{7,6},{8,9},{9,8},{10,11... | collective-permute-start | bytes 1425416 | tf_op jit(solution)/shard_map/ppermute | solution.py:163
  45.6 12.8 %collective-permute-start.28 = (bf16[64,3712]{1,0:T(8,128)(2,1)S(1)}, bf16[64,3712]{1,0:T(8,128)(2,1)S(1)}, u32[]{:S(2)}, u32[]{:S(2)}) collective-permute-start(bf16[64,3712]{1,0:T(8,128)(2,1)S(1)} %collective-permute-done.6.refs_1_), channel_id=1, source_target_pairs={{0,1},{1,0},{2,3},{3,2},{4,5},{5,4},{6,7},{7,6},{8,9},{9,8},{10,11... | collective-permute-start | bytes 1425416 | tf_op jit(solution)/shard_map/ppermute | solution.py:163
  49.8 8.6 %collective-permute-start.15 = (bf16[64,3584]{1,0:T(8,128)(2,1)S(1)}, bf16[64,3584]{1,0:T(8,128)(2,1)S(1)}, u32[]{:S(2)}, u32[]{:S(2)}) collective-permute-start(bf16[64,3584]{1,0:T(8,128)(2,1)S(1)} %get-tuple-element.31), channel_id=1, source_target_pairs={{0,16},{1,17},{2,18},{3,19},{4,20},{5,21},{6,22},{7,23},{8,24},{9,... | collective-permute-start | bytes 1376264 | tf_op jit(solution)/shard_map/ppermute | solution.py:163
  49.9 9.1 %collective-permute-start.16 = (bf16[64,3584]{1,0:T(8,128)(2,1)S(1)}, bf16[64,3584]{1,0:T(8,128)(2,1)S(1)}, u32[]{:S(2)}, u32[]{:S(2)}) collective-permute-start(bf16[64,3584]{1,0:T(8,128)(2,1)S(1)} %get-tuple-element.32), channel_id=1, source_target_pairs={{0,16},{1,17},{2,18},{3,19},{4,20},{5,21},{6,22},{7,23},{8,24},{9,... | collective-permute-start | bytes 1376264 | tf_op jit(solution)/shard_map/ppermute | solution.py:163
  50.4 8.6 %collective-permute-start.17 = (bf16[64,3584]{1,0:T(8,128)(2,1)S(1)}, bf16[64,3584]{1,0:T(8,128)(2,1)S(1)}, u32[]{:S(2)}, u32[]{:S(2)}) collective-permute-start(bf16[64,3584]{1,0:T(8,128)(2,1)S(1)} %get-tuple-element.33), channel_id=1, source_target_pairs={{0,16},{1,17},{2,18},{3,19},{4,20},{5,21},{6,22},{7,23},{8,24},{9,... | collective-permute-start | bytes 1376264 | tf_op jit(solution)/shard_map/ppermute | solution.py:163
  62.6 8.5 %collective-permute-start.20 = (bf16[64,3584]{1,0:T(8,128)(2,1)S(1)}, bf16[64,3584]{1,0:T(8,128)(2,1)S(1)}, u32[]{:S(2)}, u32[]{:S(2)}) collective-permute-start(bf16[64,3584]{1,0:T(8,128)(2,1)S(1)} %add_convert_fusion.6), channel_id=1, source_target_pairs={{0,1},{1,0},{2,3},{3,2},{4,5},{5,4},{6,7},{7,6},{8,9},{9,8},{10,11... | collective-permute-start | bytes 1376264 | tf_op jit(solution)/shard_map/ppermute | solution.py:163
  63.8 23.9 %collective-permute-start.19 = (bf16[64,3584]{1,0:T(8,128)(2,1)S(1)}, bf16[64,3584]{1,0:T(8,128)(2,1)S(1)}, u32[]{:S(2)}, u32[]{:S(2)}) collective-permute-start(bf16[64,3584]{1,0:T(8,128)(2,1)S(1)} %add_convert_fusion.7), channel_id=1, source_target_pairs={{0,1},{1,0},{2,3},{3,2},{4,5},{5,4},{6,7},{7,6},{8,9},{9,8},{10,11... | collective-permute-start | bytes 1376264 | tf_op jit(solution)/shard_map/ppermute | solution.py:163
  68.1 8.0 %collective-permute-start.32 = (bf16[64,3584]{1,0:T(8,128)(2,1)S(1)}, bf16[64,3584]{1,0:T(8,128)(2,1)S(1)}, u32[]{:S(2)}, u32[]{:S(2)}) collective-permute-start(bf16[64,3584]{1,0:T(8,128)(2,1)S(1)} %get-tuple-element.46), channel_id=1, source_target_pairs={{0,16},{1,17},{2,18},{3,19},{4,20},{5,21},{6,22},{7,23},{8,24},{9,... | collective-permute-start | bytes 1376264 | tf_op jit(solution)/shard_map/ppermute | solution.py:163
  68.6 8.3 %collective-permute-start.34 = (bf16[64,3584]{1,0:T(8,128)(2,1)S(1)}, bf16[64,3584]{1,0:T(8,128)(2,1)S(1)}, u32[]{:S(2)}, u32[]{:S(2)}) collective-permute-start(bf16[64,3584]{1,0:T(8,128)(2,1)S(1)} %get-tuple-element.48), channel_id=1, source_target_pairs={{0,16},{1,17},{2,18},{3,19},{4,20},{5,21},{6,22},{7,23},{8,24},{9,... | collective-permute-start | bytes 1376264 | tf_op jit(solution)/shard_map/ppermute | solution.py:163
  71.2 20.9 %collective-permute-start.31 = (bf16[64,3584]{1,0:T(8,128)(2,1)S(1)}, bf16[64,3584]{1,0:T(8,128)(2,1)S(1)}, u32[]{:S(2)}, u32[]{:S(2)}) collective-permute-start(bf16[64,3584]{1,0:T(8,128)(2,1)S(1)} %get-tuple-element.44), channel_id=1, source_target_pairs={{0,16},{1,17},{2,18},{3,19},{4,20},{5,21},{6,22},{7,23},{8,24},{9,... | collective-permute-start | bytes 1376264 | tf_op jit(solution)/shard_map/ppermute | solution.py:163
  71.3 16.3 %collective-permute-start.21 = (bf16[64,3584]{1,0:T(8,128)(2,1)S(1)}, bf16[64,3584]{1,0:T(8,128)(2,1)S(1)}, u32[]{:S(2)}, u32[]{:S(2)}) collective-permute-start(bf16[64,3584]{1,0:T(8,128)(2,1)S(1)} %add_convert_fusion.5), channel_id=1, source_target_pairs={{0,2},{1,3},{2,0},{3,1},{4,6},{5,7},{6,4},{7,5},{8,10},{9,11},{10,... | collective-permute-start | bytes 1376264 | tf_op jit(solution)/shard_map/ppermute | solution.py:163
  76.1 9.8 %collective-permute-start.35 = (bf16[64,3584]{1,0:T(8,128)(2,1)S(1)}, bf16[64,3584]{1,0:T(8,128)(2,1)S(1)}, u32[]{:S(2)}, u32[]{:S(2)}) collective-permute-start(bf16[64,3584]{1,0:T(8,128)(2,1)S(1)} %add_convert_fusion.2), channel_id=1, source_target_pairs={{0,1},{1,0},{2,3},{3,2},{4,5},{5,4},{6,7},{7,6},{8,9},{9,8},{10,11... | collective-permute-start | bytes 1376264 | tf_op jit(solution)/shard_map/ppermute | solution.py:163
  76.8 16.8 %collective-permute-start.33 = (bf16[64,3584]{1,0:T(8,128)(2,1)S(1)}, bf16[64,3584]{1,0:T(8,128)(2,1)S(1)}, u32[]{:S(2)}, u32[]{:S(2)}) collective-permute-start(bf16[64,3584]{1,0:T(8,128)(2,1)S(1)} %add_convert_fusion.3), channel_id=1, source_target_pairs={{0,1},{1,0},{2,3},{3,2},{4,5},{5,4},{6,7},{7,6},{8,9},{9,8},{10,11... | collective-permute-start | bytes 1376264 | tf_op jit(solution)/shard_map/ppermute | solution.py:163
  86.1 8.8 %collective-permute-start.36 = (bf16[64,3584]{1,0:T(8,128)(2,1)S(1)}, bf16[64,3584]{1,0:T(8,128)(2,1)S(1)}, u32[]{:S(2)}, u32[]{:S(2)}) collective-permute-start(bf16[64,3584]{1,0:T(8,128)(2,1)S(1)} %add_convert_fusion.1), channel_id=1, source_target_pairs={{0,2},{1,3},{2,0},{3,1},{4,6},{5,7},{6,4},{7,5},{8,10},{9,11},{10,... | collective-permute-start | bytes 1376264 | tf_op jit(solution)/shard_map/ppermute | solution.py:163
  87.9 11.2 %collective-permute-start.22 = (bf16[16,3584]{1,0:T(8,128)(2,1)S(1)}, bf16[16,3584]{1,0:T(8,128)(2,1)S(1)}, u32[]{:S(2)}, u32[]{:S(2)}) collective-permute-start(bf16[16,3584]{1,0:T(8,128)(2,1)S(1)} %get-tuple-element.50), channel_id=1, source_target_pairs={{0,4},{1,5},{2,6},{3,7},{4,0},{5,1},{6,2},{7,3},{8,12},{9,13},{10,... | collective-permute-start | bytes 344072 | tf_op jit(solution)/shard_map/ppermute | solution.py:163
  88.9 10.6 %collective-permute-start.23 = (bf16[16,3584]{1,0:T(8,128)(2,1)S(1)}, bf16[16,3584]{1,0:T(8,128)(2,1)S(1)}, u32[]{:S(2)}, u32[]{:S(2)}) collective-permute-start(bf16[16,3584]{1,0:T(8,128)(2,1)S(1)} %get-tuple-element.52), channel_id=1, source_target_pairs={{0,8},{1,9},{2,10},{3,11},{4,12},{5,13},{6,14},{7,15},{8,0},{9,1},... | collective-permute-start | bytes 344072 | tf_op jit(solution)/shard_map/ppermute | solution.py:163
  95.1 8.5 %collective-permute-start.37 = (bf16[16,3584]{1,0:T(8,128)(2,1)S(1)}, bf16[16,3584]{1,0:T(8,128)(2,1)S(1)}, u32[]{:S(2)}, u32[]{:S(2)}) collective-permute-start(bf16[16,3584]{1,0:T(8,128)(2,1)S(1)} %get-tuple-element.53), channel_id=1, source_target_pairs={{0,4},{1,5},{2,6},{3,7},{4,0},{5,1},{6,2},{7,3},{8,12},{9,13},{10,... | collective-permute-start | bytes 344072 | tf_op jit(solution)/shard_map/ppermute | solution.py:163
  96.1 12.0 %collective-permute-start.38 = (bf16[16,3584]{1,0:T(8,128)(2,1)S(1)}, bf16[16,3584]{1,0:T(8,128)(2,1)S(1)}, u32[]{:S(2)}, u32[]{:S(2)}) collective-permute-start(bf16[16,3584]{1,0:T(8,128)(2,1)S(1)} %get-tuple-element.55), channel_id=1, source_target_pairs={{0,8},{1,9},{2,10},{3,11},{4,12},{5,13},{6,14},{7,15},{8,0},{9,1},... | collective-permute-start | bytes 344072 | tf_op jit(solution)/shard_map/ppermute | solution.py:163
  99.2 8.9 %collective-permute-start.39 = (bf16[16,3584]{1,0:T(8,128)(2,1)S(1)}, bf16[16,3584]{1,0:T(8,128)(2,1)S(1)}, u32[]{:S(2)}, u32[]{:S(2)}) collective-permute-start(bf16[16,3584]{1,0:T(8,128)(2,1)S(1)} %get-tuple-element.54), channel_id=1, source_target_pairs={{0,12},{1,13},{2,14},{3,15},{4,8},{5,9},{6,10},{7,11},{8,4},{9,5},... | collective-permute-start | bytes 344072 | tf_op jit(solution)/shard_map/ppermute | solution.py:163
  (15 other events, 143.1 us)

commit v5 on v4

--- a/solution.py
+++ b/solution.py
@@ -134,6 +134,35 @@
     )(own_lane, *blocks, gate_matrix, up_matrix, down_matrix)
 
 
+def pack_kernel(experts, rows_ref, ids_ref, gates_ref, *payload_refs):
+    count, width = rows_ref.shape
+    chunk = payload_refs[0].shape[0]
+    tail_width = payload_refs[0].shape[1] - width
+    lane = lax.broadcasted_iota(jnp.int32, (tail_width, count), 0)
+    named = jnp.where(lane < experts, lane, lane - experts)
+    dense = jnp.zeros((tail_width, count), jnp.float32)
+    for k in range(ids_ref.shape[0]):
+        dense = jnp.where(ids_ref[k : k + 1, :] == named, gates_ref[k : k + 1, :], dense)
+    upper = dense.astype(jnp.bfloat16).astype(jnp.float32)
+    tail = jnp.where(lane < experts, upper, dense - upper).T.astype(jnp.bfloat16)
+    for at, payload_ref in enumerate(payload_refs):
+        payload_ref[:, :width] = rows_ref[at * chunk : (at + 1) * chunk]
+        payload_ref[:, width:] = tail[at * chunk : (at + 1) * chunk]
+
+
+def pack_rows(rows, ids, gates, experts, tail_width):
+    count, width = rows.shape
+    chunk = count // chunk_count
+    inside = pl.BlockSpec(memory_space=pltpu.VMEM)
+    return pl.pallas_call(
+        functools.partial(pack_kernel, experts),
+        out_shape=[jax.ShapeDtypeStruct((chunk, width + tail_width), rows.dtype)] * chunk_count,
+        in_specs=[inside] * 3,
+        out_specs=[inside] * chunk_count,
+        name="pack_rows",
+    )(rows, ids.T, gates.T)
+
+
 def after(value, *earlier):
     return lax.optimization_barrier((value, *earlier))[0]
 
@@ -163,18 +192,11 @@
         return lax.ppermute(value, both_axes, shift_pairs(kind, step, depth, side))
 
     place = lax.axis_index("dev")
-    named = expert_ids[:, :, None] == jnp.arange(experts, dtype=jnp.int32)[None, None, :]
-    dense_gates = jnp.sum(jnp.where(named, gate_weights[:, :, None], 0.0), axis=1)
-    kept_part = lax.reduce_precision(dense_gates, exponent_bits=8, mantissa_bits=7)
-    upper = kept_part.astype(jnp.bfloat16)
-    lower = (dense_gates - kept_part).astype(jnp.bfloat16)
-    spare = -(2 * experts) % 128
-    tail = jnp.concatenate([upper, lower, jnp.zeros((tok_count, spare), jnp.bfloat16)], axis=1)
-    tail_width = tail.shape[1]
-    payload = jnp.concatenate([moe_rows, tail], axis=1)
+    tail_width = -(-2 * experts // 128) * 128
+    payloads = list(pack_rows(moe_rows, expert_ids, gate_weights, experts, tail_width))
     lane = jnp.arange(tail_width, dtype=jnp.int32)
     own_lane = ((lane == place) | (lane == place + experts)).astype(jnp.float32)[None, :]
-    payload = after(payload, own_lane)
+    payloads[0] = after(payloads[0], own_lane)
 
     att_rows = lengths.shape[0]
     rope_rows = q_rope.reshape(att_rows, q_latent.shape[1], rope_cache.shape[1])
@@ -186,7 +208,7 @@
         return attend_rows(q_latent, key, latent_cache, rope_cache, lengths, start, count)
 
     def pieces(c):
-        return payload[c * chunk : (c + 1) * chunk]
+        return payloads[c]
 
     def along(mine):
         return [mine] + [send(mine, "z", k) for k in range(1, depth)]

time: 109 us -> 110 us (level)
  Pallas kernels: 23 us -> 24.7 us
    pallas_call x0 -> x1, Pallas kernels: none -> 1.73 us  [pack_rows(): pl.pallas_call(functools.partial(pack_kernel, experts), out_shape=[jax.Sh...]
    unnamed x17 -> x22, local copies, waits for them, and re-layouts: 2.23 us -> 3.25 us
  transfers between devices with their start and end apart: 40 -> 40, of which waited for: 11 -> 10; matrix products, arithmetic and copies ran while one was open for 3% -> 4% of each run, Pallas kernels for 21% -> 21%
where the time goes in v5:
time: 110 us
  waiting for transfers between devices  38.8 us (35%)
  starting transfers between devices  37.2 us (34%)
  Pallas kernels  24.7 us (22%)
  local copies, waits for them, and re-layouts  5 us (5%)
  other arithmetic  2.77 us (3%)
    ppermute x40, waiting for transfers between devices, send(): return lax.ppermute(value, both_axes, shift_pairs(kind, step, depth, side))  38.8 us
    ppermute x40, starting transfers between devices, send(): return lax.ppermute(value, both_axes, shift_pairs(kind, step, depth, side))  37.2 us
    pallas_call x4, Pallas kernels, expert_blocks(): pl.pallas_call(functools.partial(expert_kernel, count), out_shape=[jax.Sh...  12.2 us
    pallas_call x2, Pallas kernels, attend_rows(): pl.pallas_call(attend_kernel, out_shape=jax.ShapeDtypeStruct((count, head...  10.7 us
    unnamed x22, local copies, waits for them, and re-layouts  3.25 us
  transfers between devices with their start and end apart: 40, of which 10 were waited for; matrix products, arithmetic and copies ran while one was open for 4% of the time, Pallas kernels for 21%

profile of v5, /device:TPU:0, one launch (start us, length us, event | category | flops | bytes accessed | tf_op | source)
XLA Modules:
  0.0 109.5 jit_solution(2433260771204183319)
XLA Ops:
  0.6 1.7 %pack_rows.1 = (bf16[16,3712]{1,0:T(8,128)(2,1)}, bf16[16,3712]{1,0:T(8,128)(2,1)}) custom-call(bf16[32,3584]{1,0:T(8,128)(2,1)} %rows_ref.1, s32[8,32]{1,0:T(8,128)} %bitcast.17, f32[8,32]{1,0:T(8,128)} %bitcast.18), custom_call_target="tpu_custom_call" | custom-call | tf_op jit(solution)/shard_map/pack_rows/pallas_call | solution.py:157
  2.4 3.0 %collective-permute-start = (bf16[16,3712]{1,0:T(8,128)(2,1)}, bf16[16,3712]{1,0:T(8,128)(2,1)S(1)}, u32[]{:S(2)}, u32[]{:S(2)}) collective-permute-start(bf16[16,3712]{1,0:T(8,128)(2,1)} %get-tuple-element.29), channel_id=1, source_target_pairs={{0,4},{1,5},{2,6},{3,7},{4,0},{5,1},{6,2},{7,3},{8,12},{9,13},{10,... | collective-permute-start | bytes 356360 | tf_op jit(solution)/shard_map/ppermute | solution.py:192
  5.4 2.6 %collective-permute-start.1 = (bf16[16,3712]{1,0:T(8,128)(2,1)}, bf16[16,3712]{1,0:T(8,128)(2,1)S(1)}, u32[]{:S(2)}, u32[]{:S(2)}) collective-permute-start(bf16[16,3712]{1,0:T(8,128)(2,1)} %get-tuple-element.29), channel_id=1, source_target_pairs={{0,8},{1,9},{2,10},{3,11},{4,12},{5,13},{6,14},{7,15},{8,0},{9,1},... | collective-permute-start | bytes 356360 | tf_op jit(solution)/shard_map/ppermute | solution.py:192
  10.7 1.2 %copy-done.3 = bf16[4,64,2048]{2,1,0:T(8,128)(2,1)S(1)} copy-done((bf16[4,64,2048]{2,1,0:T(8,128)(2,1)S(1)}, bf16[4,64,2048]{2,1,0:T(8,128)(2,1)}, u32[]{:S(2)}) %copy-start.3) | copy-done | bytes 1048600
  12.8 5.1 %attend_rows.2 = bf16[2,64,512]{2,1,0:T(8,128)(2,1)S(1)} custom-call(s32[2]{0:T(128)S(1)} %get-tuple-element.61.lengths_ref, bf16[4,64,512]{2,1,0:T(8,128)(2,1)S(1)} %copy-done.5, bf16[4,64,64]{2,1,0:T(8,128)(2,1)S(1)} %reshape.44.rope_ref, bf16[4,2048,512]{2,1,0:T(8,128)(2,1)} %cache_ref.3, bf16[4,64,2048]{2,1,0:T(8,128)(2,1)S(1)} %copy-done.3), custom_call_target="tpu_custom_call" | custom-call | flops 570425344 | bytes 4718592 | tf_op jit(solution)/shard_map/attend_rows/pallas_call | solution.py:62
  18.1 1.5 %collective-permute-start.3 = (bf16[16,3712]{1,0:T(8,128)(2,1)S(1)}, bf16[16,3712]{1,0:T(8,128)(2,1)S(1)}, u32[]{:S(2)}, u32[]{:S(2)}) collective-permute-start(bf16[16,3712]{1,0:T(8,128)(2,1)S(1)} %copy-done.7), channel_id=1, source_target_pairs={{0,4},{1,5},{2,6},{3,7},{4,0},{5,1},{6,2},{7,3},{8,12},{9,13},{10,... | collective-permute-start | bytes 356360 | tf_op jit(solution)/shard_map/ppermute | solution.py:192
  19.6 2.9 %collective-permute-start.4 = (bf16[16,3712]{1,0:T(8,128)(2,1)S(1)}, bf16[16,3712]{1,0:T(8,128)(2,1)S(1)}, u32[]{:S(2)}, u32[]{:S(2)}) collective-permute-start(bf16[16,3712]{1,0:T(8,128)(2,1)S(1)} %copy-done.7), channel_id=1, source_target_pairs={{0,8},{1,9},{2,10},{3,11},{4,12},{5,13},{6,14},{7,15},{8,0},{9,1},... | collective-permute-start | bytes 356360 | tf_op jit(solution)/shard_map/ppermute | solution.py:192
  22.5 1.7 %collective-permute-start.9 = (bf16[64,3712]{1,0:T(8,128)(2,1)S(1)}, bf16[64,3712]{1,0:T(8,128)(2,1)S(1)}, u32[]{:S(2)}, u32[]{:S(2)}) collective-permute-start(bf16[64,3712]{1,0:T(8,128)(2,1)S(1)} %constant_dynamic-update-slice_fusion.refs_0_), channel_id=1, source_target_pairs={{0,2},{1,3},{2,0},{3,1},{4,6},{5,7},{6,4},{7,5},{8,10},{9,11},{10,... | collective-permute-start | bytes 1425416 | tf_op jit(solution)/shard_map/ppermute | solution.py:192
  24.2 1.5 %collective-permute-start.11 = (bf16[64,3712]{1,0:T(8,128)(2,1)S(1)}, bf16[64,3712]{1,0:T(8,128)(2,1)S(1)}, u32[]{:S(2)}, u32[]{:S(2)}) collective-permute-start(bf16[64,3712]{1,0:T(8,128)(2,1)S(1)} %constant_dynamic-update-slice_fusion.refs_0_), channel_id=1, source_target_pairs={{0,1},{1,0},{2,3},{3,2},{4,5},{5,4},{6,7},{7,6},{8,9},{9,8},{10,11... | collective-permute-start | bytes 1425416 | tf_op jit(solution)/shard_map/ppermute | solution.py:192
  25.8 5.6 %attend_rows.3 = bf16[2,64,512]{2,1,0:T(8,128)(2,1)S(1)} custom-call(s32[2]{0:T(128)S(1)} %get-tuple-element.60.lengths_ref, bf16[4,64,512]{2,1,0:T(8,128)(2,1)S(1)} %copy-done.6, bf16[4,64,64]{2,1,0:T(8,128)(2,1)S(1)} %reshape.44.rope_ref, bf16[4,2048,512]{2,1,0:T(8,128)(2,1)} %cache_ref.3, bf16[4,64,2048]{2,1,0:T(8,128)(2,1)S(1)} %copy-done.4), custom_call_target="tpu_custom_call" | custom-call | flops 570425344 | bytes 4718592 | tf_op jit(solution)/shard_map/attend_rows/pallas_call | solution.py:62
  31.5 3.7 %collective-permute-done.9.refs_1_ = bf16[64,3712]{1,0:T(8,128)(2,1)S(1)} collective-permute-done((bf16[64,3712]{1,0:T(8,128)(2,1)S(1)}, bf16[64,3712]{1,0:T(8,128)(2,1)S(1)}, u32[]{:S(2)}, u32[]{:S(2)}) %collective-permute-start.9) | collective-permute-done | bytes 475168 | tf_op jit(solution)/shard_map/ppermute | solution.py:192
  35.7 2.2 %collective-permute-start.6 = (bf16[64,3712]{1,0:T(8,128)(2,1)S(1)}, bf16[64,3712]{1,0:T(8,128)(2,1)S(1)}, u32[]{:S(2)}, u32[]{:S(2)}) collective-permute-start(bf16[64,3712]{1,0:T(8,128)(2,1)S(1)} %constant_dynamic-update-slice_fusion.4.refs_0_), channel_id=1, source_target_pairs={{0,2},{1,3},{2,0},{3,1},{4,6},{5,7},{6,4},{7,5},{8,10},{9,11},{10,... | collective-permute-start | bytes 1425416 | tf_op jit(solution)/shard_map/ppermute | solution.py:192
  38.4 6.8 %collective-permute-done.13.refs_3_ = bf16[64,3712]{1,0:T(8,128)(2,1)S(1)} collective-permute-done((bf16[64,3712]{1,0:T(8,128)(2,1)S(1)}, bf16[64,3712]{1,0:T(8,128)(2,1)S(1)}, u32[]{:S(2)}, u32[]{:S(2)}) %collective-permute-start.13) | collective-permute-done | bytes 475168 | tf_op jit(solution)/shard_map/ppermute | solution.py:192
  46.2 1.1 collective-permute-start.28
  47.3 3.0 %expert_blocks.4 = (bf16[64,3584]{1,0:T(8,128)(2,1)S(1)}, bf16[64,3584]{1,0:T(8,128)(2,1)S(1)}, bf16[64,3584]{1,0:T(8,128)(2,1)S(1)}, bf16[64,3584]{1,0:T(8,128)(2,1)S(1)}) custom-call(f32[1,128]{1,0:T(1,128)S(1)} %or_convert_fusion.lane_ref, bf16[64,3712]{1,0:T(8,128)(2,1)S(1)} %collective-permute-done.8.refs_0_, ...), custom_call_target="tpu_custom_call" | custom-call | flops 2818572288 | bytes 14680064 | tf_op jit(solution)/shard_map/expert_blocks/pallas_call | solution.py:121
  51.0 2.9 %collective-permute-done.7.refs_2_ = bf16[64,3712]{1,0:T(8,128)(2,1)S(1)} collective-permute-done((bf16[64,3712]{1,0:T(8,128)(2,1)S(1)}, bf16[64,3712]{1,0:T(8,128)(2,1)S(1)}, u32[]{:S(2)}, u32[]{:S(2)}) %collective-permute-start.7) | collective-permute-done | bytes 475168 | tf_op jit(solution)/shard_map/ppermute | solution.py:192
  54.6 4.4 %collective-permute-done.28.refs_3_ = bf16[64,3712]{1,0:T(8,128)(2,1)S(1)} collective-permute-done((bf16[64,3712]{1,0:T(8,128)(2,1)S(1)}, bf16[64,3712]{1,0:T(8,128)(2,1)S(1)}, u32[]{:S(2)}, u32[]{:S(2)}) %collective-permute-start.28) | collective-permute-done | bytes 475168 | tf_op jit(solution)/shard_map/ppermute | solution.py:192
  60.0 3.0 %expert_blocks.5 = (bf16[64,3584]{1,0:T(8,128)(2,1)S(1)}, bf16[64,3584]{1,0:T(8,128)(2,1)S(1)}, bf16[64,3584]{1,0:T(8,128)(2,1)S(1)}, bf16[64,3584]{1,0:T(8,128)(2,1)S(1)}) custom-call(f32[1,128]{1,0:T(1,128)S(1)} %or_convert_fusion.lane_ref, bf16[64,3712]{1,0:T(8,128)(2,1)S(1)} %constant_dynamic-update-slice_fusion.refs_0_, ...), custom_call_target="tpu_custom_call" | custom-call | flops 2818572288 | bytes 14680064 | tf_op jit(solution)/shard_map/expert_blocks/pallas_call | solution.py:121
  64.3 1.1 %collective-permute-start.19 = (bf16[64,3584]{1,0:T(8,128)(2,1)S(1)}, bf16[64,3584]{1,0:T(8,128)(2,1)S(1)}, u32[]{:S(2)}, u32[]{:S(2)}) collective-permute-start(bf16[64,3584]{1,0:T(8,128)(2,1)S(1)} %add_convert_fusion.7), channel_id=1, source_target_pairs={{0,1},{1,0},{2,3},{3,2},{4,5},{5,4},{6,7},{7,6},{8,9},{9,8},{10,11... | collective-permute-start | bytes 1376264 | tf_op jit(solution)/shard_map/ppermute | solution.py:192
  65.4 3.1 %expert_blocks.6 = (bf16[64,3584]{1,0:T(8,128)(2,1)S(1)}, bf16[64,3584]{1,0:T(8,128)(2,1)S(1)}, bf16[64,3584]{1,0:T(8,128)(2,1)S(1)}, bf16[64,3584]{1,0:T(8,128)(2,1)S(1)}) custom-call(f32[1,128]{1,0:T(1,128)S(1)} %or_convert_fusion.lane_ref, bf16[64,3712]{1,0:T(8,128)(2,1)S(1)} %collective-permute-done.25.refs_0_, ...), custom_call_target="tpu_custom_call" | custom-call | flops 2818572288 | bytes 14680064 | tf_op jit(solution)/shard_map/expert_blocks/pallas_call | solution.py:121
  69.2 2.5 %collective-permute-done.20 = bf16[64,3584]{1,0:T(8,128)(2,1)S(1)} collective-permute-done((bf16[64,3584]{1,0:T(8,128)(2,1)S(1)}, bf16[64,3584]{1,0:T(8,128)(2,1)S(1)}, u32[]{:S(2)}, u32[]{:S(2)}) %collective-permute-start.20) | collective-permute-done | bytes 458784 | tf_op jit(solution)/shard_map/ppermute | solution.py:192
  71.9 1.6 %collective-permute-start.21 = (bf16[64,3584]{1,0:T(8,128)(2,1)S(1)}, bf16[64,3584]{1,0:T(8,128)(2,1)S(1)}, u32[]{:S(2)}, u32[]{:S(2)}) collective-permute-start(bf16[64,3584]{1,0:T(8,128)(2,1)S(1)} %add_convert_fusion.5), channel_id=1, source_target_pairs={{0,2},{1,3},{2,0},{3,1},{4,6},{5,7},{6,4},{7,5},{8,10},{9,11},{10,... | collective-permute-start | bytes 1376264 | tf_op jit(solution)/shard_map/ppermute | solution.py:192
  73.5 3.0 %expert_blocks.7 = (bf16[64,3584]{1,0:T(8,128)(2,1)S(1)}, bf16[64,3584]{1,0:T(8,128)(2,1)S(1)}, bf16[64,3584]{1,0:T(8,128)(2,1)S(1)}, bf16[64,3584]{1,0:T(8,128)(2,1)S(1)}) custom-call(f32[1,128]{1,0:T(1,128)S(1)} %or_convert_fusion.lane_ref, bf16[64,3712]{1,0:T(8,128)(2,1)S(1)} %constant_dynamic-update-slice_fusion.4.refs_0_, ...), custom_call_target="tpu_custom_call" | custom-call | flops 2818572288 | bytes 14680064 | tf_op jit(solution)/shard_map/expert_blocks/pallas_call | solution.py:121
  77.4 1.6 %collective-permute-start.33 = (bf16[64,3584]{1,0:T(8,128)(2,1)S(1)}, bf16[64,3584]{1,0:T(8,128)(2,1)S(1)}, u32[]{:S(2)}, u32[]{:S(2)}) collective-permute-start(bf16[64,3584]{1,0:T(8,128)(2,1)S(1)} %add_convert_fusion.3), channel_id=1, source_target_pairs={{0,1},{1,0},{2,3},{3,2},{4,5},{5,4},{6,7},{7,6},{8,9},{9,8},{10,11... | collective-permute-start | bytes 1376264 | tf_op jit(solution)/shard_map/ppermute | solution.py:192
  78.9 7.5 %collective-permute-done.35 = bf16[64,3584]{1,0:T(8,128)(2,1)S(1)} collective-permute-done((bf16[64,3584]{1,0:T(8,128)(2,1)S(1)}, bf16[64,3584]{1,0:T(8,128)(2,1)S(1)}, u32[]{:S(2)}, u32[]{:S(2)}) %collective-permute-start.35) | collective-permute-done | bytes 458784 | tf_op jit(solution)/shard_map/ppermute | solution.py:192
  86.6 1.6 %collective-permute-start.36 = (bf16[64,3584]{1,0:T(8,128)(2,1)S(1)}, bf16[64,3584]{1,0:T(8,128)(2,1)S(1)}, u32[]{:S(2)}, u32[]{:S(2)}) collective-permute-start(bf16[64,3584]{1,0:T(8,128)(2,1)S(1)} %add_convert_fusion.1), channel_id=1, source_target_pairs={{0,2},{1,3},{2,0},{3,1},{4,6},{5,7},{6,4},{7,5},{8,10},{9,11},{10,... | collective-permute-start | bytes 1376264 | tf_op jit(solution)/shard_map/ppermute | solution.py:192
  88.9 3.8 %collective-permute-start.23 = (bf16[16,3584]{1,0:T(8,128)(2,1)S(1)}, bf16[16,3584]{1,0:T(8,128)(2,1)S(1)}, u32[]{:S(2)}, u32[]{:S(2)}) collective-permute-start(bf16[16,3584]{1,0:T(8,128)(2,1)S(1)} %get-tuple-element.56), channel_id=1, source_target_pairs={{0,8},{1,9},{2,10},{3,11},{4,12},{5,13},{6,14},{7,15},{8,0},{9,1},... | collective-permute-start | bytes 344072 | tf_op jit(solution)/shard_map/ppermute | solution.py:192
  92.9 1.2 %collective-permute-done.33 = bf16[64,3584]{1,0:T(8,128)(2,1)S(1)} collective-permute-done((bf16[64,3584]{1,0:T(8,128)(2,1)S(1)}, bf16[64,3584]{1,0:T(8,128)(2,1)S(1)}, u32[]{:S(2)}, u32[]{:S(2)}) %collective-permute-start.33) | collective-permute-done | bytes 458784 | tf_op jit(solution)/shard_map/ppermute | solution.py:192
  94.2 1.2 %collective-permute-done.36 = bf16[64,3584]{1,0:T(8,128)(2,1)S(1)} collective-permute-done((bf16[64,3584]{1,0:T(8,128)(2,1)S(1)}, bf16[64,3584]{1,0:T(8,128)(2,1)S(1)}, u32[]{:S(2)}, u32[]{:S(2)}) %collective-permute-start.36) | collective-permute-done | bytes 458784 | tf_op jit(solution)/shard_map/ppermute | solution.py:192
  96.3 3.5 %collective-permute-start.38 = (bf16[16,3584]{1,0:T(8,128)(2,1)S(1)}, bf16[16,3584]{1,0:T(8,128)(2,1)S(1)}, u32[]{:S(2)}, u32[]{:S(2)}) collective-permute-start(bf16[16,3584]{1,0:T(8,128)(2,1)S(1)} %get-tuple-element.59), channel_id=1, source_target_pairs={{0,8},{1,9},{2,10},{3,11},{4,12},{5,13},{6,14},{7,15},{8,0},{9,1},... | collective-permute-start | bytes 344072 | tf_op jit(solution)/shard_map/ppermute | solution.py:192
  100.2 4.2 %collective-permute-done.37 = bf16[16,3584]{1,0:T(8,128)(2,1)S(1)} collective-permute-done((bf16[16,3584]{1,0:T(8,128)(2,1)S(1)}, bf16[16,3584]{1,0:T(8,128)(2,1)S(1)}, u32[]{:S(2)}, u32[]{:S(2)}) %collective-permute-start.37) | collective-permute-done | bytes 114720 | tf_op jit(solution)/shard_map/ppermute | solution.py:192
  104.3 4.5 %collective-permute-done.38 = bf16[16,3584]{1,0:T(8,128)(2,1)S(1)} collective-permute-done((bf16[16,3584]{1,0:T(8,128)(2,1)S(1)}, bf16[16,3584]{1,0:T(8,128)(2,1)S(1)}, u32[]{:S(2)}, u32[]{:S(2)}) %collective-permute-start.38) | collective-permute-done | bytes 114720 | tf_op jit(solution)/shard_map/ppermute | solution.py:192
  (96 shorter events, 14.3 us)
Async XLA Ops:
  2.4 15.6 %collective-permute-start = (bf16[16,3712]{1,0:T(8,128)(2,1)}, bf16[16,3712]{1,0:T(8,128)(2,1)S(1)}, u32[]{:S(2)}, u32[]{:S(2)}) collective-permute-start(bf16[16,3712]{1,0:T(8,128)(2,1)} %get-tuple-element.29), channel_id=1, source_target_pairs={{0,4},{1,5},{2,6},{3,7},{4,0},{5,1},{6,2},{7,3},{8,12},{9,13},{10,... | collective-permute-start | bytes 356360 | tf_op jit(solution)/shard_map/ppermute | solution.py:192
  5.4 12.6 %collective-permute-start.1 = (bf16[16,3712]{1,0:T(8,128)(2,1)}, bf16[16,3712]{1,0:T(8,128)(2,1)S(1)}, u32[]{:S(2)}, u32[]{:S(2)}) collective-permute-start(bf16[16,3712]{1,0:T(8,128)(2,1)} %get-tuple-element.29), channel_id=1, source_target_pairs={{0,8},{1,9},{2,10},{3,11},{4,12},{5,13},{6,14},{7,15},{8,0},{9,1},... | collective-permute-start | bytes 356360 | tf_op jit(solution)/shard_map/ppermute | solution.py:192
  8.0 10.0 %collective-permute-start.2 = (bf16[16,3712]{1,0:T(8,128)(2,1)}, bf16[16,3712]{1,0:T(8,128)(2,1)S(1)}, u32[]{:S(2)}, u32[]{:S(2)}) collective-permute-start(bf16[16,3712]{1,0:T(8,128)(2,1)} %get-tuple-element.29), channel_id=1, source_target_pairs={{0,12},{1,13},{2,14},{3,15},{4,8},{5,9},{6,10},{7,11},{8,4},{9,5},... | collective-permute-start | bytes 356360 | tf_op jit(solution)/shard_map/ppermute | solution.py:192
  18.1 13.3 %collective-permute-start.3 = (bf16[16,3712]{1,0:T(8,128)(2,1)S(1)}, bf16[16,3712]{1,0:T(8,128)(2,1)S(1)}, u32[]{:S(2)}, u32[]{:S(2)}) collective-permute-start(bf16[16,3712]{1,0:T(8,128)(2,1)S(1)} %copy-done.7), channel_id=1, source_target_pairs={{0,4},{1,5},{2,6},{3,7},{4,0},{5,1},{6,2},{7,3},{8,12},{9,13},{10,... | collective-permute-start | bytes 356360 | tf_op jit(solution)/shard_map/ppermute | solution.py:192
  19.6 11.9 %collective-permute-start.4 = (bf16[16,3712]{1,0:T(8,128)(2,1)S(1)}, bf16[16,3712]{1,0:T(8,128)(2,1)S(1)}, u32[]{:S(2)}, u32[]{:S(2)}) collective-permute-start(bf16[16,3712]{1,0:T(8,128)(2,1)S(1)} %copy-done.7), channel_id=1, source_target_pairs={{0,8},{1,9},{2,10},{3,11},{4,12},{5,13},{6,14},{7,15},{8,0},{9,1},... | collective-permute-start | bytes 356360 | tf_op jit(solution)/shard_map/ppermute | solution.py:192
  22.5 9.0 %collective-permute-start.5 = (bf16[16,3712]{1,0:T(8,128)(2,1)S(1)}, bf16[16,3712]{1,0:T(8,128)(2,1)S(1)}, u32[]{:S(2)}, u32[]{:S(2)}) collective-permute-start(bf16[16,3712]{1,0:T(8,128)(2,1)S(1)} %copy-done.7), channel_id=1, source_target_pairs={{0,12},{1,13},{2,14},{3,15},{4,8},{5,9},{6,10},{7,11},{8,4},{9,5},... | collective-permute-start | bytes 356360 | tf_op jit(solution)/shard_map/ppermute | solution.py:192
  22.5 12.7 %collective-permute-start.9 = (bf16[64,3712]{1,0:T(8,128)(2,1)S(1)}, bf16[64,3712]{1,0:T(8,128)(2,1)S(1)}, u32[]{:S(2)}, u32[]{:S(2)}) collective-permute-start(bf16[64,3712]{1,0:T(8,128)(2,1)S(1)} %constant_dynamic-update-slice_fusion.refs_0_), channel_id=1, source_target_pairs={{0,2},{1,3},{2,0},{3,1},{4,6},{5,7},{6,4},{7,5},{8,10},{9,11},{10,... | collective-permute-start | bytes 1425416 | tf_op jit(solution)/shard_map/ppermute | solution.py:192
  24.2 13.7 %collective-permute-start.11 = (bf16[64,3712]{1,0:T(8,128)(2,1)S(1)}, bf16[64,3712]{1,0:T(8,128)(2,1)S(1)}, u32[]{:S(2)}, u32[]{:S(2)}) collective-permute-start(bf16[64,3712]{1,0:T(8,128)(2,1)S(1)} %constant_dynamic-update-slice_fusion.refs_0_), channel_id=1, source_target_pairs={{0,1},{1,0},{2,3},{3,2},{4,5},{5,4},{6,7},{7,6},{8,9},{9,8},{10,11... | collective-permute-start | bytes 1425416 | tf_op jit(solution)/shard_map/ppermute | solution.py:192
  31.4 13.8 %collective-permute-start.8 = (bf16[64,3712]{1,0:T(8,128)(2,1)S(1)}, bf16[64,3712]{1,0:T(8,128)(2,1)S(1)}, u32[]{:S(2)}, u32[]{:S(2)}) collective-permute-start(bf16[64,3712]{1,0:T(8,128)(2,1)S(1)} %constant_dynamic-update-slice_fusion.refs_0_), channel_id=1, source_target_pairs={{0,16},{1,17},{2,18},{3,19},{4,20},{5,21},{6,22},{7,23},{8,24},{9,... | collective-permute-start | bytes 1425416 | tf_op jit(solution)/shard_map/ppermute | solution.py:192
  35.2 10.0 %collective-permute-start.13 = (bf16[64,3712]{1,0:T(8,128)(2,1)S(1)}, bf16[64,3712]{1,0:T(8,128)(2,1)S(1)}, u32[]{:S(2)}, u32[]{:S(2)}) collective-permute-start(bf16[64,3712]{1,0:T(8,128)(2,1)S(1)} %collective-permute-done.9.refs_1_), channel_id=1, source_target_pairs={{0,1},{1,0},{2,3},{3,2},{4,5},{5,4},{6,7},{7,6},{8,9},{9,8},{10,11... | collective-permute-start | bytes 1425416 | tf_op jit(solution)/shard_map/ppermute | solution.py:192
  35.7 10.4 %collective-permute-start.6 = (bf16[64,3712]{1,0:T(8,128)(2,1)S(1)}, bf16[64,3712]{1,0:T(8,128)(2,1)S(1)}, u32[]{:S(2)}, u32[]{:S(2)}) collective-permute-start(bf16[64,3712]{1,0:T(8,128)(2,1)S(1)} %constant_dynamic-update-slice_fusion.4.refs_0_), channel_id=1, source_target_pairs={{0,2},{1,3},{2,0},{3,1},{4,6},{5,7},{6,4},{7,5},{8,10},{9,11},{10,... | collective-permute-start | bytes 1425416 | tf_op jit(solution)/shard_map/ppermute | solution.py:192
  37.9 9.3 %collective-permute-start.10 = (bf16[64,3712]{1,0:T(8,128)(2,1)S(1)}, bf16[64,3712]{1,0:T(8,128)(2,1)S(1)}, u32[]{:S(2)}, u32[]{:S(2)}) collective-permute-start(bf16[64,3712]{1,0:T(8,128)(2,1)S(1)} %collective-permute-done.9.refs_1_), channel_id=1, source_target_pairs={{0,16},{1,17},{2,18},{3,19},{4,20},{5,21},{6,22},{7,23},{8,24},{9,... | collective-permute-start | bytes 1425416 | tf_op jit(solution)/shard_map/ppermute | solution.py:192
  37.9 9.3 %collective-permute-start.12 = (bf16[64,3712]{1,0:T(8,128)(2,1)S(1)}, bf16[64,3712]{1,0:T(8,128)(2,1)S(1)}, u32[]{:S(2)}, u32[]{:S(2)}) collective-permute-start(bf16[64,3712]{1,0:T(8,128)(2,1)S(1)} %collective-permute-done.11.refs_2_), channel_id=1, source_target_pairs={{0,16},{1,17},{2,18},{3,19},{4,20},{5,21},{6,22},{7,23},{8,24},{9,... | collective-permute-start | bytes 1425416 | tf_op jit(solution)/shard_map/ppermute | solution.py:192
  45.2 8.7 %collective-permute-start.7 = (bf16[64,3712]{1,0:T(8,128)(2,1)S(1)}, bf16[64,3712]{1,0:T(8,128)(2,1)S(1)}, u32[]{:S(2)}, u32[]{:S(2)}) collective-permute-start(bf16[64,3712]{1,0:T(8,128)(2,1)S(1)} %constant_dynamic-update-slice_fusion.4.refs_0_), channel_id=1, source_target_pairs={{0,1},{1,0},{2,3},{3,2},{4,5},{5,4},{6,7},{7,6},{8,9},{9,8},{10,11... | collective-permute-start | bytes 1425416 | tf_op jit(solution)/shard_map/ppermute | solution.py:192
  46.2 12.8 %collective-permute-start.28 = (bf16[64,3712]{1,0:T(8,128)(2,1)S(1)}, bf16[64,3712]{1,0:T(8,128)(2,1)S(1)}, u32[]{:S(2)}, u32[]{:S(2)}) collective-permute-start(bf16[64,3712]{1,0:T(8,128)(2,1)S(1)} %collective-permute-done.6.refs_1_), channel_id=1, source_target_pairs={{0,1},{1,0},{2,3},{3,2},{4,5},{5,4},{6,7},{7,6},{8,9},{9,8},{10,11... | collective-permute-start | bytes 1425416 | tf_op jit(solution)/shard_map/ppermute | solution.py:192
  50.3 8.6 %collective-permute-start.15 = (bf16[64,3584]{1,0:T(8,128)(2,1)S(1)}, bf16[64,3584]{1,0:T(8,128)(2,1)S(1)}, u32[]{:S(2)}, u32[]{:S(2)}) collective-permute-start(bf16[64,3584]{1,0:T(8,128)(2,1)S(1)} %get-tuple-element.35), channel_id=1, source_target_pairs={{0,16},{1,17},{2,18},{3,19},{4,20},{5,21},{6,22},{7,23},{8,24},{9,... | collective-permute-start | bytes 1376264 | tf_op jit(solution)/shard_map/ppermute | solution.py:192
  50.4 9.1 %collective-permute-start.16 = (bf16[64,3584]{1,0:T(8,128)(2,1)S(1)}, bf16[64,3584]{1,0:T(8,128)(2,1)S(1)}, u32[]{:S(2)}, u32[]{:S(2)}) collective-permute-start(bf16[64,3584]{1,0:T(8,128)(2,1)S(1)} %get-tuple-element.36), channel_id=1, source_target_pairs={{0,16},{1,17},{2,18},{3,19},{4,20},{5,21},{6,22},{7,23},{8,24},{9,... | collective-permute-start | bytes 1376264 | tf_op jit(solution)/shard_map/ppermute | solution.py:192
  50.9 8.6 %collective-permute-start.17 = (bf16[64,3584]{1,0:T(8,128)(2,1)S(1)}, bf16[64,3584]{1,0:T(8,128)(2,1)S(1)}, u32[]{:S(2)}, u32[]{:S(2)}) collective-permute-start(bf16[64,3584]{1,0:T(8,128)(2,1)S(1)} %get-tuple-element.37), channel_id=1, source_target_pairs={{0,16},{1,17},{2,18},{3,19},{4,20},{5,21},{6,22},{7,23},{8,24},{9,... | collective-permute-start | bytes 1376264 | tf_op jit(solution)/shard_map/ppermute | solution.py:192
  63.1 8.5 %collective-permute-start.20 = (bf16[64,3584]{1,0:T(8,128)(2,1)S(1)}, bf16[64,3584]{1,0:T(8,128)(2,1)S(1)}, u32[]{:S(2)}, u32[]{:S(2)}) collective-permute-start(bf16[64,3584]{1,0:T(8,128)(2,1)S(1)} %add_convert_fusion.6), channel_id=1, source_target_pairs={{0,1},{1,0},{2,3},{3,2},{4,5},{5,4},{6,7},{7,6},{8,9},{9,8},{10,11... | collective-permute-start | bytes 1376264 | tf_op jit(solution)/shard_map/ppermute | solution.py:192
  64.3 23.9 %collective-permute-start.19 = (bf16[64,3584]{1,0:T(8,128)(2,1)S(1)}, bf16[64,3584]{1,0:T(8,128)(2,1)S(1)}, u32[]{:S(2)}, u32[]{:S(2)}) collective-permute-start(bf16[64,3584]{1,0:T(8,128)(2,1)S(1)} %add_convert_fusion.7), channel_id=1, source_target_pairs={{0,1},{1,0},{2,3},{3,2},{4,5},{5,4},{6,7},{7,6},{8,9},{9,8},{10,11... | collective-permute-start | bytes 1376264 | tf_op jit(solution)/shard_map/ppermute | solution.py:192
  68.6 8.0 %collective-permute-start.32 = (bf16[64,3584]{1,0:T(8,128)(2,1)S(1)}, bf16[64,3584]{1,0:T(8,128)(2,1)S(1)}, u32[]{:S(2)}, u32[]{:S(2)}) collective-permute-start(bf16[64,3584]{1,0:T(8,128)(2,1)S(1)} %get-tuple-element.50), channel_id=1, source_target_pairs={{0,16},{1,17},{2,18},{3,19},{4,20},{5,21},{6,22},{7,23},{8,24},{9,... | collective-permute-start | bytes 1376264 | tf_op jit(solution)/shard_map/ppermute | solution.py:192
  69.1 8.2 %collective-permute-start.34 = (bf16[64,3584]{1,0:T(8,128)(2,1)S(1)}, bf16[64,3584]{1,0:T(8,128)(2,1)S(1)}, u32[]{:S(2)}, u32[]{:S(2)}) collective-permute-start(bf16[64,3584]{1,0:T(8,128)(2,1)S(1)} %get-tuple-element.52), channel_id=1, source_target_pairs={{0,16},{1,17},{2,18},{3,19},{4,20},{5,21},{6,22},{7,23},{8,24},{9,... | collective-permute-start | bytes 1376264 | tf_op jit(solution)/shard_map/ppermute | solution.py:192
  71.7 21.0 %collective-permute-start.31 = (bf16[64,3584]{1,0:T(8,128)(2,1)S(1)}, bf16[64,3584]{1,0:T(8,128)(2,1)S(1)}, u32[]{:S(2)}, u32[]{:S(2)}) collective-permute-start(bf16[64,3584]{1,0:T(8,128)(2,1)S(1)} %get-tuple-element.48), channel_id=1, source_target_pairs={{0,16},{1,17},{2,18},{3,19},{4,20},{5,21},{6,22},{7,23},{8,24},{9,... | collective-permute-start | bytes 1376264 | tf_op jit(solution)/shard_map/ppermute | solution.py:192
  71.9 16.3 %collective-permute-start.21 = (bf16[64,3584]{1,0:T(8,128)(2,1)S(1)}, bf16[64,3584]{1,0:T(8,128)(2,1)S(1)}, u32[]{:S(2)}, u32[]{:S(2)}) collective-permute-start(bf16[64,3584]{1,0:T(8,128)(2,1)S(1)} %add_convert_fusion.5), channel_id=1, source_target_pairs={{0,2},{1,3},{2,0},{3,1},{4,6},{5,7},{6,4},{7,5},{8,10},{9,11},{10,... | collective-permute-start | bytes 1376264 | tf_op jit(solution)/shard_map/ppermute | solution.py:192
  76.6 9.8 %collective-permute-start.35 = (bf16[64,3584]{1,0:T(8,128)(2,1)S(1)}, bf16[64,3584]{1,0:T(8,128)(2,1)S(1)}, u32[]{:S(2)}, u32[]{:S(2)}) collective-permute-start(bf16[64,3584]{1,0:T(8,128)(2,1)S(1)} %add_convert_fusion.2), channel_id=1, source_target_pairs={{0,1},{1,0},{2,3},{3,2},{4,5},{5,4},{6,7},{7,6},{8,9},{9,8},{10,11... | collective-permute-start | bytes 1376264 | tf_op jit(solution)/shard_map/ppermute | solution.py:192
  77.4 16.8 %collective-permute-start.33 = (bf16[64,3584]{1,0:T(8,128)(2,1)S(1)}, bf16[64,3584]{1,0:T(8,128)(2,1)S(1)}, u32[]{:S(2)}, u32[]{:S(2)}) collective-permute-start(bf16[64,3584]{1,0:T(8,128)(2,1)S(1)} %add_convert_fusion.3), channel_id=1, source_target_pairs={{0,1},{1,0},{2,3},{3,2},{4,5},{5,4},{6,7},{7,6},{8,9},{9,8},{10,11... | collective-permute-start | bytes 1376264 | tf_op jit(solution)/shard_map/ppermute | solution.py:192
  86.6 8.8 %collective-permute-start.36 = (bf16[64,3584]{1,0:T(8,128)(2,1)S(1)}, bf16[64,3584]{1,0:T(8,128)(2,1)S(1)}, u32[]{:S(2)}, u32[]{:S(2)}) collective-permute-start(bf16[64,3584]{1,0:T(8,128)(2,1)S(1)} %add_convert_fusion.1), channel_id=1, source_target_pairs={{0,2},{1,3},{2,0},{3,1},{4,6},{5,7},{6,4},{7,5},{8,10},{9,11},{10,... | collective-permute-start | bytes 1376264 | tf_op jit(solution)/shard_map/ppermute | solution.py:192
  88.5 11.4 %collective-permute-start.22 = (bf16[16,3584]{1,0:T(8,128)(2,1)S(1)}, bf16[16,3584]{1,0:T(8,128)(2,1)S(1)}, u32[]{:S(2)}, u32[]{:S(2)}) collective-permute-start(bf16[16,3584]{1,0:T(8,128)(2,1)S(1)} %get-tuple-element.54), channel_id=1, source_target_pairs={{0,4},{1,5},{2,6},{3,7},{4,0},{5,1},{6,2},{7,3},{8,12},{9,13},{10,... | collective-permute-start | bytes 344072 | tf_op jit(solution)/shard_map/ppermute | solution.py:192
  88.9 11.2 %collective-permute-start.23 = (bf16[16,3584]{1,0:T(8,128)(2,1)S(1)}, bf16[16,3584]{1,0:T(8,128)(2,1)S(1)}, u32[]{:S(2)}, u32[]{:S(2)}) collective-permute-start(bf16[16,3584]{1,0:T(8,128)(2,1)S(1)} %get-tuple-element.56), channel_id=1, source_target_pairs={{0,8},{1,9},{2,10},{3,11},{4,12},{5,13},{6,14},{7,15},{8,0},{9,1},... | collective-permute-start | bytes 344072 | tf_op jit(solution)/shard_map/ppermute | solution.py:192
  95.6 8.7 %collective-permute-start.37 = (bf16[16,3584]{1,0:T(8,128)(2,1)S(1)}, bf16[16,3584]{1,0:T(8,128)(2,1)S(1)}, u32[]{:S(2)}, u32[]{:S(2)}) collective-permute-start(bf16[16,3584]{1,0:T(8,128)(2,1)S(1)} %get-tuple-element.57), channel_id=1, source_target_pairs={{0,4},{1,5},{2,6},{3,7},{4,0},{5,1},{6,2},{7,3},{8,12},{9,13},{10,... | collective-permute-start | bytes 344072 | tf_op jit(solution)/shard_map/ppermute | solution.py:192
  96.3 12.4 %collective-permute-start.38 = (bf16[16,3584]{1,0:T(8,128)(2,1)S(1)}, bf16[16,3584]{1,0:T(8,128)(2,1)S(1)}, u32[]{:S(2)}, u32[]{:S(2)}) collective-permute-start(bf16[16,3584]{1,0:T(8,128)(2,1)S(1)} %get-tuple-element.59), channel_id=1, source_target_pairs={{0,8},{1,9},{2,10},{3,11},{4,12},{5,13},{6,14},{7,15},{8,0},{9,1},... | collective-permute-start | bytes 344072 | tf_op jit(solution)/shard_map/ppermute | solution.py:192
  99.9 8.9 %collective-permute-start.39 = (bf16[16,3584]{1,0:T(8,128)(2,1)S(1)}, bf16[16,3584]{1,0:T(8,128)(2,1)S(1)}, u32[]{:S(2)}, u32[]{:S(2)}) collective-permute-start(bf16[16,3584]{1,0:T(8,128)(2,1)S(1)} %get-tuple-element.58), channel_id=1, source_target_pairs={{0,12},{1,13},{2,14},{3,15},{4,8},{5,9},{6,10},{7,11},{8,4},{9,5},... | collective-permute-start | bytes 344072 | tf_op jit(solution)/shard_map/ppermute | solution.py:192
  (16 other events, 148.1 us)
